TPU v7x, 512 devices: a whole 4x8x8 slice. The times are simulated.
512 devices in a mesh: doc: 16 (over z, core), ctx: 32 (over y, x).
Axes of the slice: x: 4, y: 8, z: 8, core: 2. Of those that a mesh axis runs over, the one named last changes fastest.
Arguments:
- tokens: bfloat16 [65536, 3584], P(('doc', 'ctx')), parts along dimension 0, may hold values from -6 to 6
- queries: bfloat16 [65536, 1792], P(('doc', 'ctx')), parts along dimension 0, may hold values from -320 to 320
- key_matrix: bfloat16 [3584, 256], P('ctx'), may hold values from -0.09375 to 0.09375
- value_matrix: bfloat16 [3584, 256], P('ctx'), may hold values from -0.09375 to 0.09375
- doc_tiles: int32 [32], P('doc'), parts along dimension 0, may hold values from 1 to 6, 8 in all
- question_lengths: int32 [32], P('doc'), parts along dimension 0, may hold values from 1 to 16, as said below
Outputs:
- attended: bfloat16 [65536, 1792], P(('doc', 'ctx')), parts along dimension 0
There are 16 independent parts, one for each index of `doc`. A program takes and returns all parts, laid end to end along the dimension named above; an argument that names none is the same for every part. Nothing has to cross between parts.
Inputs may be any that keep to these rules, and one draw needn't show every extreme that they name: `doc_tiles`: document lengths in tiles of 512 tokens; they sum to 8 and the longest has at most 6 tiles. `question_lengths`: some document has exactly 16 question tokens.
All inputs are finite; a program needn't handle non-finite values.
Results may differ from a plain program's by a relative error of at most 0.012.
The roundings to bfloat16 on the way count: a program that leaves them out, or rounds other values in their place, can miss the bound.
Values may be sent and summed in bfloat16 or wider, within the bound.
No kernel may reach another device: no remote copies, remote signals or barrier semaphores. Data moves between devices by JAX's collectives and lax.ppermute only.
A program may use at most 64 MiB of HBM per device.

v0:
```python
import math

import jax
import jax.numpy as jnp
from jax import lax
from jax.sharding import PartitionSpec as P

HEAD_SIZE = 128
WINDOW_REACH = 512
TILE_TOKENS = 512
QUESTION_LIMIT = 16


masked_score = -1e30


def from_behind(shard, axis, by):
    size = lax.axis_size(axis)
    pairs = [(i, i + by) for i in range(size) if 0 <= i + by < size]
    return lax.ppermute(shard, axis, pairs)


def lookup(table_values, slot_index):
    picks = jnp.arange(table_values.shape[0], dtype=jnp.int32) == slot_index
    return jnp.sum(jnp.where(picks, table_values, 0))


def neighbour(key_values, offset):
    return from_behind(key_values, "ctx", offset)


def per_device(tokens, queries, key_matrix, value_matrix, doc_tiles, question_lengths):
    row_count = tokens.shape[0]
    width_kv = key_matrix.shape[1]
    heads_kv = width_kv // HEAD_SIZE
    heads_q = queries.shape[1] // HEAD_SIZE
    query_group_count = heads_q // heads_kv
    scaling = 1.0 / math.sqrt(HEAD_SIZE)
    my_index = lax.axis_index("ctx")
    doc_count = doc_tiles.shape[0]
    key_sum = jnp.dot(
        tokens,
        lax.all_gather(key_matrix, "ctx", axis=0, tiled=True),
        preferred_element_type=jnp.float32,
    )
    value_sum = jnp.dot(
        tokens,
        lax.all_gather(value_matrix, "ctx", axis=0, tiled=True),
        preferred_element_type=jnp.float32,
    )
    key_values = jnp.concatenate([key_sum, value_sum], axis=1).astype(jnp.bfloat16)
    doc_ends = jnp.cumsum(doc_tiles) * TILE_TOKENS
    starts = doc_ends - doc_tiles * TILE_TOKENS
    first_row_index = my_index * row_count
    doc_index = jnp.sum((starts <= first_row_index).astype(jnp.int32)) - 1
    document_start = lookup(starts, doc_index)
    doc_last = lookup(doc_ends, doc_index)
    question_count = lookup(question_lengths, doc_index)
    is_start = document_start == first_row_index
    owner_index = document_start // row_count
    reach_count = WINDOW_REACH // row_count
    before = [neighbour(key_values, offset) for offset in range(reach_count, 0, -1)]
    after = [neighbour(key_values, -offset) for offset in range(1, reach_count + 1)]
    near_rows = jnp.concatenate(before + [key_values] + after, axis=0)
    head_queries = queries[:QUESTION_LIMIT]
    head_keyvals = key_values[:QUESTION_LIMIT]
    all_queries, all_keyvals = (
        lax.all_gather(head_queries, "ctx", axis=0, tiled=True),
        lax.all_gather(head_keyvals, "ctx", axis=0, tiled=True),
    )
    doc_queries = lax.dynamic_slice_in_dim(
        all_queries, owner_index * QUESTION_LIMIT, QUESTION_LIMIT, 0
    )
    doc_keyvals = lax.dynamic_slice_in_dim(
        all_keyvals, owner_index * QUESTION_LIMIT, QUESTION_LIMIT, 0
    )
    query_pos = first_row_index + jnp.arange(row_count, dtype=jnp.int32)
    key_pos = first_row_index - WINDOW_REACH + jnp.arange(near_rows.shape[0], dtype=jnp.int32)
    near_valid = (
        (jnp.abs(key_pos[None, :] - query_pos[:, None]) <= WINDOW_REACH)
        & (key_pos >= document_start + question_count)[None, :]
        & (key_pos < doc_last)[None, :]
    )
    far_valid = jnp.arange(QUESTION_LIMIT, dtype=jnp.int32) < question_count

    def attend(head_index):
        query_tile_rows = lax.dynamic_slice_in_dim(
            queries, head_index * query_group_count * HEAD_SIZE, query_group_count * HEAD_SIZE, 1
        ).reshape(row_count, query_group_count, HEAD_SIZE)
        window_keys = lax.dynamic_slice_in_dim(near_rows, head_index * HEAD_SIZE, HEAD_SIZE, 1)
        window_values = lax.dynamic_slice_in_dim(
            near_rows, width_kv + head_index * HEAD_SIZE, HEAD_SIZE, 1
        )
        distant_keys = lax.dynamic_slice_in_dim(doc_keyvals, head_index * HEAD_SIZE, HEAD_SIZE, 1)
        distant_values = lax.dynamic_slice_in_dim(
            doc_keyvals, width_kv + head_index * HEAD_SIZE, HEAD_SIZE, 1
        )
        near_scores = (
            jnp.einsum(
                "tgd,nd->gtn", query_tile_rows, window_keys, preferred_element_type=jnp.float32
            )
            * scaling
        )
        far_scores = (
            jnp.einsum(
                "tgd,nd->gtn", query_tile_rows, distant_keys, preferred_element_type=jnp.float32
            )
            * scaling
        )
        near_scores = jnp.where(near_valid, near_scores, masked_score)
        far_scores = jnp.where(far_valid, far_scores, masked_score)
        peak = jnp.maximum(near_scores.max(-1), far_scores.max(-1))
        near_probs = jnp.exp(near_scores - peak[..., None])
        far_probs = jnp.exp(far_scores - peak[..., None])
        totals = near_probs.sum(-1) + far_probs.sum(-1)
        output = jnp.einsum(
            "gtn,nd->tgd",
            near_probs.astype(jnp.bfloat16),
            window_values,
            preferred_element_type=jnp.float32,
        )
        output = output + jnp.einsum(
            "gtn,nd->tgd",
            far_probs.astype(jnp.bfloat16),
            distant_values,
            preferred_element_type=jnp.float32,
        )
        return output / jnp.transpose(totals)[..., None]

    head_outputs = lax.map(attend, jnp.arange(heads_kv, dtype=jnp.int32))
    banded = jnp.transpose(head_outputs, (1, 0, 2, 3)).reshape(row_count, heads_q * HEAD_SIZE)
    ask_queries = doc_queries.reshape(QUESTION_LIMIT, heads_kv, query_group_count, HEAD_SIZE)
    own_keys = key_values[:, :width_kv].reshape(row_count, heads_kv, HEAD_SIZE)
    own_values = (
        key_values[:, width_kv:].astype(jnp.float32).reshape(row_count, heads_kv, HEAD_SIZE)
    )
    ask_scores = (
        jnp.einsum("qkgd,nkd->qkgn", ask_queries, own_keys, preferred_element_type=jnp.float32)
        * scaling
    )
    local_peak = ask_scores.max(-1)
    doc_slot = jnp.arange(doc_count, dtype=jnp.int32) == doc_index
    marked = jnp.where(doc_slot[:, None, None, None], local_peak[None], masked_score)
    highest_all = lax.pmax(marked, "ctx")
    highest = lax.dynamic_index_in_dim(highest_all, doc_index, 0, keepdims=False)
    weights = jnp.exp(ask_scores - highest[..., None])
    weight_sum = weights.sum(-1)
    partial_value = jnp.einsum(
        "qkgn,nkd->qkgd", weights, own_values, precision=lax.Precision.HIGHEST
    )
    summed_part, summed_weight = lax.psum(
        (
            jnp.where(doc_slot[:, None, None, None, None], partial_value[None], 0.0),
            jnp.where(doc_slot[:, None, None, None], weight_sum[None], 0.0),
        ),
        "ctx",
    )
    partial_value = lax.dynamic_index_in_dim(summed_part, doc_index, 0, keepdims=False)
    weight_sum = lax.dynamic_index_in_dim(summed_weight, doc_index, 0, keepdims=False)
    weight_sum = jnp.where(is_start, weight_sum, 1.0)
    answer = (partial_value / weight_sum[..., None]).reshape(QUESTION_LIMIT, heads_q * HEAD_SIZE)
    chosen = (jnp.arange(QUESTION_LIMIT, dtype=jnp.int32) < question_count) & is_start
    head_rows = jnp.where(chosen[:, None], answer, banded[:QUESTION_LIMIT])
    return jnp.concatenate([head_rows, banded[QUESTION_LIMIT:]], axis=0).astype(jnp.bfloat16)


def solution(mesh):
    return jax.shard_map(
        per_device,
        mesh=mesh,
        in_specs=(
            P(("doc", "ctx"), None),
            P(("doc", "ctx"), None),
            P("ctx", None),
            P("ctx", None),
            P("doc"),
            P("doc"),
        ),
        out_specs=P(("doc", "ctx"), None),
        check_vma=False,
    )
```

profile of v0, /device:TPU:10, one launch (start us, length us, event | category | flops | bytes accessed | tf_op | source)
XLA Modules:
  0.0 597.9 jit_solution(6435852701368145705)
XLA Ops:
  8.1 1.4 slice.27
  17.6 1.4 select_reduce_fusion.1
  21.7 74.7 %all-gather.4.cloned.1.call-done = bf16[3584,256]{1,0:T(8,128)(2,1)} async-done(((bf16[112,256]{1,0:T(8,128)(2,1)}), bf16[3584,256]{1,0:T(8,128)(2,1)}) %all-gather.4.cloned.1.call-update) | async-done | bytes 1835024 | tf_op jit(solution)/shard_map/all_gather | solution.py:48
  96.4 1.9 convolution_convert_fusion.1
  98.3 81.7 %all-gather.6.cloned.1.call-done = bf16[3584,256]{1,0:T(8,128)(2,1)} async-done(((bf16[112,256]{1,0:T(8,128)(2,1)}), bf16[3584,256]{1,0:T(8,128)(2,1)}) %all-gather.6.cloned.1.call-update) | async-done | bytes 1835024 | tf_op jit(solution)/shard_map/all_gather | solution.py:43
  180.0 1.9 convolution_convert_fusion
  181.9 3.6 collective-permute-start
  185.5 3.4 collective-permute-start.1
  188.9 4.1 collective-permute-start.2
  193.0 3.7 collective-permute-start.3
  196.7 2.1 collective-permute-start.4
  198.9 48.5 %all_gather.15 = bf16[512,512]{1,0:T(8,128)(2,1)S(1)} all-gather(bf16[16,512]{1,0:T(8,128)(2,1)S(1)} %fusion.39), channel_id=1, replica_groups=mesh['doc'=16,'ctx'=32] {'ctx'}, dimensions={0}, use_global_device_ids=true | all-gather | bytes 540672 | tf_op jit(solution)/shard_map/all_gather | solution.py:69
  247.4 16.4 %all-gather.8.cloned.1.call-done = bf16[512,1792]{1,0:T(8,128)(2,1)} async-done(((bf16[16,1792]{1,0:T(8,128)(2,1)}), bf16[512,1792]{1,0:T(8,128)(2,1)}) %all-gather.8.cloned.1.call-update) | async-done | bytes 1835024 | tf_op jit(solution)/shard_map/all_gather | solution.py:68
  265.1 130.6 %pmax.7 = f32[2,16,2,7]{3,2,1,0:T(2,128)S(1)} all-reduce(f32[2,16,2,7]{3,2,1,0:T(2,128)S(1)} %broadcast_select_fusion.2), channel_id=1, replica_groups=mesh['doc'=16,'ctx'=32] {'ctx'}, use_global_device_ids=true, to_apply=%region_5.6 | all-reduce | flops 448 | bytes 3584 | tf_op jit(solution)/shard_map/pmax | solution.py:144
  397.4 139.9 %psum.15 = f32[2,16,2,7]{3,2,1,0:T(2,128)S(1)} all-reduce(f32[2,16,2,7]{3,2,1,0:T(2,128)S(1)} %broadcast_select_fusion.1), channel_id=1, replica_groups=mesh['doc'=16,'ctx'=32] {'ctx'}, use_global_device_ids=true, to_apply=%region_8.9 | all-reduce | flops 448 | bytes 3584 | tf_op jit(solution)/shard_map/psum | solution.py:151
  537.4 6.1 %collective-permute-start.5 = (bf16[128,512]{1,0:T(8,128)(2,1)S(1)}, bf16[128,512]{1,0:T(8,128)(2,1)S(1)}, u32[]{:S(2)}, u32[]{:S(2)}) collective-permute-start(bf16[128,512]{1,0:T(8,128)(2,1)S(1)} %pad_maximum_fusion.1), channel_id=1, source_target_pairs={{2,0},{3,1},{4,2},{5,3},{6,4},{7,5},{8,6},{9,7},{10,8},{11,9},{12,... | collective-permute-start | bytes 393224 | tf_op jit(solution)/shard_map/ppermute | solution.py:20
  543.6 8.6 %collective-permute-start.6 = (bf16[128,512]{1,0:T(8,128)(2,1)S(1)}, bf16[128,512]{1,0:T(8,128)(2,1)S(1)}, u32[]{:S(2)}, u32[]{:S(2)}) collective-permute-start(bf16[128,512]{1,0:T(8,128)(2,1)S(1)} %pad_maximum_fusion.1), channel_id=1, source_target_pairs={{3,0},{4,1},{5,2},{6,3},{7,4},{8,5},{9,6},{10,7},{11,8},{12,9},{13... | collective-permute-start | bytes 393224 | tf_op jit(solution)/shard_map/ppermute | solution.py:20
  552.2 1.9 collective-permute-start.7
  554.7 4.4 collective-permute-done.7
  559.2 28.6 %while.13 = (s32[]{:T(128)}, bf16[2,128,7,128]{1,3,2,0:T(8,128)(2,1)}, s32[2]{0:T(128)S(1)}, bf16[1152,512]{1,0:T(8,128)(2,1)S(1)}, bf16[128,1792]{1,0:T(8,128)(...) while((s32[]{:T(128)}, ...), condition=%wide.region_15.16_spmd.clone, body=%wide.region_10.15_spmd.clone.sunk | while | flops 544112896 | bytes 39041256 | solution.py:130
  563.1 2.7 fusion.73
  568.0 3.2 fusion.75
  577.4 2.7 fusion.73
  582.3 3.2 fusion.75
  (107 shorter events, 28.1 us)
Async XLA Ops:
  6.5 89.9 %copy-start = (bf16[128,3584]{1,0:T(8,128)(2,1)S(1)}, bf16[128,3584]{1,0:T(8,128)(2,1)}, u32[]{:S(2)}) copy-start(bf16[128,3584]{1,0:T(8,128)(2,1)} %param.8) | copy-start | bytes 2752516
  6.5 89.9 %all-gather.4.cloned.1.call-start = ((), (), s32[]{:S(2)}) async-start(), calls=%async_computation | async-start | bytes 1892352 | tf_op jit(solution)/shard_map/all_gather | solution.py:48
  7.3 172.7 %all-gather.6.cloned.1.call-start = ((), (), s32[]{:S(2)}) async-start(), calls=%async_computation.1 | async-start | bytes 1892352 | tf_op jit(solution)/shard_map/all_gather | solution.py:43
  8.0 255.7 %all-gather.8.cloned.1.call-start = ((), (), s32[]{:S(2)}) async-start(), calls=%async_computation.2 | async-start | bytes 1892352 | tf_op jit(solution)/shard_map/all_gather | solution.py:68
  9.5 580.0 %all-reduce.2.cloned.1.call-start = ((), (), s32[]{:S(2)}) async-start(), calls=%async_computation.3 | async-start | bytes 524288 | tf_op jit(solution)/shard_map/psum | solution.py:151
  181.9 355.5 %collective-permute-start = (bf16[128,512]{1,0:T(8,128)(2,1)S(1)}, bf16[128,512]{1,0:T(8,128)(2,1)S(1)}, u32[]{:S(2)}, u32[]{:S(2)}) collective-permute-start(bf16[128,512]{1,0:T(8,128)(2,1)S(1)} %pad_maximum_fusion.1), channel_id=1, source_target_pairs={{0,4},{1,5},{2,6},{3,7},{4,8},{5,9},{6,10},{7,11},{8,12},{9,13},{1... | collective-permute-start | bytes 393224 | tf_op jit(solution)/shard_map/ppermute | solution.py:20
  185.5 358.1 %collective-permute-start.1 = (bf16[128,512]{1,0:T(8,128)(2,1)S(1)}, bf16[128,512]{1,0:T(8,128)(2,1)S(1)}, u32[]{:S(2)}, u32[]{:S(2)}) collective-permute-start(bf16[128,512]{1,0:T(8,128)(2,1)S(1)} %pad_maximum_fusion.1), channel_id=1, source_target_pairs={{0,3},{1,4},{2,5},{3,6},{4,7},{5,8},{6,9},{7,10},{8,11},{9,12},{10... | collective-permute-start | bytes 393224 | tf_op jit(solution)/shard_map/ppermute | solution.py:20
  188.9 363.3 %collective-permute-start.2 = (bf16[128,512]{1,0:T(8,128)(2,1)S(1)}, bf16[128,512]{1,0:T(8,128)(2,1)S(1)}, u32[]{:S(2)}, u32[]{:S(2)}) collective-permute-start(bf16[128,512]{1,0:T(8,128)(2,1)S(1)} %pad_maximum_fusion.1), channel_id=1, source_target_pairs={{0,2},{1,3},{2,4},{3,5},{4,6},{5,7},{6,8},{7,9},{8,10},{9,11},{10,... | collective-permute-start | bytes 393224 | tf_op jit(solution)/shard_map/ppermute | solution.py:20
  193.0 361.2 %collective-permute-start.3 = (bf16[128,512]{1,0:T(8,128)(2,1)S(1)}, bf16[128,512]{1,0:T(8,128)(2,1)S(1)}, u32[]{:S(2)}, u32[]{:S(2)}) collective-permute-start(bf16[128,512]{1,0:T(8,128)(2,1)S(1)} %pad_maximum_fusion.1), channel_id=1, source_target_pairs={{0,1},{1,2},{2,3},{3,4},{4,5},{5,6},{6,7},{7,8},{8,9},{9,10},{10,1... | collective-permute-start | bytes 393224 | tf_op jit(solution)/shard_map/ppermute | solution.py:20
  196.7 357.5 %collective-permute-start.4 = (bf16[128,512]{1,0:T(8,128)(2,1)S(1)}, bf16[128,512]{1,0:T(8,128)(2,1)S(1)}, u32[]{:S(2)}, u32[]{:S(2)}) collective-permute-start(bf16[128,512]{1,0:T(8,128)(2,1)S(1)} %pad_maximum_fusion.1), channel_id=1, source_target_pairs={{1,0},{2,1},{3,2},{4,3},{5,4},{6,5},{7,6},{8,7},{9,8},{10,9},{11,1... | collective-permute-start | bytes 393224 | tf_op jit(solution)/shard_map/ppermute | solution.py:20
  537.4 16.8 %collective-permute-start.5 = (bf16[128,512]{1,0:T(8,128)(2,1)S(1)}, bf16[128,512]{1,0:T(8,128)(2,1)S(1)}, u32[]{:S(2)}, u32[]{:S(2)}) collective-permute-start(bf16[128,512]{1,0:T(8,128)(2,1)S(1)} %pad_maximum_fusion.1), channel_id=1, source_target_pairs={{2,0},{3,1},{4,2},{5,3},{6,4},{7,5},{8,6},{9,7},{10,8},{11,9},{12,... | collective-permute-start | bytes 393224 | tf_op jit(solution)/shard_map/ppermute | solution.py:20
  543.6 11.1 %collective-permute-start.6 = (bf16[128,512]{1,0:T(8,128)(2,1)S(1)}, bf16[128,512]{1,0:T(8,128)(2,1)S(1)}, u32[]{:S(2)}, u32[]{:S(2)}) collective-permute-start(bf16[128,512]{1,0:T(8,128)(2,1)S(1)} %pad_maximum_fusion.1), channel_id=1, source_target_pairs={{3,0},{4,1},{5,2},{6,3},{7,4},{8,5},{9,6},{10,7},{11,8},{12,9},{13... | collective-permute-start | bytes 393224 | tf_op jit(solution)/shard_map/ppermute | solution.py:20
  552.2 6.9 %collective-permute-start.7 = (bf16[128,512]{1,0:T(8,128)(2,1)S(1)}, bf16[128,512]{1,0:T(8,128)(2,1)S(1)}, u32[]{:S(2)}, u32[]{:S(2)}) collective-permute-start(bf16[128,512]{1,0:T(8,128)(2,1)S(1)} %pad_maximum_fusion.1), channel_id=1, source_target_pairs={{4,0},{5,1},{6,2},{7,3},{8,4},{9,5},{10,6},{11,7},{12,8},{13,9},{1... | collective-permute-start | bytes 393224 | tf_op jit(solution)/shard_map/ppermute | solution.py:20
  568.0 3.4 copy-start.1
  571.4 0.8 copy-start.2
  571.4 1.1 copy-start.3
  572.7 0.8 copy-start.4
  582.3 3.4 copy-start.1
  585.7 0.8 copy-start.2
  585.7 1.1 copy-start.3
  587.0 0.8 copy-start.4
  587.8 1.5 copy-start.5
Sparse Core Ops, SparseCore 0:
  10.5 85.8 all-gather.3
  99.5 80.4 all-gather.5
  183.2 80.5 all-gather.7
  397.3 162.2 all-reduce.1
where the time goes:
time: 599 us; the launch traced here: 598 us
  blocking collectives  319 us (53%)
  waiting for transfers between devices  179 us (30%)
  starting transfers between devices  33.6 us (6%)
  between operations  19.3 us (3%)
  matrix products  18.1 us (3%)
  local copies, waits for them, and re-layouts  13.2 us (2%)
  other arithmetic  13 us (2%)
    psum x1, blocking collectives, per_device(): lax.psum((jnp.where(doc_slot[:, None, None, None, None], partial_value[No...  140 us
    pmax x1, blocking collectives, per_device(): highest_all = lax.pmax(marked, 'ctx')  131 us
    all_gather x1, waiting for transfers between devices, per_device(): lax.all_gather(key_matrix, 'ctx', axis=0, tiled=True)  81.7 us
    all_gather x1, waiting for transfers between devices, per_device(): lax.all_gather(value_matrix, 'ctx', axis=0, tiled=True)  74.7 us
    all_gather x1, blocking collectives, per_device(): lax.all_gather(head_keyvals, 'ctx', axis=0, tiled=True)  48.5 us
    ppermute x8, starting transfers between devices, from_behind(): return lax.ppermute(shard, axis, pairs)  33.5 us
    all_gather x1, waiting for transfers between devices, per_device(): lax.all_gather(head_queries, 'ctx', axis=0, tiled=True)  16.4 us
  transfers between devices with their start and end apart: 12, of which 5 were waited for; matrix products, arithmetic and copies ran while one was open for 7% of the time, Pallas kernels for 0%

commit v1 on v0

v1 whole, which is shorter than its diff:
```python
import functools
import math

import jax
import jax.numpy as jnp
from jax import lax
from jax.experimental import pallas as pl
from jax.experimental.pallas import tpu as pltpu
from jax.sharding import Mesh, PartitionSpec as P

HEAD = 128
TILE = 512
ASK = 16
GROUP = 7
KV = 2
ROWS = 128
XS = 4
YS = 8
PACK = KV * GROUP * ASK + 16
SCALE = 1.0 / math.sqrt(HEAD)
MASKED = -1e30
NT = (((1,), (1,)), ((), ()))
bf16, f32 = jnp.bfloat16, jnp.float32

Y, X, CORE, START, STOP, ASKED = range(6)


def spec(space):
    return pl.BlockSpec(memory_space=space)


def call(body, out, ins, scratch=(), flops=0, moved=0):
    return pl.pallas_call(
        body,
        out_shape=out,
        in_specs=[spec(pltpu.SMEM)] + [spec(pltpu.VMEM)] * (ins - 1),
        out_specs=spec(pltpu.VMEM),
        scratch_shapes=list(scratch),
        compiler_params=pltpu.CompilerParams(vmem_limit_bytes=24 * 1024 * 1024),
        cost_estimate=pl.CostEstimate(flops=flops, bytes_accessed=moved, transcendentals=0),
    )


def project_body(ids, weights, mine, theirs, out, whole):
    depth = weights.shape[2]
    for x in range(XS):
        for y in range(YS):
            whole[pl.ds((XS * y + x) * depth, depth), :] = weights[x, y]
    core = ids[CORE]
    for part, tokens in ((core, mine), (1 - core, theirs)):
        rows = jnp.dot(tokens[...], whole[...], preferred_element_type=f32).astype(bf16)
        for x in range(XS):
            out[part, x] = rows


def to_row(column):
    shape = (column.shape[0], 128)
    same = lax.broadcasted_iota(jnp.int32, shape, 0) == lax.broadcasted_iota(jnp.int32, shape, 1)
    return jnp.sum(jnp.where(same, column, 0.0), axis=0, keepdims=True)


def to_column(row, n):
    shape = (n, 128)
    same = lax.broadcasted_iota(jnp.int32, shape, 0) == lax.broadcasted_iota(jnp.int32, shape, 1)
    return jnp.sum(jnp.where(same, row, 0.0), axis=1, keepdims=True)


def ask_body(ids, tile, asked, out):
    start = ids[START]
    tail = jnp.zeros((16, 128), f32)
    place = lax.broadcasted_iota(jnp.int32, (16, 128), 0)
    rows = asked[start]
    parts = []
    for h in range(KV):
        queries = jnp.concatenate(
            [rows[:, (GROUP * h + g) * HEAD : (GROUP * h + g + 1) * HEAD] for g in range(GROUP)], axis=0
        )
        keys = tile[0, :, h * HEAD : (h + 1) * HEAD]
        values = tile[1, :, h * HEAD : (h + 1) * HEAD]
        scores = lax.dot_general(queries, keys, NT, preferred_element_type=f32) * SCALE
        peak = jnp.max(scores, axis=1, keepdims=True)
        weights = jnp.exp(scores - peak)
        total = jnp.sum(weights, axis=1, keepdims=True)
        high = weights.astype(bf16)
        low = (weights - high.astype(f32)).astype(bf16)
        sums = jnp.dot(high, values, preferred_element_type=f32)
        sums = sums + jnp.dot(low, values, preferred_element_type=f32)
        parts.append((sums / total).astype(bf16))
        rest = to_row(peak + jnp.log(total))
        for i in range(3):
            piece = rest.astype(bf16).astype(f32)
            tail = jnp.where(place == 3 * h + i, piece, tail)
            rest = rest - piece
    parts.append(tail.astype(bf16))
    packed = jnp.concatenate(parts, axis=0)
    for y in range(YS):
        out[y] = packed

    @pl.when(ids[Y] == start)
    def _():
        for y in range(YS):

            @pl.when(start != y)
            def _():
                for kind in range(2):
                    for h in range(KV):
                        out[y, pl.ds((KV * kind + h) * ASK, ASK), :] = tile[
                            kind, 0:ASK, h * HEAD : (h + 1) * HEAD
                        ]


def attend_body(ids, queries, own, above, below, packs, out, side, bias):
    y, x, start, stop, asked = ids[Y], ids[X], ids[START], ids[STOP], ids[ASKED]
    for kind in range(2):
        side[kind, 0:ROWS, :] = above[kind, pl.ds(pl.multiple_of(x * ROWS, ROWS), ROWS), :]
        side[kind, 4 * ROWS : 5 * ROWS, :] = below[kind, pl.ds(pl.multiple_of(x * ROWS, ROWS), ROWS), :]
        for i in range(1, 4):

            @pl.when(x + i < XS)
            def _():
                at = pl.multiple_of(jnp.minimum(x + i, XS - 1) * ROWS, ROWS)
                side[kind, i * ROWS : (i + 1) * ROWS, :] = above[kind, pl.ds(at, ROWS), :]

            @pl.when(x + i >= XS)
            def _():
                at = pl.multiple_of(jnp.maximum(x + i - XS, 0) * ROWS, ROWS)
                side[kind, i * ROWS : (i + 1) * ROWS, :] = below[kind, pl.ds(at, ROWS), :]

        for h in range(KV):
            side[kind, 5 * ROWS : 5 * ROWS + ASK, h * HEAD : (h + 1) * HEAD] = packs[
                start, pl.ds((KV * kind + h) * ASK, ASK), :
            ]
        side[kind, 5 * ROWS + ASK :, :] = jnp.zeros((ROWS - ASK, KV * HEAD), bf16)

    i = lax.broadcasted_iota(jnp.int32, (ROWS, ROWS), 0)
    j = lax.broadcasted_iota(jnp.int32, (ROWS, ROWS), 1)
    up, down = y > start, y + 1 < stop
    first = jnp.where((y == start + 1) & (x == 0), asked, 0)
    limit = jnp.where(up, 0, ROWS)
    bias[:, 0:ROWS] = jnp.where((j >= i) & (j >= first) & (j >= limit), 0.0, MASKED)
    for b in range(1, 4):
        fine = jnp.where(x + b < XS, up.astype(jnp.int32), down.astype(jnp.int32))
        bias[:, b * ROWS : (b + 1) * ROWS] = jnp.where(j < fine * ROWS, 0.0, MASKED)
    limit = jnp.where(down, ROWS, 0)
    bias[:, 4 * ROWS : 5 * ROWS] = jnp.where((j <= i) & (j < limit), 0.0, MASKED)
    bias[:, 5 * ROWS :] = jnp.where(j < jnp.where(up, asked, 0), 0.0, MASKED)

    for h in range(KV):
        columns = slice(h * HEAD, (h + 1) * HEAD)
        for g in range(GROUP):
            mine = slice((GROUP * h + g) * HEAD, (GROUP * h + g + 1) * HEAD)
            q = queries[:, mine]
            near = lax.dot_general(q, own[0, :, columns], NT, preferred_element_type=f32) * SCALE
            far = lax.dot_general(q, side[0, :, columns], NT, preferred_element_type=f32) * SCALE + bias[...]
            peak = jnp.maximum(jnp.max(near, axis=1, keepdims=True), jnp.max(far, axis=1, keepdims=True))
            near = jnp.exp(near - peak)
            far = jnp.exp(far - peak)
            total = jnp.sum(near, axis=1, keepdims=True) + jnp.sum(far, axis=1, keepdims=True)
            sums = jnp.dot(near.astype(bf16), own[1, :, columns], preferred_element_type=f32)
            sums = sums + jnp.dot(far.astype(bf16), side[1, :, columns], preferred_element_type=f32)
            out[:, mine] = (sums / total).astype(bf16)

    @pl.when((y == start) & (x == 0))
    def _():
        n = GROUP * ASK
        for h in range(KV):
            logs = []
            for s in range(YS):
                tail = packs[s, KV * n : KV * n + 16, :].astype(f32)
                log = tail[3 * h : 3 * h + 1] + tail[3 * h + 1 : 3 * h + 2] + tail[3 * h + 2 : 3 * h + 3]
                logs.append(jnp.where((s >= start) & (s < stop), log, MASKED))
            peak = functools.reduce(jnp.maximum, logs)
            shares = [
                jnp.where((s >= start) & (s < stop), jnp.exp(logs[s] - peak), 0.0) for s in range(YS)
            ]
            total = sum(shares)
            answer = jnp.zeros((n, HEAD), f32)
            for s in range(YS):
                block = packs[s, h * n : (h + 1) * n, :].astype(f32)
                block = jnp.where((s >= start) & (s < stop), block, 0.0)
                answer = answer + to_column(shares[s] / total, n) * block
            chosen = lax.broadcasted_iota(jnp.int32, (ASK, HEAD), 0) < asked
            for g in range(GROUP):
                mine = slice((GROUP * h + g) * HEAD, (GROUP * h + g + 1) * HEAD)
                old = out[0:ASK, mine].astype(f32)
                out[0:ASK, mine] = jnp.where(chosen, answer[g * ASK : (g + 1) * ASK], old).astype(bf16)


def exchange(array, axis):
    return lax.all_to_all(array, axis, 0, 0, tiled=False)


def copies(array, n):
    return jnp.broadcast_to(array[None], (n,) + array.shape)


def per_device(tokens, queries, key_matrix, value_matrix, doc_tiles, question_lengths):
    y, x, core = lax.axis_index("y"), lax.axis_index("x"), lax.axis_index("core")
    theirs = lax.ppermute(tokens, "core", [(0, 1), (1, 0)])

    shard = jnp.where(core == 0, key_matrix, value_matrix)
    column = exchange(copies(shard, YS), "y")
    column, head = lax.optimization_barrier((column, queries[:ASK]))
    weights = exchange(copies(column, XS), "x")
    asked = exchange(copies(head, YS), "y")

    second = y >= doc_tiles[0]
    ids = jnp.stack(
        [
            y,
            x,
            core,
            jnp.where(second, doc_tiles[0], 0),
            jnp.where(second, doc_tiles[0] + doc_tiles[1], doc_tiles[0]),
            jnp.where(second, question_lengths[1], question_lengths[0]),
        ]
    ).astype(jnp.int32)

    rows = call(
        project_body,
        jax.ShapeDtypeStruct((2, XS, ROWS, KV * HEAD), bf16),
        4,
        [pltpu.VMEM((weights.shape[0] * weights.shape[1] * weights.shape[2], KV * HEAD), bf16)],
        flops=2 * 2 * tokens.size * KV * HEAD,
        moved=4 * tokens.size + 2 * weights.size,
    )(ids, weights, tokens, theirs)
    tile = exchange(rows.reshape(2 * XS, ROWS, KV * HEAD), ("core", "x")).reshape(2, TILE, KV * HEAD)

    packs = call(
        ask_body,
        jax.ShapeDtypeStruct((YS, PACK, HEAD), bf16),
        3,
        flops=3 * 2 * KV * GROUP * ASK * TILE * HEAD,
        moved=2 * tile.size + 4 * YS * PACK * HEAD,
    )(ids, tile, asked)
    packs = exchange(packs, "y")
    above = lax.ppermute(tile, "y", [(i, i + 1) for i in range(YS - 1)])
    below = lax.ppermute(tile, "y", [(i + 1, i) for i in range(YS - 1)])

    return call(
        attend_body,
        jax.ShapeDtypeStruct(queries.shape, bf16),
        6,
        [pltpu.VMEM((2, 6 * ROWS, KV * HEAD), bf16), pltpu.VMEM((ROWS, 6 * ROWS), f32)],
        flops=4 * queries.size * 10 * ROWS,
        moved=4 * queries.size + 6 * tile.size + 2 * packs.size,
    )(ids, queries, tile, above, below, packs)


def solution(mesh):
    devices = mesh.devices
    split = Mesh(devices.reshape(devices.shape[0] // 2, 2, YS, XS), ("z", "core", "y", "x"))
    rows = P(("z", "core", "y", "x"), None)
    return jax.shard_map(
        per_device,
        mesh=split,
        in_specs=(
            rows,
            rows,
            P(("y", "x"), None),
            P(("y", "x"), None),
            P(("z", "core")),
            P(("z", "core")),
        ),
        out_specs=rows,
        check_vma=False,
    )
```

time: 599 us -> 125 us (0.21)
  the two profiles are of different devices: /device:TPU:10 before, /device:TPU:472 now
where the time goes in v1:
time: 125 us; the launch traced here: 124 us
  waiting for transfers between devices  55.2 us (44%)
  starting transfers between devices  35.9 us (29%)
  blocking collectives  12.1 us (10%)
  Pallas kernels  11.3 us (9%)
  local copies, waits for them, and re-layouts  4.41 us (4%)
  between operations  4.25 us (3%)
    all_to_all x4, waiting for transfers between devices, exchange(): return lax.all_to_all(array, axis, 0, 0, tiled=False)  36.4 us
    all_to_all x4, starting transfers between devices, exchange(): return lax.all_to_all(array, axis, 0, 0, tiled=False)  27.5 us
    ppermute x1, waiting for transfers between devices, per_device(): above = lax.ppermute(tile, 'y', [(i, i + 1) for i in range(YS - 1)])  16.5 us
    all_to_all x1, blocking collectives, exchange(): return lax.all_to_all(array, axis, 0, 0, tiled=False)  12.1 us
    pallas_call x1, Pallas kernels, per_device(): call(attend_body, jax.ShapeDtypeStruct(queries.shape, bf16), 6, [pltpu.VM...  7.06 us
    ppermute x1, starting transfers between devices, per_device(): above = lax.ppermute(tile, 'y', [(i, i + 1) for i in range(YS - 1)])  4.58 us
    broadcast_in_dim x3, local copies, waits for them, and re-layouts, copies(): return jnp.broadcast_to(array[None], (n,) + array.shape)  3 us
  transfers between devices with their start and end apart: 7, of which 5 were waited for; matrix products, arithmetic and copies ran while one was open for 2% of the time, Pallas kernels for 2%

profile of v1, /device:TPU:472, one launch (start us, length us, event | category | flops | bytes accessed | tf_op | source)
XLA Modules:
  0.0 124.0 jit_solution(18378455099823683745)
XLA Ops:
  0.0 0.8 broadcast_select_fusion
  0.8 0.8 broadcast_in_dim.6
  1.6 7.3 %all-to-all-start = ((bf16[8,112,256]{2,1,0:T(8,128)(2,1)}), bf16[8,112,256]{2,1,0:T(8,128)(2,1)S(1)}, u32[]{:S(2)}, u32[]{:S(2)}) async-start(bf16[8,112,256]{2,1,0:T(8,128)(2,1)} %broadcast_in_dim.6), calls=%async_computation | async-start | bytes 917504 | tf_op jit(solution)/shard_map/all_to_all | solution.py:190
  9.0 12.2 %all-to-all-done = bf16[8,112,256]{2,1,0:T(8,128)(2,1)S(1)} async-done(((bf16[8,112,256]{2,1,0:T(8,128)(2,1)}), bf16[8,112,256]{2,1,0:T(8,128)(2,1)S(1)}, u32[]{:S(2)}, u32[]{:S(2)}) %all-to-all-start) | async-done | bytes 458784 | tf_op jit(solution)/shard_map/all_to_all | solution.py:190
  21.2 1.4 %broadcast_in_dim.7 = bf16[4,8,112,256]{3,2,1,0:T(8,128)(2,1)} broadcast(bf16[8,112,256]{2,1,0:T(8,128)(2,1)S(1)} %all-to-all-done), dimensions={1,2,3} | broadcast | bytes 2293760 | tf_op jit(solution)/shard_map/broadcast_in_dim | solution.py:194
  22.6 4.4 %all-to-all-start.1 = ((bf16[4,8,112,256]{3,2,1,0:T(8,128)(2,1)}), bf16[4,8,112,256]{3,2,1,0:T(8,128)(2,1)S(1)}, u32[]{:S(2)}, u32[]{:S(2)}) async-start(bf16[4,8,112,256]{3,2,1,0:T(8,128)(2,1)} %broadcast_in_dim.7), calls=%async_computation.1 | async-start | bytes 3670016 | tf_op jit(solution)/shard_map/all_to_all | solution.py:190
  27.0 1.9 %collective-permute-start = (bf16[128,3584]{1,0:T(8,128)(2,1)}, bf16[128,3584]{1,0:T(8,128)(2,1)}, u32[]{:S(2)}, u32[]{:S(2)}) collective-permute-start(bf16[128,3584]{1,0:T(8,128)(2,1)} %mine.1), channel_id=1, source_target_pairs={{0,32},{32,0},{1,33},{33,1},{2,34},{34,2},{3,35},{35,3},{4,36},{36... | collective-permute-start | bytes 2752520 | tf_op jit(solution)/shard_map/ppermute | solution.py:199
  28.9 20.4 %all-to-all-done.1.weights = bf16[4,8,112,256]{3,2,1,0:T(8,128)(2,1)S(1)} async-done(((bf16[4,8,112,256]{3,2,1,0:T(8,128)(2,1)}), bf16[4,8,112,256]{3,2,1,0:T(8,128)(2,1)S(1)}, u32[]{:S(2)}, u32[]{:S(2)}) %all-to-all-start.1) | async-done | bytes 1835040 | tf_op jit(solution)/shard_map/all_to_all | solution.py:190
  49.3 0.8 broadcast_in_dim.8
  50.1 8.5 %all-to-all-start.3 = ((bf16[8,16,1792]{2,1,0:T(8,128)(2,1)}), bf16[8,16,1792]{2,1,0:T(8,128)(2,1)S(1)}, u32[]{:S(2)}, u32[]{:S(2)}) async-start(bf16[8,16,1792]{2,1,0:T(8,128)(2,1)} %broadcast_in_dim.8), calls=%async_computation.3 | async-start | bytes 917504 | tf_op jit(solution)/shard_map/all_to_all | solution.py:190
  58.7 0.7 fusion.1
  62.3 0.6 fusion
  64.2 0.1 stack.27.ids
  64.3 2.1 %shard_map.64 = bf16[2,4,128,256]{3,2,1,0:T(8,128)(2,1)S(1)} custom-call(s32[6]{0:T(128)S(1)} %stack.27.ids, bf16[4,8,112,256]{3,2,1,0:T(8,128)(2,1)S(1)} %all-to-all-done.1.weights, bf16[128,3584]{1,0:T(8,128)(2,1)} %mine.1, bf16[128,3584]{1,0:T(8,128)(2,1)} %collective-permute-done.theirs), custom_call_target="tpu_custom_call" | custom-call | flops 469762048 | bytes 3670016 | tf_op jit(solution)/shard_map/pallas_call | solution.py:219
  66.4 0.0 copy-start
  66.4 3.7 %all-to-all-done.3.asked = bf16[8,16,1792]{2,1,0:T(8,128)(2,1)S(1)} async-done(((bf16[8,16,1792]{2,1,0:T(8,128)(2,1)}), bf16[8,16,1792]{2,1,0:T(8,128)(2,1)S(1)}, u32[]{:S(2)}, u32[]{:S(2)}) %all-to-all-start.3) | async-done | bytes 458784 | tf_op jit(solution)/shard_map/all_to_all | solution.py:190
  70.2 12.1 %all_to_all.25 = bf16[8,128,256]{2,1,0:T(8,128)(2,1)S(1)} all-to-all(bf16[8,128,256]{2,1,0:T(8,128)(2,1)S(1)} %bitcast.12), channel_id=1, replica_groups=mesh['z'=8,'core'=2,'y'=8,'x'=4] {'core','x'}, dimensions={0} | all-to-all | bytes 1048576 | tf_op jit(solution)/shard_map/all_to_all | solution.py:190
  82.3 2.1 %shard_map.65 = bf16[8,240,128]{2,1,0:T(8,128)(2,1)} custom-call(s32[6]{0:T(128)S(1)} %stack.27.ids, bf16[2,512,256]{2,1,0:T(8,128)(2,1)S(1)} %bitcast.13, bf16[8,16,1792]{2,1,0:T(8,128)(2,1)S(1)} %all-to-all-done.3.asked), custom_call_target="tpu_custom_call" | custom-call | flops 88080384 | bytes 1507328 | tf_op jit(solution)/shard_map/pallas_call | solution.py:229
  84.4 7.2 %all-to-all-start.4 = ((bf16[8,240,128]{2,1,0:T(8,128)(2,1)}), bf16[8,240,128]{2,1,0:T(8,128)(2,1)S(1)}, u32[]{:S(2)}, u32[]{:S(2)}) async-start(bf16[8,240,128]{2,1,0:T(8,128)(2,1)} %shard_map.65), calls=%async_computation.4 | async-start | bytes 983040 | tf_op jit(solution)/shard_map/all_to_all | solution.py:190
  91.6 4.6 %collective-permute-start.1 = (bf16[2,512,256]{2,1,0:T(8,128)(2,1)S(1)}, bf16[2,512,256]{2,1,0:T(8,128)(2,1)S(1)}, u32[]{:S(2)}, u32[]{:S(2)}) collective-permute-start(bf16[2,512,256]{2,1,0:T(8,128)(2,1)S(1)} %bitcast.14), channel_id=1, source_target_pairs={{0,4},{4,8},{8,12},{12,16},{16,20},{20,24},{24,28},{1,5},{5,9},{9,... | collective-permute-start | bytes 1572872 | tf_op jit(solution)/shard_map/ppermute | solution.py:237
  96.2 1.9 %collective-permute-start.2 = (bf16[2,512,256]{2,1,0:T(8,128)(2,1)S(1)}, bf16[2,512,256]{2,1,0:T(8,128)(2,1)S(1)}, u32[]{:S(2)}, u32[]{:S(2)}) collective-permute-start(bf16[2,512,256]{2,1,0:T(8,128)(2,1)S(1)} %bitcast.15), channel_id=1, source_target_pairs={{4,0},{8,4},{12,8},{16,12},{20,16},{24,20},{28,24},{5,1},{9,5},{13... | collective-permute-start | bytes 1572872 | tf_op jit(solution)/shard_map/ppermute | solution.py:238
  98.1 16.5 %collective-permute-done.1.above = bf16[2,512,256]{2,1,0:T(8,128)(2,1)S(1)} collective-permute-done((bf16[2,512,256]{2,1,0:T(8,128)(2,1)S(1)}, bf16[2,512,256]{2,1,0:T(8,128)(2,1)S(1)}, u32[]{:S(2)}, u32[]{:S(2)}) %collective-permute-start.1) | collective-permute-done | bytes 524320 | tf_op jit(solution)/shard_map/ppermute | solution.py:237
  114.6 2.4 %collective-permute-done.2.below = bf16[2,512,256]{2,1,0:T(8,128)(2,1)S(1)} collective-permute-done((bf16[2,512,256]{2,1,0:T(8,128)(2,1)S(1)}, bf16[2,512,256]{2,1,0:T(8,128)(2,1)S(1)}, u32[]{:S(2)}, u32[]{:S(2)}) %collective-permute-start.2) | collective-permute-done | bytes 524320 | tf_op jit(solution)/shard_map/ppermute | solution.py:238
  117.0 7.1 %shard_map.66 = bf16[128,1792]{1,0:T(8,128)(2,1)} custom-call(s32[6]{0:T(128)S(1)} %stack.27.ids, bf16[128,1792]{1,0:T(8,128)(2,1)S(1)} %copy-done, bf16[2,512,256]{2,1,0:T(8,128)(2,1)S(1)} %bitcast.16, bf16[2,512,256]{2,1,0:T(8,128)(2,1)S(1)} %collective-permute-done.1.above, bf16[2,512,256]{2,1,0:T(8,128)(2,1)S(1)} %collective-permute-done.2.below, ...), custom_call_target="tpu_custom_call" | custom-call | flops 1174405120 | bytes 2981888 | tf_op jit(solution)/shard_map/pallas_call | solution.py:240
  (9 shorter events, 0.0 us)
Async XLA Ops:
  1.6 19.5 %all-to-all-start = ((bf16[8,112,256]{2,1,0:T(8,128)(2,1)}), bf16[8,112,256]{2,1,0:T(8,128)(2,1)S(1)}, u32[]{:S(2)}, u32[]{:S(2)}) async-start(bf16[8,112,256]{2,1,0:T(8,128)(2,1)} %broadcast_in_dim.6), calls=%async_computation | async-start | bytes 917504 | tf_op jit(solution)/shard_map/all_to_all | solution.py:190
  22.6 26.8 %slice-start = ((bf16[128,1792]{1,0:T(8,128)(2,1)}), bf16[16,1792]{1,0:T(8,128)(2,1)S(1)}, s32[]{:S(2)}) async-start(bf16[128,1792]{1,0:T(8,128)(2,1)} %queries.1), calls=%async_computation.5 | async-start | bytes 114688 | tf_op jit(solution)/shard_map/slice | solution.py:203
  22.6 36.1 %copy-start.1 = (s32[2]{0:T(128)S(1)}, s32[2]{0:T(128)}, u32[]{:S(2)}) copy-start(s32[2]{0:T(128)} %param.10) | copy-start | bytes 28
  22.6 39.7 %copy-start.2 = (s32[2]{0:T(128)S(1)}, s32[2]{0:T(128)}, u32[]{:S(2)}) copy-start(s32[2]{0:T(128)} %param.11) | copy-start | bytes 28
  22.6 26.8 %all-to-all-start.1 = ((bf16[4,8,112,256]{3,2,1,0:T(8,128)(2,1)}), bf16[4,8,112,256]{3,2,1,0:T(8,128)(2,1)S(1)}, u32[]{:S(2)}, u32[]{:S(2)}) async-start(bf16[4,8,112,256]{3,2,1,0:T(8,128)(2,1)} %broadcast_in_dim.7), calls=%async_computation.1 | async-start | bytes 3670016 | tf_op jit(solution)/shard_map/all_to_all | solution.py:190
  27.0 37.3 %collective-permute-start = (bf16[128,3584]{1,0:T(8,128)(2,1)}, bf16[128,3584]{1,0:T(8,128)(2,1)}, u32[]{:S(2)}, u32[]{:S(2)}) collective-permute-start(bf16[128,3584]{1,0:T(8,128)(2,1)} %mine.1), channel_id=1, source_target_pairs={{0,32},{32,0},{1,33},{33,1},{2,34},{34,2},{3,35},{35,3},{4,36},{36... | collective-permute-start | bytes 2752520 | tf_op jit(solution)/shard_map/ppermute | solution.py:199
  50.1 20.0 %all-to-all-start.3 = ((bf16[8,16,1792]{2,1,0:T(8,128)(2,1)}), bf16[8,16,1792]{2,1,0:T(8,128)(2,1)S(1)}, u32[]{:S(2)}, u32[]{:S(2)}) async-start(bf16[8,16,1792]{2,1,0:T(8,128)(2,1)} %broadcast_in_dim.8), calls=%async_computation.3 | async-start | bytes 917504 | tf_op jit(solution)/shard_map/all_to_all | solution.py:190
  66.4 50.6 %copy-start = (bf16[128,1792]{1,0:T(8,128)(2,1)S(1)}, bf16[128,1792]{1,0:T(8,128)(2,1)}, u32[]{:S(2)}) copy-start(bf16[128,1792]{1,0:T(8,128)(2,1)} %queries.1) | copy-start | bytes 1376260
  84.4 32.6 %all-to-all-start.4 = ((bf16[8,240,128]{2,1,0:T(8,128)(2,1)}), bf16[8,240,128]{2,1,0:T(8,128)(2,1)S(1)}, u32[]{:S(2)}, u32[]{:S(2)}) async-start(bf16[8,240,128]{2,1,0:T(8,128)(2,1)} %shard_map.65), calls=%async_computation.4 | async-start | bytes 983040 | tf_op jit(solution)/shard_map/all_to_all | solution.py:190
  91.6 23.0 %collective-permute-start.1 = (bf16[2,512,256]{2,1,0:T(8,128)(2,1)S(1)}, bf16[2,512,256]{2,1,0:T(8,128)(2,1)S(1)}, u32[]{:S(2)}, u32[]{:S(2)}) collective-permute-start(bf16[2,512,256]{2,1,0:T(8,128)(2,1)S(1)} %bitcast.14), channel_id=1, source_target_pairs={{0,4},{4,8},{8,12},{12,16},{16,20},{20,24},{24,28},{1,5},{5,9},{9,... | collective-permute-start | bytes 1572872 | tf_op jit(solution)/shard_map/ppermute | solution.py:237
  96.2 20.8 %collective-permute-start.2 = (bf16[2,512,256]{2,1,0:T(8,128)(2,1)S(1)}, bf16[2,512,256]{2,1,0:T(8,128)(2,1)S(1)}, u32[]{:S(2)}, u32[]{:S(2)}) collective-permute-start(bf16[2,512,256]{2,1,0:T(8,128)(2,1)S(1)} %bitcast.15), channel_id=1, source_target_pairs={{4,0},{8,4},{12,8},{16,12},{20,16},{24,20},{28,24},{5,1},{9,5},{13... | collective-permute-start | bytes 1572872 | tf_op jit(solution)/shard_map/ppermute | solution.py:238

commit v2 on v1

--- a/solution.py
+++ b/solution.py
@@ -16,37 +16,44 @@
 ROWS = 128
 XS = 4
 YS = 8
-PACK = KV * GROUP * ASK + 16
+TOKENS = ASK // XS
+SLICE = 32
+PACK = KV * SLICE + 16
 SCALE = 1.0 / math.sqrt(HEAD)
 MASKED = -1e30
 NT = (((1,), (1,)), ((), ()))
 bf16, f32 = jnp.bfloat16, jnp.float32
 
-Y, X, CORE, START, STOP, ASKED = range(6)
-
-
 def spec(space):
     return pl.BlockSpec(memory_space=space)
 
 
-def call(body, out, ins, scratch=(), flops=0, moved=0):
+def call(body, out, ins, scratch=(), micros=1):
     return pl.pallas_call(
         body,
         out_shape=out,
-        in_specs=[spec(pltpu.SMEM)] + [spec(pltpu.VMEM)] * (ins - 1),
-        out_specs=spec(pltpu.VMEM),
+        in_specs=[spec(pltpu.SMEM)] * 2 + [spec(pltpu.VMEM)] * ins,
+        out_specs=jax.tree.map(lambda _: spec(pltpu.VMEM), out),
         scratch_shapes=list(scratch),
         compiler_params=pltpu.CompilerParams(vmem_limit_bytes=24 * 1024 * 1024),
-        cost_estimate=pl.CostEstimate(flops=flops, bytes_accessed=moved, transcendentals=0),
+        cost_estimate=pl.CostEstimate(flops=0, bytes_accessed=micros * 3690000, transcendentals=0),
     )
 
 
-def project_body(ids, weights, mine, theirs, out, whole):
+def place(tiles, lengths):
+    y, x = lax.axis_index("y"), lax.axis_index("x")
+    second = y >= tiles[0]
+    start = jnp.where(second, tiles[0], 0)
+    stop = jnp.where(second, tiles[0] + tiles[1], tiles[0])
+    return y, x, start, stop, jnp.where(second, lengths[1], lengths[0])
+
+
+def project_body(tiles, lengths, weights, mine, theirs, out, whole):
     depth = weights.shape[2]
     for x in range(XS):
         for y in range(YS):
             whole[pl.ds((XS * y + x) * depth, depth), :] = weights[x, y]
-    core = ids[CORE]
+    core = lax.axis_index("core")
     for part, tokens in ((core, mine), (1 - core, theirs)):
         rows = jnp.dot(tokens[...], whole[...], preferred_element_type=f32).astype(bf16)
         for x in range(XS):
@@ -65,16 +72,46 @@
     return jnp.sum(jnp.where(same, row, 0.0), axis=1, keepdims=True)
 
 
-def ask_body(ids, tile, asked, out):
-    start = ids[START]
+def cut_body(head, out):
+    rows = head[...].astype(f32)
+    blank = jnp.zeros((SLICE - GROUP * TOKENS, HEAD), f32)
+    for x in range(XS):
+        parts = []
+        for h in range(KV):
+            for g in range(GROUP):
+                n = GROUP * h + g
+                parts.append(rows[x * TOKENS : (x + 1) * TOKENS, n * HEAD : (n + 1) * HEAD])
+            parts.append(blank)
+        out[x] = jnp.concatenate(parts, axis=0).astype(bf16)
+
+
+def pick_body(tiles, lengths, own, r1, r2, r3, above, out):
+    y, x, start, _, _ = place(tiles, lengths)
+    for column, source in enumerate((own, r1, r2, r3)):
+
+        @pl.when((y == start) & (x == column))
+        def _():
+            out[...] = source[...]
+
+    @pl.when(y != start)
+    def _():
+        out[...] = above[...]
+
+
+def ask_body(tiles, lengths, tile, near, far2, far4, out, asked):
+    y, x, start, stop, _ = place(tiles, lengths)
+    shift = y - start
+    for low, high, source in ((0, 2, near), (2, 4, far2), (4, YS, far4)):
+
+        @pl.when((shift >= low) & (shift < high))
+        def _():
+            asked[...] = source[...]
+
     tail = jnp.zeros((16, 128), f32)
-    place = lax.broadcasted_iota(jnp.int32, (16, 128), 0)
-    rows = asked[start]
+    line = lax.broadcasted_iota(jnp.int32, (16, 128), 0)
     parts = []
     for h in range(KV):
-        queries = jnp.concatenate(
-            [rows[:, (GROUP * h + g) * HEAD : (GROUP * h + g + 1) * HEAD] for g in range(GROUP)], axis=0
-        )
+        queries = asked[h * SLICE : (h + 1) * SLICE, :]
         keys = tile[0, :, h * HEAD : (h + 1) * HEAD]
         values = tile[1, :, h * HEAD : (h + 1) * HEAD]
         scores = lax.dot_general(queries, keys, NT, preferred_element_type=f32) * SCALE
@@ -89,28 +126,47 @@
         rest = to_row(peak + jnp.log(total))
         for i in range(3):
             piece = rest.astype(bf16).astype(f32)
-            tail = jnp.where(place == 3 * h + i, piece, tail)
+            tail = jnp.where(line == 3 * h + i, piece, tail)
             rest = rest - piece
     parts.append(tail.astype(bf16))
     packed = jnp.concatenate(parts, axis=0)
-    for y in range(YS):
-        out[y] = packed
-
-    @pl.when(ids[Y] == start)
+    for to in range(YS):
+        out[to] = packed
+
+    @pl.when(y == start)
     def _():
-        for y in range(YS):
-
-            @pl.when(start != y)
+        for to in range(YS):
+
+            @pl.when(start != to)
             def _():
                 for kind in range(2):
                     for h in range(KV):
-                        out[y, pl.ds((KV * kind + h) * ASK, ASK), :] = tile[
+                        out[to, pl.ds((KV * kind + h) * ASK, ASK), :] = tile[
                             kind, 0:ASK, h * HEAD : (h + 1) * HEAD
                         ]
 
 
-def attend_body(ids, queries, own, above, below, packs, out, side, bias):
-    y, x, start, stop, asked = ids[Y], ids[X], ids[START], ids[STOP], ids[ASKED]
+def merge_body(tiles, lengths, packs, out):
+    _, _, start, stop, _ = place(tiles, lengths)
+    for h in range(KV):
+        logs = []
+        for s in range(YS):
+            tail = packs[s, KV * SLICE : KV * SLICE + 16, :].astype(f32)
+            log = tail[3 * h : 3 * h + 1] + tail[3 * h + 1 : 3 * h + 2] + tail[3 * h + 2 : 3 * h + 3]
+            logs.append(jnp.where((s >= start) & (s < stop), log, MASKED))
+        peak = functools.reduce(jnp.maximum, logs)
+        shares = [jnp.where((s >= start) & (s < stop), jnp.exp(logs[s] - peak), 0.0) for s in range(YS)]
+        total = sum(shares)
+        answer = jnp.zeros((SLICE, HEAD), f32)
+        for s in range(YS):
+            block = packs[s, h * SLICE : (h + 1) * SLICE, :].astype(f32)
+            block = jnp.where((s >= start) & (s < stop), block, 0.0)
+            answer = answer + to_column(shares[s] / total, SLICE) * block
+        out[h * SLICE : (h + 1) * SLICE, :] = answer.astype(bf16)
+
+
+def attend_body(tiles, lengths, queries, own, above, below, packs, a0, a1, a2, a3, out, side, bias):
+    y, x, start, stop, asked = place(tiles, lengths)
     for kind in range(2):
         side[kind, 0:ROWS, :] = above[kind, pl.ds(pl.multiple_of(x * ROWS, ROWS), ROWS), :]
         side[kind, 4 * ROWS : 5 * ROWS, :] = below[kind, pl.ds(pl.multiple_of(x * ROWS, ROWS), ROWS), :]
@@ -162,89 +218,80 @@
 
     @pl.when((y == start) & (x == 0))
     def _():
-        n = GROUP * ASK
+        chosen = lax.broadcasted_iota(jnp.int32, (ASK, HEAD), 0) < asked
+        answers = [a[...].astype(f32) for a in (a0, a1, a2, a3)]
         for h in range(KV):
-            logs = []
-            for s in range(YS):
-                tail = packs[s, KV * n : KV * n + 16, :].astype(f32)
-                log = tail[3 * h : 3 * h + 1] + tail[3 * h + 1 : 3 * h + 2] + tail[3 * h + 2 : 3 * h + 3]
-                logs.append(jnp.where((s >= start) & (s < stop), log, MASKED))
-            peak = functools.reduce(jnp.maximum, logs)
-            shares = [
-                jnp.where((s >= start) & (s < stop), jnp.exp(logs[s] - peak), 0.0) for s in range(YS)
-            ]
-            total = sum(shares)
-            answer = jnp.zeros((n, HEAD), f32)
-            for s in range(YS):
-                block = packs[s, h * n : (h + 1) * n, :].astype(f32)
-                block = jnp.where((s >= start) & (s < stop), block, 0.0)
-                answer = answer + to_column(shares[s] / total, n) * block
-            chosen = lax.broadcasted_iota(jnp.int32, (ASK, HEAD), 0) < asked
             for g in range(GROUP):
                 mine = slice((GROUP * h + g) * HEAD, (GROUP * h + g + 1) * HEAD)
+                at = h * SLICE + g * TOKENS
+                answer = jnp.concatenate([a[at : at + TOKENS] for a in answers], axis=0)
                 old = out[0:ASK, mine].astype(f32)
-                out[0:ASK, mine] = jnp.where(chosen, answer[g * ASK : (g + 1) * ASK], old).astype(bf16)
+                out[0:ASK, mine] = jnp.where(chosen, answer, old).astype(bf16)
 
 
 def exchange(array, axis):
     return lax.all_to_all(array, axis, 0, 0, tiled=False)
 
 
+def down(array, shift):
+    return lax.ppermute(array, "y", [(y, y + shift) for y in range(YS) if 0 <= y + shift < YS])
+
+
 def copies(array, n):
     return jnp.broadcast_to(array[None], (n,) + array.shape)
 
 
 def per_device(tokens, queries, key_matrix, value_matrix, doc_tiles, question_lengths):
-    y, x, core = lax.axis_index("y"), lax.axis_index("x"), lax.axis_index("core")
+    core = lax.axis_index("core")
+    plane = ("y", "x")
+    slice_shape = jax.ShapeDtypeStruct((KV * SLICE, HEAD), bf16)
+    at = (doc_tiles, question_lengths)
     theirs = lax.ppermute(tokens, "core", [(0, 1), (1, 0)])
+    slices = pl.pallas_call(
+        cut_body,
+        out_shape=jax.ShapeDtypeStruct((XS,) + slice_shape.shape, bf16),
+        in_specs=[spec(pltpu.VMEM)],
+        out_specs=spec(pltpu.VMEM),
+    )(queries[:ASK])
 
     shard = jnp.where(core == 0, key_matrix, value_matrix)
     column = exchange(copies(shard, YS), "y")
-    column, head = lax.optimization_barrier((column, queries[:ASK]))
+    spread = [
+        lax.ppermute(slices[x], plane, [(XS * y, XS * y + x) for y in range(YS)]) for x in range(1, XS)
+    ]
+    column, theirs, spread = lax.optimization_barrier((column, theirs, spread))
     weights = exchange(copies(column, XS), "x")
-    asked = exchange(copies(head, YS), "y")
-
-    second = y >= doc_tiles[0]
-    ids = jnp.stack(
-        [
-            y,
-            x,
-            core,
-            jnp.where(second, doc_tiles[0], 0),
-            jnp.where(second, doc_tiles[0] + doc_tiles[1], doc_tiles[0]),
-            jnp.where(second, question_lengths[1], question_lengths[0]),
-        ]
-    ).astype(jnp.int32)
+    joined = jnp.where(lax.axis_index("x") == 0, slices[0], spread[0] + spread[1] + spread[2])
+    first = down(joined, 1)
+    near = call(pick_body, slice_shape, 5)(*at, slices[0], *spread, first)
+    far2, far4 = down(near, 2), down(near, 4)
+    weights, near, far2, far4 = lax.optimization_barrier((weights, near, far2, far4))
 
     rows = call(
         project_body,
         jax.ShapeDtypeStruct((2, XS, ROWS, KV * HEAD), bf16),
-        4,
+        3,
         [pltpu.VMEM((weights.shape[0] * weights.shape[1] * weights.shape[2], KV * HEAD), bf16)],
-        flops=2 * 2 * tokens.size * KV * HEAD,
-        moved=4 * tokens.size + 2 * weights.size,
-    )(ids, weights, tokens, theirs)
+    )(*at, weights, tokens, theirs)
     tile = exchange(rows.reshape(2 * XS, ROWS, KV * HEAD), ("core", "x")).reshape(2, TILE, KV * HEAD)
 
     packs = call(
-        ask_body,
-        jax.ShapeDtypeStruct((YS, PACK, HEAD), bf16),
-        3,
-        flops=3 * 2 * KV * GROUP * ASK * TILE * HEAD,
-        moved=2 * tile.size + 4 * YS * PACK * HEAD,
-    )(ids, tile, asked)
+        ask_body, jax.ShapeDtypeStruct((YS, PACK, HEAD), bf16), 4, [pltpu.VMEM(slice_shape.shape, bf16)]
+    )(*at, tile, near, far2, far4)
     packs = exchange(packs, "y")
-    above = lax.ppermute(tile, "y", [(i, i + 1) for i in range(YS - 1)])
-    below = lax.ppermute(tile, "y", [(i + 1, i) for i in range(YS - 1)])
+    above, below = down(tile, 1), down(tile, -1)
+    answer = call(merge_body, slice_shape, 1)(*at, packs)
+    answers = [answer] + [
+        lax.ppermute(answer, plane, [(XS * y + x, XS * y) for y in range(YS)]) for x in range(1, XS)
+    ]
 
     return call(
         attend_body,
         jax.ShapeDtypeStruct(queries.shape, bf16),
-        6,
+        9,
         [pltpu.VMEM((2, 6 * ROWS, KV * HEAD), bf16), pltpu.VMEM((ROWS, 6 * ROWS), f32)],
-        flops=4 * queries.size * 10 * ROWS,
-        moved=4 * queries.size + 6 * tile.size + 2 * packs.size,
-    )(ids, queries, tile, above, below, packs)
+        micros=7,
+    )(*at, queries, tile, above, below, packs, *answers)
 
 
 def solution(mesh):

time: 125 us -> 112 us (0.90)
  the two profiles are of different devices: /device:TPU:472 before, /device:TPU:8 now
where the time goes in v2:
time: 112 us; the launch traced here: 111 us
  starting transfers between devices  38 us (34%)
  blocking collectives  27.8 us (25%)
  waiting for transfers between devices  25.2 us (22%)
  Pallas kernels  12.5 us (11%)
  local copies, waits for them, and re-layouts  5.76 us (5%)
  other arithmetic  1.56 us (1%)
    all_to_all x2, blocking collectives, exchange(): return lax.all_to_all(array, axis, 0, 0, tiled=False)  27.8 us
    all_to_all x2, waiting for transfers between devices, exchange(): return lax.all_to_all(array, axis, 0, 0, tiled=False)  14.2 us
    ppermute x5, starting transfers between devices, down(): lax.ppermute(array, 'y', [(y, y + shift) for y in range(YS) if 0 <= y + s...  13.7 us
    all_to_all x2, starting transfers between devices, exchange(): return lax.all_to_all(array, axis, 0, 0, tiled=False)  12.9 us
    pallas_call x1, Pallas kernels, per_device(): call(attend_body, jax.ShapeDtypeStruct(queries.shape, bf16), 9, [pltpu.VM...  7.26 us
    ppermute x3, starting transfers between devices, per_device(): lax.ppermute(slices[x], plane, [(XS * y, XS * y + x) for y in range(YS)])  5.58 us
    ppermute x5, waiting for transfers between devices, down(): lax.ppermute(array, 'y', [(y, y + shift) for y in range(YS) if 0 <= y + s...  5.13 us
    ppermute x3, waiting for transfers between devices, per_device(): lax.ppermute(answer, plane, [(XS * y + x, XS * y) for y in range(YS)])  4.54 us
  transfers between devices with their start and end apart: 14, of which 8 were waited for; matrix products, arithmetic and copies ran while one was open for 4% of the time, Pallas kernels for 4%

profile of v2, /device:TPU:8, one launch (start us, length us, event | category | flops | bytes accessed | tf_op | source)
XLA Modules:
  0.0 111.1 jit_solution(18111959755677689025)
XLA Ops:
  0.0 1.9 %collective-permute-start = (bf16[128,3584]{1,0:T(8,128)(2,1)}, bf16[128,3584]{1,0:T(8,128)(2,1)S(1)}, u32[]{:S(2)}, u32[]{:S(2)}) collective-permute-start(bf16[128,3584]{1,0:T(8,128)(2,1)} %mine.1), channel_id=1, source_target_pairs={{0,32},{32,0},{1,33},{33,1},{2,34},{34,2},{3,35},{35,3},{4,36},{36... | collective-permute-start | bytes 2752520 | tf_op jit(solution)/shard_map/ppermute | solution.py:249
  3.6 9.2 %all-to-all-start = ((bf16[8,112,256]{2,1,0:T(8,128)(2,1)}), bf16[8,112,256]{2,1,0:T(8,128)(2,1)S(1)}, u32[]{:S(2)}, u32[]{:S(2)}) async-start(bf16[8,112,256]{2,1,0:T(8,128)(2,1)} %broadcast_in_dim.4), calls=%async_computation | async-start | bytes 917504 | tf_op jit(solution)/shard_map/all_to_all | solution.py:233
  12.8 1.4 %slice.16.head = bf16[16,1792]{1,0:T(8,128)(2,1)} slice(bf16[128,1792]{1,0:T(8,128)(2,1)} %queries.1), slice={[0:16], [0:1792]} | slice | bytes 114688 | tf_op jit(solution)/shard_map/slice | solution.py:255
  14.2 1.5 %shard_map.64 = bf16[4,64,128]{2,1,0:T(8,128)(2,1)} custom-call(bf16[16,1792]{1,0:T(8,128)(2,1)} %slice.16.head), custom_call_target="tpu_custom_call" | custom-call | tf_op jit(solution)/shard_map/pallas_call | solution.py:250
  16.4 3.0 %collective-permute-start.3 = (bf16[64,128]{1,0:T(8,128)(2,1)S(1)}, bf16[64,128]{1,0:T(8,128)(2,1)S(1)}, u32[]{:S(2)}, u32[]{:S(2)}) collective-permute-start(bf16[64,128]{1,0:T(8,128)(2,1)S(1)} %get-tuple-element.24), channel_id=1, source_target_pairs={{0,3},{4,7},{8,11},{12,15},{16,19},{20,23},{24,27},{28,31},{32,35}... | collective-permute-start | bytes 49160 | tf_op jit(solution)/shard_map/ppermute | solution.py:260
  22.2 1.3 %collective-permute-done.1.r1 = bf16[64,128]{1,0:T(8,128)(2,1)S(1)} collective-permute-done((bf16[64,128]{1,0:T(8,128)(2,1)S(1)}, bf16[64,128]{1,0:T(8,128)(2,1)S(1)}, u32[]{:S(2)}, u32[]{:S(2)}) %collective-permute-start.1) | collective-permute-done | bytes 16416 | tf_op jit(solution)/shard_map/ppermute | solution.py:260
  23.5 4.9 %all-to-all-done = bf16[8,112,256]{2,1,0:T(8,128)(2,1)S(1)} async-done(((bf16[8,112,256]{2,1,0:T(8,128)(2,1)}), bf16[8,112,256]{2,1,0:T(8,128)(2,1)S(1)}, u32[]{:S(2)}, u32[]{:S(2)}) %all-to-all-start) | async-done | bytes 458784 | tf_op jit(solution)/shard_map/all_to_all | solution.py:233
  28.4 1.5 %broadcast_in_dim.5 = bf16[4,8,112,256]{3,2,1,0:T(8,128)(2,1)} broadcast(bf16[8,112,256]{2,1,0:T(8,128)(2,1)S(1)} %all-to-all-done), dimensions={1,2,3} | broadcast | bytes 2293760 | tf_op jit(solution)/shard_map/broadcast_in_dim | solution.py:241
  29.9 3.7 %all-to-all-start.1 = ((bf16[4,8,112,256]{3,2,1,0:T(8,128)(2,1)}), bf16[4,8,112,256]{3,2,1,0:T(8,128)(2,1)S(1)}, u32[]{:S(2)}, u32[]{:S(2)}) async-start(bf16[4,8,112,256]{3,2,1,0:T(8,128)(2,1)} %broadcast_in_dim.5), calls=%async_computation.1 | async-start | bytes 3670016 | tf_op jit(solution)/shard_map/all_to_all | solution.py:233
  34.4 1.9 %collective-permute-start.4 = (bf16[64,128]{1,0:T(8,128)(2,1)S(1)}, bf16[64,128]{1,0:T(8,128)(2,1)S(1)}, u32[]{:S(2)}, u32[]{:S(2)}) collective-permute-start(bf16[64,128]{1,0:T(8,128)(2,1)S(1)} %add_select_fusion), channel_id=1, source_target_pairs={{0,4},{4,8},{8,12},{12,16},{16,20},{20,24},{24,28},{1,5},{5,9},{9,... | collective-permute-start | bytes 49160 | tf_op jit(solution)/shard_map/ppermute | solution.py:237
  36.3 3.7 %collective-permute-done.4.above = bf16[64,128]{1,0:T(8,128)(2,1)S(1)} collective-permute-done((bf16[64,128]{1,0:T(8,128)(2,1)S(1)}, bf16[64,128]{1,0:T(8,128)(2,1)S(1)}, u32[]{:S(2)}, u32[]{:S(2)}) %collective-permute-start.4) | collective-permute-done | bytes 16416 | tf_op jit(solution)/shard_map/ppermute | solution.py:237
  40.6 3.3 %collective-permute-start.6 = (bf16[64,128]{1,0:T(8,128)(2,1)S(1)}, bf16[64,128]{1,0:T(8,128)(2,1)S(1)}, u32[]{:S(2)}, u32[]{:S(2)}) collective-permute-start(bf16[64,128]{1,0:T(8,128)(2,1)S(1)} %shard_map.65.near), channel_id=1, source_target_pairs={{0,16},{4,20},{8,24},{12,28},{1,17},{5,21},{9,25},{13,29},{2,18},{... | collective-permute-start | bytes 49160 | tf_op jit(solution)/shard_map/ppermute | solution.py:237
  43.9 2.7 %collective-permute-start.5 = (bf16[64,128]{1,0:T(8,128)(2,1)S(1)}, bf16[64,128]{1,0:T(8,128)(2,1)S(1)}, u32[]{:S(2)}, u32[]{:S(2)}) collective-permute-start(bf16[64,128]{1,0:T(8,128)(2,1)S(1)} %shard_map.65.near), channel_id=1, source_target_pairs={{0,8},{4,12},{8,16},{12,20},{16,24},{20,28},{1,9},{5,13},{9,17},{1... | collective-permute-start | bytes 49160 | tf_op jit(solution)/shard_map/ppermute | solution.py:237
  46.6 1.4 %collective-permute-done.5.far2 = bf16[64,128]{1,0:T(8,128)(2,1)S(1)} collective-permute-done((bf16[64,128]{1,0:T(8,128)(2,1)S(1)}, bf16[64,128]{1,0:T(8,128)(2,1)S(1)}, u32[]{:S(2)}, u32[]{:S(2)}) %collective-permute-start.5) | collective-permute-done | bytes 16416 | tf_op jit(solution)/shard_map/ppermute | solution.py:237
  48.0 9.3 %all-to-all-done.1.weights = bf16[4,8,112,256]{3,2,1,0:T(8,128)(2,1)S(1)} async-done(((bf16[4,8,112,256]{3,2,1,0:T(8,128)(2,1)}), bf16[4,8,112,256]{3,2,1,0:T(8,128)(2,1)S(1)}, u32[]{:S(2)}, u32[]{:S(2)}) %all-to-all-start.1) | async-done | bytes 1835040 | tf_op jit(solution)/shard_map/all_to_all | solution.py:233
  59.7 12.3 %all_to_all.20 = bf16[8,128,256]{2,1,0:T(8,128)(2,1)S(1)} all-to-all(bf16[8,128,256]{2,1,0:T(8,128)(2,1)S(1)} %bitcast.16), channel_id=1, replica_groups=mesh['z'=8,'core'=2,'y'=8,'x'=4] {'core','x'}, dimensions={0} | all-to-all | bytes 1048576 | tf_op jit(solution)/shard_map/all_to_all | solution.py:233
  72.0 3.8 %collective-permute-start.8 = (bf16[2,512,256]{2,1,0:T(8,128)(2,1)S(1)}, bf16[2,512,256]{2,1,0:T(8,128)(2,1)S(1)}, u32[]{:S(2)}, u32[]{:S(2)}) collective-permute-start(bf16[2,512,256]{2,1,0:T(8,128)(2,1)S(1)} %bitcast.12), channel_id=1, source_target_pairs={{4,0},{8,4},{12,8},{16,12},{20,16},{24,20},{28,24},{5,1},{9,5},{13... | collective-permute-start | bytes 1572872 | tf_op jit(solution)/shard_map/ppermute | solution.py:237
  75.7 2.1 %collective-permute-start.7 = (bf16[2,512,256]{2,1,0:T(8,128)(2,1)S(1)}, bf16[2,512,256]{2,1,0:T(8,128)(2,1)S(1)}, u32[]{:S(2)}, u32[]{:S(2)}) collective-permute-start(bf16[2,512,256]{2,1,0:T(8,128)(2,1)S(1)} %bitcast.13), channel_id=1, source_target_pairs={{0,4},{4,8},{8,12},{12,16},{16,20},{20,24},{24,28},{1,5},{5,9},{9,... | collective-permute-start | bytes 1572872 | tf_op jit(solution)/shard_map/ppermute | solution.py:237
  79.0 15.6 %all_to_all.21.packs = bf16[8,80,128]{2,1,0:T(8,128)(2,1)S(1)} all-to-all(bf16[8,80,128]{2,1,0:T(8,128)(2,1)S(1)} %shard_map.67), channel_id=1, replica_groups=mesh['z'=8,'core'=2,'y'=8,'x'=4] {'y'}, dimensions={0} | all-to-all | bytes 327680 | tf_op jit(solution)/shard_map/all_to_all | solution.py:233
  95.3 1.3 %collective-permute-start.11 = (bf16[64,128]{1,0:T(8,128)(2,1)S(1)}, bf16[64,128]{1,0:T(8,128)(2,1)S(1)}, u32[]{:S(2)}, u32[]{:S(2)}) collective-permute-start(bf16[64,128]{1,0:T(8,128)(2,1)S(1)} %shard_map.68.a0), channel_id=1, source_target_pairs={{3,0},{7,4},{11,8},{15,12},{19,16},{23,20},{27,24},{31,28},{35,32}... | collective-permute-start | bytes 49160 | tf_op jit(solution)/shard_map/ppermute | solution.py:285
  96.6 1.3 %collective-permute-start.10 = (bf16[64,128]{1,0:T(8,128)(2,1)S(1)}, bf16[64,128]{1,0:T(8,128)(2,1)S(1)}, u32[]{:S(2)}, u32[]{:S(2)}) collective-permute-start(bf16[64,128]{1,0:T(8,128)(2,1)S(1)} %shard_map.68.a0), channel_id=1, source_target_pairs={{2,0},{6,4},{10,8},{14,12},{18,16},{22,20},{26,24},{30,28},{34,32}... | collective-permute-start | bytes 49160 | tf_op jit(solution)/shard_map/ppermute | solution.py:285
  99.2 2.9 %collective-permute-done.11.a3 = bf16[64,128]{1,0:T(8,128)(2,1)S(1)} collective-permute-done((bf16[64,128]{1,0:T(8,128)(2,1)S(1)}, bf16[64,128]{1,0:T(8,128)(2,1)S(1)}, u32[]{:S(2)}, u32[]{:S(2)}) %collective-permute-start.11) | collective-permute-done | bytes 16416 | tf_op jit(solution)/shard_map/ppermute | solution.py:285
  102.2 1.6 %collective-permute-done.10.a2 = bf16[64,128]{1,0:T(8,128)(2,1)S(1)} collective-permute-done((bf16[64,128]{1,0:T(8,128)(2,1)S(1)}, bf16[64,128]{1,0:T(8,128)(2,1)S(1)}, u32[]{:S(2)}, u32[]{:S(2)}) %collective-permute-start.10) | collective-permute-done | bytes 16416 | tf_op jit(solution)/shard_map/ppermute | solution.py:285
  103.8 7.3 %shard_map.69 = bf16[128,1792]{1,0:T(8,128)(2,1)} custom-call(s32[2]{0:T(128)S(1)} %copy-done.4, s32[2]{0:T(128)S(1)} %copy-done.5, bf16[128,1792]{1,0:T(8,128)(2,1)S(1)} %copy-done.3, bf16[2,512,256]{2,1,0:T(8,128)(2,1)S(1)} %bitcast.15, bf16[2,512,256]{2,1,0:T(8,128)(2,1)S(1)} %collective-permute-done.7.above, ...), custom_call_target="tpu_custom_call" | custom-call | bytes 25830000 | tf_op jit(solution)/shard_map/pallas_call | solution.py:288
  (30 shorter events, 12.1 us)
Async XLA Ops:
  0.0 28.4 %collective-permute-start = (bf16[128,3584]{1,0:T(8,128)(2,1)}, bf16[128,3584]{1,0:T(8,128)(2,1)S(1)}, u32[]{:S(2)}, u32[]{:S(2)}) collective-permute-start(bf16[128,3584]{1,0:T(8,128)(2,1)} %mine.1), channel_id=1, source_target_pairs={{0,32},{32,0},{1,33},{33,1},{2,34},{34,2},{3,35},{35,3},{4,36},{36... | collective-permute-start | bytes 2752520 | tf_op jit(solution)/shard_map/ppermute | solution.py:249
  3.6 24.8 %all-to-all-start = ((bf16[8,112,256]{2,1,0:T(8,128)(2,1)}), bf16[8,112,256]{2,1,0:T(8,128)(2,1)S(1)}, u32[]{:S(2)}, u32[]{:S(2)}) async-start(bf16[8,112,256]{2,1,0:T(8,128)(2,1)} %broadcast_in_dim.4), calls=%async_computation | async-start | bytes 917504 | tf_op jit(solution)/shard_map/all_to_all | solution.py:233
  16.4 5.6 %collective-permute-start.3 = (bf16[64,128]{1,0:T(8,128)(2,1)S(1)}, bf16[64,128]{1,0:T(8,128)(2,1)S(1)}, u32[]{:S(2)}, u32[]{:S(2)}) collective-permute-start(bf16[64,128]{1,0:T(8,128)(2,1)S(1)} %get-tuple-element.24), channel_id=1, source_target_pairs={{0,3},{4,7},{8,11},{12,15},{16,19},{20,23},{24,27},{28,31},{32,35}... | collective-permute-start | bytes 49160 | tf_op jit(solution)/shard_map/ppermute | solution.py:260
  19.4 2.7 %collective-permute-start.2 = (bf16[64,128]{1,0:T(8,128)(2,1)S(1)}, bf16[64,128]{1,0:T(8,128)(2,1)S(1)}, u32[]{:S(2)}, u32[]{:S(2)}) collective-permute-start(bf16[64,128]{1,0:T(8,128)(2,1)S(1)} %get-tuple-element.25), channel_id=1, source_target_pairs={{0,2},{4,6},{8,10},{12,14},{16,18},{20,22},{24,26},{28,30},{32,34}... | collective-permute-start | bytes 49160 | tf_op jit(solution)/shard_map/ppermute | solution.py:260
  20.7 2.7 %collective-permute-start.1 = (bf16[64,128]{1,0:T(8,128)(2,1)S(1)}, bf16[64,128]{1,0:T(8,128)(2,1)S(1)}, u32[]{:S(2)}, u32[]{:S(2)}) collective-permute-start(bf16[64,128]{1,0:T(8,128)(2,1)S(1)} %get-tuple-element.26), channel_id=1, source_target_pairs={{0,1},{4,5},{8,9},{12,13},{16,17},{20,21},{24,25},{28,29},{32,33},... | collective-permute-start | bytes 49160 | tf_op jit(solution)/shard_map/ppermute | solution.py:260
  28.4 1.6 %copy-start.1 = (bf16[128,3584]{1,0:T(8,128)(2,1)}, bf16[128,3584]{1,0:T(8,128)(2,1)S(1)}, u32[]{:S(2)}) copy-start(bf16[128,3584]{1,0:T(8,128)(2,1)S(1)} %collective-permute-done.theirs) | copy-start | bytes 2752516
  29.9 10.1 %copy-start.4 = (s32[2]{0:T(128)S(1)}, s32[2]{0:T(128)}, u32[]{:S(2)}) copy-start(s32[2]{0:T(128)} %tiles.9) | copy-start | bytes 28
  29.9 10.1 %copy-start.5 = (s32[2]{0:T(128)S(1)}, s32[2]{0:T(128)}, u32[]{:S(2)}) copy-start(s32[2]{0:T(128)} %lengths.9) | copy-start | bytes 28
  29.9 27.4 %copy-start = (bf16[128,3584]{1,0:T(8,128)(2,1)S(1)}, bf16[128,3584]{1,0:T(8,128)(2,1)}, u32[]{:S(2)}) copy-start(bf16[128,3584]{1,0:T(8,128)(2,1)} %mine.1) | copy-start | bytes 2752516
  29.9 27.4 %all-to-all-start.1 = ((bf16[4,8,112,256]{3,2,1,0:T(8,128)(2,1)}), bf16[4,8,112,256]{3,2,1,0:T(8,128)(2,1)S(1)}, u32[]{:S(2)}, u32[]{:S(2)}) async-start(bf16[4,8,112,256]{3,2,1,0:T(8,128)(2,1)} %broadcast_in_dim.5), calls=%async_computation.1 | async-start | bytes 3670016 | tf_op jit(solution)/shard_map/all_to_all | solution.py:233
  34.4 5.6 %collective-permute-start.4 = (bf16[64,128]{1,0:T(8,128)(2,1)S(1)}, bf16[64,128]{1,0:T(8,128)(2,1)S(1)}, u32[]{:S(2)}, u32[]{:S(2)}) collective-permute-start(bf16[64,128]{1,0:T(8,128)(2,1)S(1)} %add_select_fusion), channel_id=1, source_target_pairs={{0,4},{4,8},{8,12},{12,16},{16,20},{20,24},{24,28},{1,5},{5,9},{9,... | collective-permute-start | bytes 49160 | tf_op jit(solution)/shard_map/ppermute | solution.py:237
  40.6 6.0 %collective-permute-start.6 = (bf16[64,128]{1,0:T(8,128)(2,1)S(1)}, bf16[64,128]{1,0:T(8,128)(2,1)S(1)}, u32[]{:S(2)}, u32[]{:S(2)}) collective-permute-start(bf16[64,128]{1,0:T(8,128)(2,1)S(1)} %shard_map.65.near), channel_id=1, source_target_pairs={{0,16},{4,20},{8,24},{12,28},{1,17},{5,21},{9,25},{13,29},{2,18},{... | collective-permute-start | bytes 49160 | tf_op jit(solution)/shard_map/ppermute | solution.py:237
  43.9 4.1 %collective-permute-start.5 = (bf16[64,128]{1,0:T(8,128)(2,1)S(1)}, bf16[64,128]{1,0:T(8,128)(2,1)S(1)}, u32[]{:S(2)}, u32[]{:S(2)}) collective-permute-start(bf16[64,128]{1,0:T(8,128)(2,1)S(1)} %shard_map.65.near), channel_id=1, source_target_pairs={{0,8},{4,12},{8,16},{12,20},{16,24},{20,28},{1,9},{5,13},{9,17},{1... | collective-permute-start | bytes 49160 | tf_op jit(solution)/shard_map/ppermute | solution.py:237
  57.3 1.2 %copy-start.2 = (bf16[128,3584]{1,0:T(8,128)(2,1)S(1)}, bf16[128,3584]{1,0:T(8,128)(2,1)}, u32[]{:S(2)}) copy-start(bf16[128,3584]{1,0:T(8,128)(2,1)} %copy-done.1) | copy-start | bytes 2752516
  59.7 44.1 %copy-start.3 = (bf16[128,1792]{1,0:T(8,128)(2,1)S(1)}, bf16[128,1792]{1,0:T(8,128)(2,1)}, u32[]{:S(2)}) copy-start(bf16[128,1792]{1,0:T(8,128)(2,1)} %queries.1) | copy-start | bytes 1376260
  72.0 31.8 %collective-permute-start.8 = (bf16[2,512,256]{2,1,0:T(8,128)(2,1)S(1)}, bf16[2,512,256]{2,1,0:T(8,128)(2,1)S(1)}, u32[]{:S(2)}, u32[]{:S(2)}) collective-permute-start(bf16[2,512,256]{2,1,0:T(8,128)(2,1)S(1)} %bitcast.12), channel_id=1, source_target_pairs={{4,0},{8,4},{12,8},{16,12},{20,16},{24,20},{28,24},{5,1},{9,5},{13... | collective-permute-start | bytes 1572872 | tf_op jit(solution)/shard_map/ppermute | solution.py:237
  75.7 28.1 %collective-permute-start.7 = (bf16[2,512,256]{2,1,0:T(8,128)(2,1)S(1)}, bf16[2,512,256]{2,1,0:T(8,128)(2,1)S(1)}, u32[]{:S(2)}, u32[]{:S(2)}) collective-permute-start(bf16[2,512,256]{2,1,0:T(8,128)(2,1)S(1)} %bitcast.13), channel_id=1, source_target_pairs={{0,4},{4,8},{8,12},{12,16},{16,20},{20,24},{24,28},{1,5},{5,9},{9,... | collective-permute-start | bytes 1572872 | tf_op jit(solution)/shard_map/ppermute | solution.py:237
  95.3 6.8 %collective-permute-start.11 = (bf16[64,128]{1,0:T(8,128)(2,1)S(1)}, bf16[64,128]{1,0:T(8,128)(2,1)S(1)}, u32[]{:S(2)}, u32[]{:S(2)}) collective-permute-start(bf16[64,128]{1,0:T(8,128)(2,1)S(1)} %shard_map.68.a0), channel_id=1, source_target_pairs={{3,0},{7,4},{11,8},{15,12},{19,16},{23,20},{27,24},{31,28},{35,32}... | collective-permute-start | bytes 49160 | tf_op jit(solution)/shard_map/ppermute | solution.py:285
  96.6 7.1 %collective-permute-start.10 = (bf16[64,128]{1,0:T(8,128)(2,1)S(1)}, bf16[64,128]{1,0:T(8,128)(2,1)S(1)}, u32[]{:S(2)}, u32[]{:S(2)}) collective-permute-start(bf16[64,128]{1,0:T(8,128)(2,1)S(1)} %shard_map.68.a0), channel_id=1, source_target_pairs={{2,0},{6,4},{10,8},{14,12},{18,16},{22,20},{26,24},{30,28},{34,32}... | collective-permute-start | bytes 49160 | tf_op jit(solution)/shard_map/ppermute | solution.py:285
  97.9 5.8 %collective-permute-start.9 = (bf16[64,128]{1,0:T(8,128)(2,1)S(1)}, bf16[64,128]{1,0:T(8,128)(2,1)S(1)}, u32[]{:S(2)}, u32[]{:S(2)}) collective-permute-start(bf16[64,128]{1,0:T(8,128)(2,1)S(1)} %shard_map.68.a0), channel_id=1, source_target_pairs={{1,0},{5,4},{9,8},{13,12},{17,16},{21,20},{25,24},{29,28},{33,32},... | collective-permute-start | bytes 49160 | tf_op jit(solution)/shard_map/ppermute | solution.py:285

commit v3 on v1

v3 whole, which is shorter than its diff:
```python
import functools
import math

import jax
import jax.numpy as jnp
from jax import lax
from jax.experimental import pallas as pl
from jax.experimental.pallas import tpu as pltpu
from jax.sharding import Mesh, PartitionSpec as P

HEAD = 128
TILE = 512
ASK = 16
GROUP = 7
KV = 2
ROWS = 128
XS = 4
YS = 8
BLOCK = GROUP * ASK
PACK = KV * BLOCK + 16
SCALE = math.log2(math.e) / math.sqrt(HEAD)
MASKED = -1e30
NT = (((1,), (1,)), ((), ()))
bf16, f32 = jnp.bfloat16, jnp.float32

def spec(space):
    return pl.BlockSpec(memory_space=space)


def call(body, out, ins, scratch=(), micros=1):
    return pl.pallas_call(
        body,
        out_shape=out,
        in_specs=[spec(pltpu.SMEM)] * 2 + [spec(pltpu.VMEM)] * ins,
        out_specs=jax.tree.map(lambda _: spec(pltpu.VMEM), out),
        scratch_shapes=list(scratch),
        compiler_params=pltpu.CompilerParams(vmem_limit_bytes=24 * 1024 * 1024),
        cost_estimate=pl.CostEstimate(flops=0, bytes_accessed=micros * 3690000, transcendentals=0),
    )


def place(tiles, lengths):
    y, x = lax.axis_index("y"), lax.axis_index("x")
    second = y >= tiles[0]
    start = jnp.where(second, tiles[0], 0)
    stop = jnp.where(second, tiles[0] + tiles[1], tiles[0])
    return y, x, start, stop, jnp.where(second, lengths[1], lengths[0])


def project_body(tiles, lengths, weights, mine, sibling, across, corner, out, whole):
    depth = weights.shape[2]
    for x in range(XS):
        for y in range(YS):
            whole[pl.ds((XS * y + x) * depth, depth), :] = weights[x, y]
    pair, core = lax.axis_index("pair"), lax.axis_index("core")
    for z, c, tokens in (
        (pair, core, mine),
        (pair, 1 - core, sibling),
        (1 - pair, core, across),
        (1 - pair, 1 - core, corner),
    ):
        rows = jnp.dot(tokens[...], whole[...], preferred_element_type=f32).astype(bf16)
        for x in range(XS):
            out[z, c, x] = rows


def to_row(column):
    shape = (column.shape[0], 128)
    same = lax.broadcasted_iota(jnp.int32, shape, 0) == lax.broadcasted_iota(jnp.int32, shape, 1)
    return jnp.sum(jnp.where(same, column, 0.0), axis=0, keepdims=True)


def to_column(row, n):
    shape = (n, 128)
    same = lax.broadcasted_iota(jnp.int32, shape, 0) == lax.broadcasted_iota(jnp.int32, shape, 1)
    return jnp.sum(jnp.where(same, row, 0.0), axis=1, keepdims=True)


def head_columns(n):
    return slice(n * HEAD, (n + 1) * HEAD)


def ask_body(tiles, lengths, own, below, head, head2, head4, out, asked):
    y, x, start, stop, _ = place(tiles, lengths)
    shift = y - start
    for at, source in ((2, head2), (4, head4)):

        @pl.when(shift == at)
        def _():
            asked[...] = source[...]

    @pl.when((shift != 2) & (shift != 4))
    def _():
        asked[...] = head[...]

    more = y + 1 < stop
    tail = jnp.zeros((16, 128), f32)
    line = lax.broadcasted_iota(jnp.int32, (16, 128), 0)
    for h in range(KV):
        queries = jnp.concatenate([asked[:, head_columns(GROUP * h + g)] for g in range(GROUP)], axis=0)
        near = lax.dot_general(queries, own[h, 0], NT, preferred_element_type=f32)
        far = lax.dot_general(queries, below[h, 0], NT, preferred_element_type=f32)
        far = jnp.where(more, far, MASKED)
        peak = jnp.maximum(jnp.max(near, axis=1, keepdims=True), jnp.max(far, axis=1, keepdims=True))
        sums, total = jnp.zeros((BLOCK, HEAD), f32), jnp.zeros((BLOCK, 1), f32)
        for scores, block in ((near, own), (far, below)):
            weights = jnp.exp2((scores - peak) * SCALE)
            total = total + jnp.sum(weights, axis=1, keepdims=True)
            high = weights.astype(bf16)
            low = (weights - high.astype(f32)).astype(bf16)
            sums = sums + jnp.dot(high, block[h, 1], preferred_element_type=f32)
            sums = sums + jnp.dot(low, block[h, 1], preferred_element_type=f32)
        out[h * BLOCK : (h + 1) * BLOCK, :] = (sums / total).astype(bf16)
        rest = to_row(peak * SCALE + jnp.log2(total))
        for i in range(3):
            piece = rest.astype(bf16).astype(f32)
            tail = jnp.where(line == 3 * h + i, piece, tail)
            rest = rest - piece
    out[KV * BLOCK :, :] = tail.astype(bf16)


def attend_body(
    tiles, lengths, queries, own, above, below, questions, pack, back2, back4, out, side, bias, rows
):
    y, x, start, stop, asked = place(tiles, lengths)
    at = pl.multiple_of(x * ROWS, ROWS)
    side[:, :, 0:ROWS, :] = above[:, :, pl.ds(at, ROWS), :]
    side[:, :, 4 * ROWS : 5 * ROWS, :] = below[:, :, pl.ds(at, ROWS), :]
    for h in range(KV):
        for kind in range(2):
            side[h, kind, 5 * ROWS : 5 * ROWS + ASK, :] = questions[start, 2 * h + kind]
            side[h, kind, 5 * ROWS + ASK :, :] = jnp.zeros((ROWS - ASK, HEAD), bf16)
    for i in range(1, 4):

        @pl.when(x + i < XS)
        def _():
            at = pl.multiple_of(jnp.minimum(x + i, XS - 1) * ROWS, ROWS)
            side[:, :, i * ROWS : (i + 1) * ROWS, :] = above[:, :, pl.ds(at, ROWS), :]

        @pl.when(x + i >= XS)
        def _():
            at = pl.multiple_of(jnp.maximum(x + i - XS, 0) * ROWS, ROWS)
            side[:, :, i * ROWS : (i + 1) * ROWS, :] = below[:, :, pl.ds(at, ROWS), :]

    i = lax.broadcasted_iota(jnp.int32, (ROWS, ROWS), 0)
    j = lax.broadcasted_iota(jnp.int32, (ROWS, ROWS), 1)
    up, down = y > start, y + 1 < stop
    first = jnp.where((y == start + 1) & (x == 0), asked, 0)
    limit = jnp.where(up, 0, ROWS)
    bias[:, 0:ROWS] = jnp.where((j >= i) & (j >= first) & (j >= limit), 0.0, MASKED)
    for b in range(1, 4):
        fine = jnp.where(x + b < XS, up.astype(jnp.int32), down.astype(jnp.int32))
        bias[:, b * ROWS : (b + 1) * ROWS] = jnp.where(j < fine * ROWS, 0.0, MASKED)
    limit = jnp.where(down, ROWS, 0)
    bias[:, 4 * ROWS : 5 * ROWS] = jnp.where((j <= i) & (j < limit), 0.0, MASKED)
    bias[:, 5 * ROWS :] = jnp.where(j < jnp.where(up, asked, 0), 0.0, MASKED)

    for n in range(KV * GROUP):
        rows[n * ROWS : (n + 1) * ROWS, :] = queries[:, head_columns(n)]
    for h in range(KV):
        q = rows[h * GROUP * ROWS : (h + 1) * GROUP * ROWS, :]
        near = lax.dot_general(q, own[h, 0], NT, preferred_element_type=f32)
        far = lax.dot_general(q, side[h, 0], NT, preferred_element_type=f32)
        far = (far.reshape(GROUP, ROWS, 6 * ROWS) + bias[...][None]).reshape(GROUP * ROWS, 6 * ROWS)
        peak = jnp.maximum(jnp.max(near, axis=1, keepdims=True), jnp.max(far, axis=1, keepdims=True))
        near = jnp.exp2((near - peak) * SCALE)
        far = jnp.exp2((far - peak) * SCALE)
        total = jnp.sum(near, axis=1, keepdims=True) + jnp.sum(far, axis=1, keepdims=True)
        sums = jnp.dot(near.astype(bf16), own[h, 1], preferred_element_type=f32)
        sums = sums + jnp.dot(far.astype(bf16), side[h, 1], preferred_element_type=f32)
        answer = (sums / total).astype(bf16)
        for g in range(GROUP):
            out[:, head_columns(GROUP * h + g)] = answer[g * ROWS : (g + 1) * ROWS]

    @pl.when((y == start) & (x == 0))
    def _():
        chosen = lax.broadcasted_iota(jnp.int32, (ASK, HEAD), 0) < asked
        sources = ((pack, True), (back2, start + 2 < stop), (back4, start + 4 < stop))
        for h in range(KV):
            logs = []
            for source, valid in sources:
                tail = source[KV * BLOCK :, :].astype(f32)
                log = tail[3 * h : 3 * h + 1] + tail[3 * h + 1 : 3 * h + 2] + tail[3 * h + 2 : 3 * h + 3]
                logs.append(jnp.where(valid, log, MASKED))
            peak = functools.reduce(jnp.maximum, logs)
            shares = [jnp.exp2(log - peak) for log in logs]
            total = sum(shares)
            answer = jnp.zeros((BLOCK, HEAD), f32)
            for share, (source, valid) in zip(shares, sources):
                block = jnp.where(valid, source[h * BLOCK : (h + 1) * BLOCK, :].astype(f32), 0.0)
                answer = answer + to_column(share / total, BLOCK) * block
            for g in range(GROUP):
                mine = head_columns(GROUP * h + g)
                old = out[0:ASK, mine].astype(f32)
                out[0:ASK, mine] = jnp.where(chosen, answer[g * ASK : (g + 1) * ASK], old).astype(bf16)


def exchange(array, axis):
    return lax.all_to_all(array, axis, 0, 0, tiled=False)


def down(array, shift):
    return lax.ppermute(array, "y", [(y, y + shift) for y in range(YS) if 0 <= y + shift < YS])


def copies(array, n):
    return jnp.broadcast_to(array[None], (n,) + array.shape)


def along(array, shift):
    pairs = [(XS * y, XS * (y + shift)) for y in range(YS) if 0 <= y + shift < YS]
    return lax.ppermute(array, ("y", "x"), pairs)


def per_device(tokens, queries, key_matrix, value_matrix, doc_tiles, question_lengths):
    core, pair = lax.axis_index("core"), lax.axis_index("pair")
    swap = [(0, 1), (1, 0)]
    at = (doc_tiles, question_lengths)
    across = lax.ppermute(tokens, "pair", swap)

    shard = jnp.where(core == 0, key_matrix, value_matrix)
    shard = jnp.where(pair == 0, shard[:, :HEAD], shard[:, HEAD:])
    column = exchange(copies(shard, YS), "y")
    column, mine, head = lax.optimization_barrier((column, tokens, queries[:ASK]))
    sibling, corner = lax.ppermute(mine, "core", swap), lax.ppermute(across, "core", swap)
    weights = exchange(copies(column, XS), "x")
    head2, head4 = along(head, 2), along(head, 4)
    weights, head2, head4 = lax.optimization_barrier((weights, head2, head4))

    rows = call(
        project_body,
        jax.ShapeDtypeStruct((2, 2, XS, ROWS, HEAD), bf16),
        5,
        [pltpu.VMEM((weights.shape[0] * weights.shape[1] * weights.shape[2], HEAD), bf16)],
        micros=2,
    )(*at, weights, tokens, sibling, across, corner)
    tile = exchange(rows.reshape(4 * XS, ROWS, HEAD), ("pair", "core", "x")).reshape(KV, 2, TILE, HEAD)

    above, below = down(tile, 1), down(tile, -1)
    questions = exchange(copies(tile[:, :, :ASK].reshape(2 * KV, ASK, HEAD), YS), "y")
    pack = call(
        ask_body,
        jax.ShapeDtypeStruct((PACK, HEAD), bf16),
        5,
        [pltpu.VMEM(head.shape, bf16)],
        micros=2,
    )(*at, tile, below, head, head2, head4)
    back2, back4 = along(pack, -2), along(pack, -4)

    return call(
        attend_body,
        jax.ShapeDtypeStruct(queries.shape, bf16),
        8,
        [
            pltpu.VMEM((KV, 2, 6 * ROWS, HEAD), bf16),
            pltpu.VMEM((ROWS, 6 * ROWS), f32),
            pltpu.VMEM((KV * GROUP * ROWS, HEAD), bf16),
        ],
        micros=5,
    )(*at, queries, tile, above, below, questions, pack, back2, back4)


def solution(mesh):
    devices = mesh.devices
    split = Mesh(devices.reshape(devices.shape[0] // 4, 2, 2, YS, XS), ("z", "pair", "core", "y", "x"))
    rows = P(("z", "pair", "core", "y", "x"), None)
    return jax.shard_map(
        per_device,
        mesh=split,
        in_specs=(
            rows,
            rows,
            P(("y", "x"), None),
            P(("y", "x"), None),
            P(("z", "pair", "core")),
            P(("z", "pair", "core")),
        ),
        out_specs=rows,
        check_vma=False,
    )
```

time: 125 us -> 99.7 us (0.80)
  the two profiles are of different devices: /device:TPU:472 before, /device:TPU:152 now
where the time goes in v3:
time: 99.7 us; the launch traced here: 99 us
  starting transfers between devices  43.3 us (43%)
  waiting for transfers between devices  27.3 us (27%)
  blocking collectives  14.2 us (14%)
  Pallas kernels  9.93 us (10%)
  local copies, waits for them, and re-layouts  3.28 us (3%)
    all_to_all x3, starting transfers between devices, exchange(): return lax.all_to_all(array, axis, 0, 0, tiled=False)  17.9 us
    all_to_all x1, blocking collectives, exchange(): return lax.all_to_all(array, axis, 0, 0, tiled=False)  14.2 us
    ppermute x4, waiting for transfers between devices, along(): return lax.ppermute(array, ('y', 'x'), pairs)  13.6 us
    ppermute x4, starting transfers between devices, along(): return lax.ppermute(array, ('y', 'x'), pairs)  10.2 us
    all_to_all x3, waiting for transfers between devices, exchange(): return lax.all_to_all(array, axis, 0, 0, tiled=False)  7.88 us
    ppermute x2, starting transfers between devices, down(): lax.ppermute(array, 'y', [(y, y + shift) for y in range(YS) if 0 <= y + s...  7.04 us
    pallas_call x1, Pallas kernels, per_device(): call(attend_body, jax.ShapeDtypeStruct(queries.shape, bf16), 8, [pltpu.VM...  5.74 us
    ppermute x1, starting transfers between devices, per_device(): across = lax.ppermute(tokens, 'pair', swap)  4.4 us
  transfers between devices with their start and end apart: 12, of which 7 were waited for; matrix products, arithmetic and copies ran while one was open for 4% of the time, Pallas kernels for 2%

profile of v3, /device:TPU:152, one launch (start us, length us, event | category | flops | bytes accessed | tf_op | source)
XLA Modules:
  0.0 99.0 jit_solution(16556116928307876295)
XLA Ops:
  0.0 4.4 %collective-permute-start.3 = (bf16[128,3584]{1,0:T(8,128)(2,1)}, bf16[128,3584]{1,0:T(8,128)(2,1)S(1)}, u32[]{:S(2)}, u32[]{:S(2)}) collective-permute-start(bf16[128,3584]{1,0:T(8,128)(2,1)} %mine.1), channel_id=1, source_target_pairs={{0,64},{64,0},{1,65},{65,1},{2,66},{66,2},{3,67},{67,3},{4,68},{68... | collective-permute-start | bytes 2752520 | tf_op jit(solution)/shard_map/ppermute | solution.py:219
  4.4 0.8 broadcast_select_fusion
  6.0 7.3 %all-to-all-start = ((bf16[8,112,128]{2,1,0:T(8,128)(2,1)}), bf16[8,112,128]{2,1,0:T(8,128)(2,1)S(1)}, u32[]{:S(2)}, u32[]{:S(2)}) async-start(bf16[8,112,128]{2,1,0:T(8,128)(2,1)} %broadcast_in_dim.8), calls=%async_computation | async-start | bytes 458752 | tf_op jit(solution)/shard_map/all_to_all | solution.py:199
  14.1 6.5 %all-to-all-done = bf16[8,112,128]{2,1,0:T(8,128)(2,1)S(1)} async-done(((bf16[8,112,128]{2,1,0:T(8,128)(2,1)}), bf16[8,112,128]{2,1,0:T(8,128)(2,1)S(1)}, u32[]{:S(2)}, u32[]{:S(2)}) %all-to-all-start) | async-done | bytes 229408 | tf_op jit(solution)/shard_map/all_to_all | solution.py:199
  20.6 1.9 %collective-permute-start.2 = (bf16[128,3584]{1,0:T(8,128)(2,1)S(1)}, bf16[128,3584]{1,0:T(8,128)(2,1)}, u32[]{:S(2)}, u32[]{:S(2)}) collective-permute-start(bf16[128,3584]{1,0:T(8,128)(2,1)S(1)} %copy-done), channel_id=1, source_target_pairs={{0,32},{32,0},{1,33},{33,1},{2,34},{34,2},{3,35},{35,3},{4,36},{36... | collective-permute-start | bytes 2752520 | tf_op jit(solution)/shard_map/ppermute | solution.py:225
  22.6 2.4 %collective-permute-done.3.across = bf16[128,3584]{1,0:T(8,128)(2,1)S(1)} collective-permute-done((bf16[128,3584]{1,0:T(8,128)(2,1)}, bf16[128,3584]{1,0:T(8,128)(2,1)S(1)}, u32[]{:S(2)}, u32[]{:S(2)}) %collective-permute-start.3) | collective-permute-done | bytes 917536 | tf_op jit(solution)/shard_map/ppermute | solution.py:219
  25.0 1.9 %collective-permute-start.4 = (bf16[128,3584]{1,0:T(8,128)(2,1)S(1)}, bf16[128,3584]{1,0:T(8,128)(2,1)}, u32[]{:S(2)}, u32[]{:S(2)}) collective-permute-start(bf16[128,3584]{1,0:T(8,128)(2,1)S(1)} %collective-permute-done.3.across), channel_id=1, source_target_pairs={{0,32},{32,0},{1,33},{33,1},{2,34},{34,2},{3,35},{35,3},{4,36},{36... | collective-permute-start | bytes 2752520 | tf_op jit(solution)/shard_map/ppermute | solution.py:225
  26.9 1.0 %broadcast_in_dim.9 = bf16[4,8,112,128]{3,2,1,0:T(8,128)(2,1)} broadcast(bf16[8,112,128]{2,1,0:T(8,128)(2,1)S(1)} %all-to-all-done), dimensions={1,2,3} | broadcast | bytes 1146880 | tf_op jit(solution)/shard_map/broadcast_in_dim | solution.py:207
  27.9 4.4 %all-to-all-start.1 = ((bf16[4,8,112,128]{3,2,1,0:T(8,128)(2,1)}), bf16[4,8,112,128]{3,2,1,0:T(8,128)(2,1)S(1)}, u32[]{:S(2)}, u32[]{:S(2)}) async-start(bf16[4,8,112,128]{3,2,1,0:T(8,128)(2,1)} %broadcast_in_dim.9), calls=%async_computation.1 | async-start | bytes 1835008 | tf_op jit(solution)/shard_map/all_to_all | solution.py:199
  32.3 5.0 %collective-permute-start.1 = (bf16[16,1792]{1,0:T(8,128)(2,1)S(1)}, bf16[16,1792]{1,0:T(8,128)(2,1)S(1)}, u32[]{:S(2)}, u32[]{:S(2)}) collective-permute-start(bf16[16,1792]{1,0:T(8,128)(2,1)S(1)} %slice.14.head), channel_id=1, source_target_pairs={{0,16},{4,20},{8,24},{12,28},{32,48},{36,52},{40,56},{44,60},{64,8... | collective-permute-start | bytes 172040 | tf_op jit(solution)/shard_map/ppermute | solution.py:212
  37.4 1.9 %collective-permute-start = (bf16[16,1792]{1,0:T(8,128)(2,1)S(1)}, bf16[16,1792]{1,0:T(8,128)(2,1)S(1)}, u32[]{:S(2)}, u32[]{:S(2)}) collective-permute-start(bf16[16,1792]{1,0:T(8,128)(2,1)S(1)} %slice.14.head), channel_id=1, source_target_pairs={{0,8},{4,12},{8,16},{12,20},{16,24},{20,28},{32,40},{36,44},{40,48... | collective-permute-start | bytes 172040 | tf_op jit(solution)/shard_map/ppermute | solution.py:212
  39.3 6.0 %collective-permute-done.head2 = bf16[16,1792]{1,0:T(8,128)(2,1)S(1)} collective-permute-done((bf16[16,1792]{1,0:T(8,128)(2,1)S(1)}, bf16[16,1792]{1,0:T(8,128)(2,1)S(1)}, u32[]{:S(2)}, u32[]{:S(2)}) %collective-permute-start) | collective-permute-done | bytes 57376 | tf_op jit(solution)/shard_map/ppermute | solution.py:212
  45.3 1.4 %all-to-all-done.1.weights = bf16[4,8,112,128]{3,2,1,0:T(8,128)(2,1)S(1)} async-done(((bf16[4,8,112,128]{3,2,1,0:T(8,128)(2,1)}), bf16[4,8,112,128]{3,2,1,0:T(8,128)(2,1)S(1)}, u32[]{:S(2)}, u32[]{:S(2)}) %all-to-all-start.1) | async-done | bytes 917536 | tf_op jit(solution)/shard_map/all_to_all | solution.py:199
  46.7 2.6 %shard_map.64 = bf16[2,2,4,128,128]{4,3,2,1,0:T(8,128)(2,1)S(1)} custom-call(s32[2]{0:T(128)S(1)} %copy-done.2, s32[2]{0:T(128)S(1)} %copy-done.3, bf16[4,8,112,128]{3,2,1,0:T(8,128)(2,1)S(1)} %all-to-all-done.1.weights, bf16[128,3584]{1,0:T(8,128)(2,1)S(1)} %copy-done, bf16[128,3584]{1,0:T(8,128)(2,1)} %collective-permute-done.2.sibling, ...), custom_call_target="tpu_custom_call" | custom-call | bytes 7380000 | tf_op jit(solution)/shard_map/pallas_call | solution.py:230
  49.4 14.2 %all_to_all.20 = bf16[16,128,128]{2,1,0:T(8,128)(2,1)S(1)} all-to-all(bf16[16,128,128]{2,1,0:T(8,128)(2,1)S(1)} %bitcast.8), channel_id=1, replica_groups=mesh['z'=4,'pair'=2,'core'=2,'y'=8,'x'=4] {'pair','core','x'}, dimensions={0} | all-to-all | bytes 1048576 | tf_op jit(solution)/shard_map/all_to_all | solution.py:199
  63.6 2.3 %collective-permute-start.6 = (bf16[2,2,512,128]{3,2,1,0:T(8,128)(2,1)S(1)}, bf16[2,2,512,128]{3,2,1,0:T(8,128)(2,1)S(1)}, u32[]{:S(2)}, u32[]{:S(2)}) collective-permute-start(bf16[2,2,512,128]{3,2,1,0:T(8,128)(2,1)S(1)} %bitcast.3), channel_id=1, source_target_pairs={{4,0},{8,4},{12,8},{16,12},{20,16},{24,20},{28,24},{5,1},{9,5},{13... | collective-permute-start | bytes 1572872 | tf_op jit(solution)/shard_map/ppermute | solution.py:203
  65.9 4.7 %collective-permute-start.5 = (bf16[2,2,512,128]{3,2,1,0:T(8,128)(2,1)S(1)}, bf16[2,2,512,128]{3,2,1,0:T(8,128)(2,1)S(1)}, u32[]{:S(2)}, u32[]{:S(2)}) collective-permute-start(bf16[2,2,512,128]{3,2,1,0:T(8,128)(2,1)S(1)} %bitcast.4), channel_id=1, source_target_pairs={{0,4},{4,8},{8,12},{12,16},{16,20},{20,24},{24,28},{1,5},{5,9},{9,... | collective-permute-start | bytes 1572872 | tf_op jit(solution)/shard_map/ppermute | solution.py:203
  71.3 6.1 %all-to-all-start.3 = ((bf16[8,4,16,128]{3,2,1,0:T(8,128)(2,1)}), bf16[8,4,16,128]{3,2,1,0:T(8,128)(2,1)S(1)}, u32[]{:S(2)}, u32[]{:S(2)}) async-start(bf16[8,4,16,128]{3,2,1,0:T(8,128)(2,1)} %broadcast_in_dim.22), calls=%async_computation.3 | async-start | bytes 262144 | tf_op jit(solution)/shard_map/all_to_all | solution.py:199
  77.4 3.5 %collective-permute-done.6.below = bf16[2,2,512,128]{3,2,1,0:T(8,128)(2,1)S(1)} collective-permute-done((bf16[2,2,512,128]{3,2,1,0:T(8,128)(2,1)S(1)}, bf16[2,2,512,128]{3,2,1,0:T(8,128)(2,1)S(1)}, u32[]{:S(2)}, u32[]{:S(2)}) %collective-permute-start.6) | collective-permute-done | bytes 524320 | tf_op jit(solution)/shard_map/ppermute | solution.py:203
  80.9 1.6 %shard_map.65.pack = bf16[240,128]{1,0:T(8,128)(2,1)S(1)} custom-call(s32[2]{0:T(128)S(1)} %copy-done.2, s32[2]{0:T(128)S(1)} %copy-done.3, bf16[2,2,512,128]{3,2,1,0:T(8,128)(2,1)S(1)} %bitcast.6, bf16[2,2,512,128]{3,2,1,0:T(8,128)(2,1)S(1)} %collective-permute-done.6.below, bf16[16,1792]{1,0:T(8,128)(2,1)S(1)} %slice.14.head, ...), custom_call_target="tpu_custom_call" | custom-call | bytes 7380000 | tf_op jit(solution)/shard_map/pallas_call | solution.py:241
  82.4 1.3 %collective-permute-start.8 = (bf16[240,128]{1,0:T(8,128)(2,1)S(1)}, bf16[240,128]{1,0:T(8,128)(2,1)S(1)}, u32[]{:S(2)}, u32[]{:S(2)}) collective-permute-start(bf16[240,128]{1,0:T(8,128)(2,1)S(1)} %shard_map.65.pack), channel_id=1, source_target_pairs={{16,0},{20,4},{24,8},{28,12},{48,32},{52,36},{56,40},{60,44},{80,6... | collective-permute-start | bytes 184328 | tf_op jit(solution)/shard_map/ppermute | solution.py:212
  83.7 1.9 %collective-permute-start.7 = (bf16[240,128]{1,0:T(8,128)(2,1)S(1)}, bf16[240,128]{1,0:T(8,128)(2,1)S(1)}, u32[]{:S(2)}, u32[]{:S(2)}) collective-permute-start(bf16[240,128]{1,0:T(8,128)(2,1)S(1)} %shard_map.65.pack), channel_id=1, source_target_pairs={{8,0},{12,4},{16,8},{20,12},{24,16},{28,20},{40,32},{44,36},{48,40... | collective-permute-start | bytes 184328 | tf_op jit(solution)/shard_map/ppermute | solution.py:212
  85.7 7.0 %collective-permute-done.8.back4 = bf16[240,128]{1,0:T(8,128)(2,1)S(1)} collective-permute-done((bf16[240,128]{1,0:T(8,128)(2,1)S(1)}, bf16[240,128]{1,0:T(8,128)(2,1)S(1)}, u32[]{:S(2)}, u32[]{:S(2)}) %collective-permute-start.8) | collective-permute-done | bytes 61472 | tf_op jit(solution)/shard_map/ppermute | solution.py:212
  93.3 5.7 %shard_map.66 = bf16[128,1792]{1,0:T(8,128)(2,1)} custom-call(s32[2]{0:T(128)S(1)} %copy-done.2, s32[2]{0:T(128)S(1)} %copy-done.3, bf16[128,1792]{1,0:T(8,128)(2,1)S(1)} %copy-done.1, bf16[2,2,512,128]{3,2,1,0:T(8,128)(2,1)S(1)} %bitcast.7, bf16[2,2,512,128]{3,2,1,0:T(8,128)(2,1)S(1)} %collective-permute-done.5.above, ...), custom_call_target="tpu_custom_call" | custom-call | bytes 18450000 | tf_op jit(solution)/shard_map/pallas_call | solution.py:250
  (19 shorter events, 2.9 us)
Async XLA Ops:
  0.0 20.6 %copy-start = (bf16[128,3584]{1,0:T(8,128)(2,1)S(1)}, bf16[128,3584]{1,0:T(8,128)(2,1)}, u32[]{:S(2)}) copy-start(bf16[128,3584]{1,0:T(8,128)(2,1)} %mine.1) | copy-start | bytes 2752516
  0.0 25.0 %collective-permute-start.3 = (bf16[128,3584]{1,0:T(8,128)(2,1)}, bf16[128,3584]{1,0:T(8,128)(2,1)S(1)}, u32[]{:S(2)}, u32[]{:S(2)}) collective-permute-start(bf16[128,3584]{1,0:T(8,128)(2,1)} %mine.1), channel_id=1, source_target_pairs={{0,64},{64,0},{1,65},{65,1},{2,66},{66,2},{3,67},{67,3},{4,68},{68... | collective-permute-start | bytes 2752520 | tf_op jit(solution)/shard_map/ppermute | solution.py:219
  6.0 14.6 %all-to-all-start = ((bf16[8,112,128]{2,1,0:T(8,128)(2,1)}), bf16[8,112,128]{2,1,0:T(8,128)(2,1)S(1)}, u32[]{:S(2)}, u32[]{:S(2)}) async-start(bf16[8,112,128]{2,1,0:T(8,128)(2,1)} %broadcast_in_dim.8), calls=%async_computation | async-start | bytes 458752 | tf_op jit(solution)/shard_map/all_to_all | solution.py:199
  20.6 26.1 %collective-permute-start.2 = (bf16[128,3584]{1,0:T(8,128)(2,1)S(1)}, bf16[128,3584]{1,0:T(8,128)(2,1)}, u32[]{:S(2)}, u32[]{:S(2)}) collective-permute-start(bf16[128,3584]{1,0:T(8,128)(2,1)S(1)} %copy-done), channel_id=1, source_target_pairs={{0,32},{32,0},{1,33},{33,1},{2,34},{34,2},{3,35},{35,3},{4,36},{36... | collective-permute-start | bytes 2752520 | tf_op jit(solution)/shard_map/ppermute | solution.py:225
  25.0 21.7 %collective-permute-start.4 = (bf16[128,3584]{1,0:T(8,128)(2,1)S(1)}, bf16[128,3584]{1,0:T(8,128)(2,1)}, u32[]{:S(2)}, u32[]{:S(2)}) collective-permute-start(bf16[128,3584]{1,0:T(8,128)(2,1)S(1)} %collective-permute-done.3.across), channel_id=1, source_target_pairs={{0,32},{32,0},{1,33},{33,1},{2,34},{34,2},{3,35},{35,3},{4,36},{36... | collective-permute-start | bytes 2752520 | tf_op jit(solution)/shard_map/ppermute | solution.py:225
  27.9 18.8 %copy-start.2 = (s32[2]{0:T(128)S(1)}, s32[2]{0:T(128)}, u32[]{:S(2)}) copy-start(s32[2]{0:T(128)} %tiles.5) | copy-start | bytes 28
  27.9 18.8 %copy-start.3 = (s32[2]{0:T(128)S(1)}, s32[2]{0:T(128)}, u32[]{:S(2)}) copy-start(s32[2]{0:T(128)} %lengths.5) | copy-start | bytes 28
  27.9 18.8 %all-to-all-start.1 = ((bf16[4,8,112,128]{3,2,1,0:T(8,128)(2,1)}), bf16[4,8,112,128]{3,2,1,0:T(8,128)(2,1)S(1)}, u32[]{:S(2)}, u32[]{:S(2)}) async-start(bf16[4,8,112,128]{3,2,1,0:T(8,128)(2,1)} %broadcast_in_dim.9), calls=%async_computation.1 | async-start | bytes 1835008 | tf_op jit(solution)/shard_map/all_to_all | solution.py:199
  32.3 7.0 %collective-permute-start.1 = (bf16[16,1792]{1,0:T(8,128)(2,1)S(1)}, bf16[16,1792]{1,0:T(8,128)(2,1)S(1)}, u32[]{:S(2)}, u32[]{:S(2)}) collective-permute-start(bf16[16,1792]{1,0:T(8,128)(2,1)S(1)} %slice.14.head), channel_id=1, source_target_pairs={{0,16},{4,20},{8,24},{12,28},{32,48},{36,52},{40,56},{44,60},{64,8... | collective-permute-start | bytes 172040 | tf_op jit(solution)/shard_map/ppermute | solution.py:212
  37.4 8.0 %collective-permute-start = (bf16[16,1792]{1,0:T(8,128)(2,1)S(1)}, bf16[16,1792]{1,0:T(8,128)(2,1)S(1)}, u32[]{:S(2)}, u32[]{:S(2)}) collective-permute-start(bf16[16,1792]{1,0:T(8,128)(2,1)S(1)} %slice.14.head), channel_id=1, source_target_pairs={{0,8},{4,12},{8,16},{12,20},{16,24},{20,28},{32,40},{36,44},{40,48... | collective-permute-start | bytes 172040 | tf_op jit(solution)/shard_map/ppermute | solution.py:212
  63.6 17.3 %collective-permute-start.6 = (bf16[2,2,512,128]{3,2,1,0:T(8,128)(2,1)S(1)}, bf16[2,2,512,128]{3,2,1,0:T(8,128)(2,1)S(1)}, u32[]{:S(2)}, u32[]{:S(2)}) collective-permute-start(bf16[2,2,512,128]{3,2,1,0:T(8,128)(2,1)S(1)} %bitcast.3), channel_id=1, source_target_pairs={{4,0},{8,4},{12,8},{16,12},{20,16},{24,20},{28,24},{5,1},{9,5},{13... | collective-permute-start | bytes 1572872 | tf_op jit(solution)/shard_map/ppermute | solution.py:203
  65.9 19.8 %collective-permute-start.5 = (bf16[2,2,512,128]{3,2,1,0:T(8,128)(2,1)S(1)}, bf16[2,2,512,128]{3,2,1,0:T(8,128)(2,1)S(1)}, u32[]{:S(2)}, u32[]{:S(2)}) collective-permute-start(bf16[2,2,512,128]{3,2,1,0:T(8,128)(2,1)S(1)} %bitcast.4), channel_id=1, source_target_pairs={{0,4},{4,8},{8,12},{12,16},{16,20},{20,24},{24,28},{1,5},{5,9},{9,... | collective-permute-start | bytes 1572872 | tf_op jit(solution)/shard_map/ppermute | solution.py:203
  71.3 14.4 %all-to-all-start.3 = ((bf16[8,4,16,128]{3,2,1,0:T(8,128)(2,1)}), bf16[8,4,16,128]{3,2,1,0:T(8,128)(2,1)S(1)}, u32[]{:S(2)}, u32[]{:S(2)}) async-start(bf16[8,4,16,128]{3,2,1,0:T(8,128)(2,1)} %broadcast_in_dim.22), calls=%async_computation.3 | async-start | bytes 262144 | tf_op jit(solution)/shard_map/all_to_all | solution.py:199
  77.4 15.9 %copy-start.1 = (bf16[128,1792]{1,0:T(8,128)(2,1)S(1)}, bf16[128,1792]{1,0:T(8,128)(2,1)}, u32[]{:S(2)}) copy-start(bf16[128,1792]{1,0:T(8,128)(2,1)} %queries.1) | copy-start | bytes 1376260
  82.4 10.2 %collective-permute-start.8 = (bf16[240,128]{1,0:T(8,128)(2,1)S(1)}, bf16[240,128]{1,0:T(8,128)(2,1)S(1)}, u32[]{:S(2)}, u32[]{:S(2)}) collective-permute-start(bf16[240,128]{1,0:T(8,128)(2,1)S(1)} %shard_map.65.pack), channel_id=1, source_target_pairs={{16,0},{20,4},{24,8},{28,12},{48,32},{52,36},{56,40},{60,44},{80,6... | collective-permute-start | bytes 184328 | tf_op jit(solution)/shard_map/ppermute | solution.py:212
  83.7 9.5 %collective-permute-start.7 = (bf16[240,128]{1,0:T(8,128)(2,1)S(1)}, bf16[240,128]{1,0:T(8,128)(2,1)S(1)}, u32[]{:S(2)}, u32[]{:S(2)}) collective-permute-start(bf16[240,128]{1,0:T(8,128)(2,1)S(1)} %shard_map.65.pack), channel_id=1, source_target_pairs={{8,0},{12,4},{16,8},{20,12},{24,16},{28,20},{40,32},{44,36},{48,40... | collective-permute-start | bytes 184328 | tf_op jit(solution)/shard_map/ppermute | solution.py:212

commit v4 on v3

--- a/solution.py
+++ b/solution.py
@@ -27,12 +27,12 @@
     return pl.BlockSpec(memory_space=space)
 
 
-def call(body, out, ins, scratch=(), micros=1):
+def call(body, out, ins, scratch=(), micros=1, scalars=2):
     return pl.pallas_call(
         body,
         out_shape=out,
-        in_specs=[spec(pltpu.SMEM)] * 2 + [spec(pltpu.VMEM)] * ins,
-        out_specs=jax.tree.map(lambda _: spec(pltpu.VMEM), out),
+        in_specs=[spec(pltpu.SMEM)] * scalars + [spec(pltpu.VMEM)] * ins,
+        out_specs=spec(pltpu.VMEM),
         scratch_shapes=list(scratch),
         compiler_params=pltpu.CompilerParams(vmem_limit_bytes=24 * 1024 * 1024),
         cost_estimate=pl.CostEstimate(flops=0, bytes_accessed=micros * 3690000, transcendentals=0),
@@ -47,11 +47,7 @@
     return y, x, start, stop, jnp.where(second, lengths[1], lengths[0])
 
 
-def project_body(tiles, lengths, weights, mine, sibling, across, corner, out, whole):
-    depth = weights.shape[2]
-    for x in range(XS):
-        for y in range(YS):
-            whole[pl.ds((XS * y + x) * depth, depth), :] = weights[x, y]
+def project_body(weights, mine, sibling, across, corner, out):
     pair, core = lax.axis_index("pair"), lax.axis_index("core")
     for z, c, tokens in (
         (pair, core, mine),
@@ -59,7 +55,7 @@
         (1 - pair, core, across),
         (1 - pair, 1 - core, corner),
     ):
-        rows = jnp.dot(tokens[...], whole[...], preferred_element_type=f32).astype(bf16)
+        rows = jnp.dot(tokens[...], weights[...], preferred_element_type=f32).astype(bf16)
         for x in range(XS):
             out[z, c, x] = rows
 
@@ -120,7 +116,7 @@
 
 
 def attend_body(
-    tiles, lengths, queries, own, above, below, questions, pack, back2, back4, out, side, bias, rows
+    tiles, lengths, queries, own, above, below, questions, out, side, bias, rows
 ):
     y, x, start, stop, asked = place(tiles, lengths)
     at = pl.multiple_of(x * ROWS, ROWS)
@@ -171,6 +167,11 @@
         answer = (sums / total).astype(bf16)
         for g in range(GROUP):
             out[:, head_columns(GROUP * h + g)] = answer[g * ROWS : (g + 1) * ROWS]
+
+
+def patch_body(tiles, lengths, banded, pack, back2, back4, out):
+    y, x, start, stop, asked = place(tiles, lengths)
+    out[...] = banded[...]
 
     @pl.when((y == start) & (x == 0))
     def _():
@@ -220,20 +221,15 @@
 
     shard = jnp.where(core == 0, key_matrix, value_matrix)
     shard = jnp.where(pair == 0, shard[:, :HEAD], shard[:, HEAD:])
-    column = exchange(copies(shard, YS), "y")
-    column, mine, head = lax.optimization_barrier((column, tokens, queries[:ASK]))
-    sibling, corner = lax.ppermute(mine, "core", swap), lax.ppermute(across, "core", swap)
-    weights = exchange(copies(column, XS), "x")
+    weights = exchange(copies(shard, YS * XS), ("y", "x")).reshape(tokens.shape[1], HEAD)
+    head = queries[:ASK]
+    sibling, corner = lax.ppermute(tokens, "core", swap), lax.ppermute(across, "core", swap)
     head2, head4 = along(head, 2), along(head, 4)
     weights, head2, head4 = lax.optimization_barrier((weights, head2, head4))
 
     rows = call(
-        project_body,
-        jax.ShapeDtypeStruct((2, 2, XS, ROWS, HEAD), bf16),
-        5,
-        [pltpu.VMEM((weights.shape[0] * weights.shape[1] * weights.shape[2], HEAD), bf16)],
-        micros=2,
-    )(*at, weights, tokens, sibling, across, corner)
+        project_body, jax.ShapeDtypeStruct((2, 2, XS, ROWS, HEAD), bf16), 5, micros=2, scalars=0
+    )(weights, tokens, sibling, across, corner)
     tile = exchange(rows.reshape(4 * XS, ROWS, HEAD), ("pair", "core", "x")).reshape(KV, 2, TILE, HEAD)
 
     above, below = down(tile, 1), down(tile, -1)
@@ -247,17 +243,28 @@
     )(*at, tile, below, head, head2, head4)
     back2, back4 = along(pack, -2), along(pack, -4)
 
-    return call(
+    banded = call(
         attend_body,
         jax.ShapeDtypeStruct(queries.shape, bf16),
-        8,
+        5,
         [
             pltpu.VMEM((KV, 2, 6 * ROWS, HEAD), bf16),
             pltpu.VMEM((ROWS, 6 * ROWS), f32),
             pltpu.VMEM((KV * GROUP * ROWS, HEAD), bf16),
         ],
         micros=5,
-    )(*at, queries, tile, above, below, questions, pack, back2, back4)
+    )(*at, queries, tile, above, below, questions)
+    top = pl.BlockSpec((ASK, queries.shape[1]), lambda i: (0, 0))
+    return pl.pallas_call(
+        patch_body,
+        out_shape=jax.ShapeDtypeStruct(queries.shape, bf16),
+        grid=(1,),
+        in_specs=[spec(pltpu.SMEM)] * 2 + [top] + [spec(pltpu.VMEM)] * 3,
+        out_specs=top,
+        input_output_aliases={2: 0},
+        compiler_params=pltpu.CompilerParams(vmem_limit_bytes=4 * 1024 * 1024),
+        cost_estimate=pl.CostEstimate(flops=0, bytes_accessed=3690000, transcendentals=0),
+    )(*at, banded, pack, back2, back4)
 
 
 def solution(mesh):

time: 99.7 us -> 91.7 us (0.920)
  the two profiles are of different devices: /device:TPU:152 before, /device:TPU:176 now
where the time goes in v4:
time: 91.7 us; the launch traced here: 91.1 us
  starting transfers between devices  41.3 us (45%)
  waiting for transfers between devices  22.6 us (25%)
  blocking collectives  13.3 us (15%)
  Pallas kernels  11.2 us (12%)
  local copies, waits for them, and re-layouts  1.74 us (2%)
    all_to_all x2, starting transfers between devices, exchange(): return lax.all_to_all(array, axis, 0, 0, tiled=False)  16.8 us
    all_to_all x1, blocking collectives, exchange(): return lax.all_to_all(array, axis, 0, 0, tiled=False)  13.3 us
    ppermute x4, waiting for transfers between devices, along(): return lax.ppermute(array, ('y', 'x'), pairs)  11.9 us
    ppermute x4, starting transfers between devices, along(): return lax.ppermute(array, ('y', 'x'), pairs)  10.6 us
    ppermute x1, waiting for transfers between devices, per_device(): across = lax.ppermute(tokens, 'pair', swap)  6.91 us
    ppermute x2, starting transfers between devices, down(): lax.ppermute(array, 'y', [(y, y + shift) for y in range(YS) if 0 <= y + s...  5.86 us
    pallas_call x1, Pallas kernels, per_device(): call(attend_body, jax.ShapeDtypeStruct(queries.shape, bf16), 5, [pltpu.VM...  5.55 us
    ppermute x1, starting transfers between devices, per_device(): across = lax.ppermute(tokens, 'pair', swap)  4.27 us
  transfers between devices with their start and end apart: 11, of which 3 were waited for; matrix products, arithmetic and copies ran while one was open for 3% of the time, Pallas kernels for 8%

profile of v4, /device:TPU:176, one launch (start us, length us, event | category | flops | bytes accessed | tf_op | source)
XLA Modules:
  0.0 91.1 jit_solution(7300616789892776921)
XLA Ops:
  0.0 4.3 %collective-permute-start.3 = (bf16[128,3584]{1,0:T(8,128)(2,1)}, bf16[128,3584]{1,0:T(8,128)(2,1)S(1)}, u32[]{:S(2)}, u32[]{:S(2)}) collective-permute-start(bf16[128,3584]{1,0:T(8,128)(2,1)} %mine.1), channel_id=1, source_target_pairs={{0,64},{64,0},{1,65},{65,1},{2,66},{66,2},{3,67},{67,3},{4,68},{68... | collective-permute-start | bytes 2752520 | tf_op jit(solution)/shard_map/ppermute | solution.py:220
  4.3 0.8 broadcast_select_fusion
  5.1 1.0 %broadcast_in_dim.6 = bf16[32,112,128]{2,1,0:T(8,128)(2,1)} broadcast(bf16[112,128]{1,0:T(8,128)(2,1)S(1)} %slice_select_fusion), dimensions={1,2} | broadcast | bytes 946176 | tf_op jit(solution)/shard_map/broadcast_in_dim | solution.py:208
  6.2 9.8 %all-to-all-start = ((bf16[32,112,128]{2,1,0:T(8,128)(2,1)}), bf16[32,112,128]{2,1,0:T(8,128)(2,1)S(1)}, u32[]{:S(2)}, u32[]{:S(2)}) async-start(bf16[32,112,128]{2,1,0:T(8,128)(2,1)} %broadcast_in_dim.6), calls=%async_computation | async-start | bytes 1835008 | tf_op jit(solution)/shard_map/all_to_all | solution.py:200
  16.0 1.9 %collective-permute-start.2 = (bf16[128,3584]{1,0:T(8,128)(2,1)S(1)}, bf16[128,3584]{1,0:T(8,128)(2,1)}, u32[]{:S(2)}, u32[]{:S(2)}) collective-permute-start(bf16[128,3584]{1,0:T(8,128)(2,1)S(1)} %copy-done), channel_id=1, source_target_pairs={{0,32},{32,0},{1,33},{33,1},{2,34},{34,2},{3,35},{35,3},{4,36},{36... | collective-permute-start | bytes 2752520 | tf_op jit(solution)/shard_map/ppermute | solution.py:226
  17.9 6.9 %collective-permute-done.3.across = bf16[128,3584]{1,0:T(8,128)(2,1)S(1)} collective-permute-done((bf16[128,3584]{1,0:T(8,128)(2,1)}, bf16[128,3584]{1,0:T(8,128)(2,1)S(1)}, u32[]{:S(2)}, u32[]{:S(2)}) %collective-permute-start.3) | collective-permute-done | bytes 917536 | tf_op jit(solution)/shard_map/ppermute | solution.py:220
  24.8 1.9 %collective-permute-start.4 = (bf16[128,3584]{1,0:T(8,128)(2,1)S(1)}, bf16[128,3584]{1,0:T(8,128)(2,1)}, u32[]{:S(2)}, u32[]{:S(2)}) collective-permute-start(bf16[128,3584]{1,0:T(8,128)(2,1)S(1)} %collective-permute-done.3.across), channel_id=1, source_target_pairs={{0,32},{32,0},{1,33},{33,1},{2,34},{34,2},{3,35},{35,3},{4,36},{36... | collective-permute-start | bytes 2752520 | tf_op jit(solution)/shard_map/ppermute | solution.py:226
  26.8 1.3 %collective-permute-start.1 = (bf16[16,1792]{1,0:T(8,128)(2,1)S(1)}, bf16[16,1792]{1,0:T(8,128)(2,1)S(1)}, u32[]{:S(2)}, u32[]{:S(2)}) collective-permute-start(bf16[16,1792]{1,0:T(8,128)(2,1)S(1)} %slice.14.head), channel_id=1, source_target_pairs={{0,16},{4,20},{8,24},{12,28},{32,48},{36,52},{40,56},{44,60},{64,8... | collective-permute-start | bytes 172040 | tf_op jit(solution)/shard_map/ppermute | solution.py:213
  28.1 1.3 %collective-permute-start = (bf16[16,1792]{1,0:T(8,128)(2,1)S(1)}, bf16[16,1792]{1,0:T(8,128)(2,1)S(1)}, u32[]{:S(2)}, u32[]{:S(2)}) collective-permute-start(bf16[16,1792]{1,0:T(8,128)(2,1)S(1)} %slice.14.head), channel_id=1, source_target_pairs={{0,8},{4,12},{8,16},{12,20},{16,24},{20,28},{32,40},{36,44},{40,48... | collective-permute-start | bytes 172040 | tf_op jit(solution)/shard_map/ppermute | solution.py:213
  29.4 11.9 %collective-permute-done.1.head4 = bf16[16,1792]{1,0:T(8,128)(2,1)S(1)} collective-permute-done((bf16[16,1792]{1,0:T(8,128)(2,1)S(1)}, bf16[16,1792]{1,0:T(8,128)(2,1)S(1)}, u32[]{:S(2)}, u32[]{:S(2)}) %collective-permute-start.1) | collective-permute-done | bytes 57376 | tf_op jit(solution)/shard_map/ppermute | solution.py:213
  41.3 0.0 collective-permute-done.head2
  41.3 0.0 all-to-all-done
  41.3 2.6 %shard_map.64 = bf16[2,2,4,128,128]{4,3,2,1,0:T(8,128)(2,1)S(1)} custom-call(bf16[3584,128]{1,0:T(8,128)(2,1)S(1)} %bitcast.9, bf16[128,3584]{1,0:T(8,128)(2,1)S(1)} %copy-done, bf16[128,3584]{1,0:T(8,128)(2,1)} %collective-permute-done.2.sibling, bf16[128,3584]{1,0:T(8,128)(2,1)S(1)} %collective-permute-done.3.across, ...), custom_call_target="tpu_custom_call" | custom-call | bytes 7380000 | tf_op jit(solution)/shard_map/pallas_call | solution.py:230
  43.9 13.3 %all_to_all.15 = bf16[16,128,128]{2,1,0:T(8,128)(2,1)S(1)} all-to-all(bf16[16,128,128]{2,1,0:T(8,128)(2,1)S(1)} %bitcast.10), channel_id=1, replica_groups=mesh['z'=4,'pair'=2,'core'=2,'y'=8,'x'=4] {'pair','core','x'}, dimensions={0} | all-to-all | bytes 1048576 | tf_op jit(solution)/shard_map/all_to_all | solution.py:200
  57.2 3.4 %collective-permute-start.6 = (bf16[2,2,512,128]{3,2,1,0:T(8,128)(2,1)S(1)}, bf16[2,2,512,128]{3,2,1,0:T(8,128)(2,1)S(1)}, u32[]{:S(2)}, u32[]{:S(2)}) collective-permute-start(bf16[2,2,512,128]{3,2,1,0:T(8,128)(2,1)S(1)} %bitcast.4), channel_id=1, source_target_pairs={{4,0},{8,4},{12,8},{16,12},{20,16},{24,20},{28,24},{5,1},{9,5},{13... | collective-permute-start | bytes 1572872 | tf_op jit(solution)/shard_map/ppermute | solution.py:204
  60.6 2.4 %collective-permute-start.5 = (bf16[2,2,512,128]{3,2,1,0:T(8,128)(2,1)S(1)}, bf16[2,2,512,128]{3,2,1,0:T(8,128)(2,1)S(1)}, u32[]{:S(2)}, u32[]{:S(2)}) collective-permute-start(bf16[2,2,512,128]{3,2,1,0:T(8,128)(2,1)S(1)} %bitcast.5), channel_id=1, source_target_pairs={{0,4},{4,8},{8,12},{12,16},{16,20},{20,24},{24,28},{1,5},{5,9},{9,... | collective-permute-start | bytes 1572872 | tf_op jit(solution)/shard_map/ppermute | solution.py:204
  63.0 0.7 broadcast_in_dim.15
  63.7 7.0 %all-to-all-start.2 = ((bf16[8,4,16,128]{3,2,1,0:T(8,128)(2,1)}), bf16[8,4,16,128]{3,2,1,0:T(8,128)(2,1)S(1)}, u32[]{:S(2)}, u32[]{:S(2)}) async-start(bf16[8,4,16,128]{3,2,1,0:T(8,128)(2,1)} %broadcast_in_dim.15), calls=%async_computation.2 | async-start | bytes 262144 | tf_op jit(solution)/shard_map/all_to_all | solution.py:200
  70.7 3.7 %collective-permute-done.6.below = bf16[2,2,512,128]{3,2,1,0:T(8,128)(2,1)S(1)} collective-permute-done((bf16[2,2,512,128]{3,2,1,0:T(8,128)(2,1)S(1)}, bf16[2,2,512,128]{3,2,1,0:T(8,128)(2,1)S(1)}, u32[]{:S(2)}, u32[]{:S(2)}) %collective-permute-start.6) | collective-permute-done | bytes 524320 | tf_op jit(solution)/shard_map/ppermute | solution.py:204
  74.5 1.6 %shard_map.66.pack = bf16[240,128]{1,0:T(8,128)(2,1)S(1)} custom-call(s32[2]{0:T(128)S(1)} %copy-done.2, s32[2]{0:T(128)S(1)} %copy-done.3, bf16[2,2,512,128]{3,2,1,0:T(8,128)(2,1)S(1)} %bitcast.7, bf16[2,2,512,128]{3,2,1,0:T(8,128)(2,1)S(1)} %collective-permute-done.6.below, bf16[16,1792]{1,0:T(8,128)(2,1)S(1)} %slice.14.head, ...), custom_call_target="tpu_custom_call" | custom-call | bytes 7380000 | tf_op jit(solution)/shard_map/pallas_call | solution.py:237
  76.0 2.7 %collective-permute-start.8 = (bf16[240,128]{1,0:T(8,128)(2,1)S(1)}, bf16[240,128]{1,0:T(8,128)(2,1)S(1)}, u32[]{:S(2)}, u32[]{:S(2)}) collective-permute-start(bf16[240,128]{1,0:T(8,128)(2,1)S(1)} %shard_map.66.pack), channel_id=1, source_target_pairs={{16,0},{20,4},{24,8},{28,12},{48,32},{52,36},{56,40},{60,44},{80,6... | collective-permute-start | bytes 184328 | tf_op jit(solution)/shard_map/ppermute | solution.py:213
  78.8 5.2 %collective-permute-start.7 = (bf16[240,128]{1,0:T(8,128)(2,1)S(1)}, bf16[240,128]{1,0:T(8,128)(2,1)S(1)}, u32[]{:S(2)}, u32[]{:S(2)}) collective-permute-start(bf16[240,128]{1,0:T(8,128)(2,1)S(1)} %shard_map.66.pack), channel_id=1, source_target_pairs={{8,0},{12,4},{16,8},{20,12},{24,16},{28,20},{40,32},{44,36},{48,40... | collective-permute-start | bytes 184328 | tf_op jit(solution)/shard_map/ppermute | solution.py:213
  84.1 5.6 %shard_map.65.banded = bf16[128,1792]{1,0:T(8,128)(2,1)} custom-call(s32[2]{0:T(128)S(1)} %copy-done.2, s32[2]{0:T(128)S(1)} %copy-done.3, bf16[128,1792]{1,0:T(8,128)(2,1)S(1)} %copy-done.1, bf16[2,2,512,128]{3,2,1,0:T(8,128)(2,1)S(1)} %bitcast.8, bf16[2,2,512,128]{3,2,1,0:T(8,128)(2,1)S(1)} %collective-permute-done.5.above, ...), custom_call_target="tpu_custom_call" | custom-call | bytes 18450000 | tf_op jit(solution)/shard_map/pallas_call | solution.py:246
  89.6 1.5 %shard_map.67 = bf16[128,1792]{1,0:T(8,128)(2,1)} custom-call(s32[2]{0:T(128)S(1)} %copy-done.2, s32[2]{0:T(128)S(1)} %copy-done.3, bf16[128,1792]{1,0:T(8,128)(2,1)} %shard_map.65.banded, bf16[240,128]{1,0:T(8,128)(2,1)S(1)} %shard_map.66.pack, bf16[240,128]{1,0:T(8,128)(2,1)S(1)} %collective-permute-done.7.back2, ...), custom_call_target="tpu_custom_call", output_to_operand_aliasing={{}: (2, {})} | custom-call | bytes 3690000 | tf_op jit(solution)/shard_map/pallas_call | solution.py:258
  (17 shorter events, 0.1 us)
Async XLA Ops:
  0.0 24.8 %collective-permute-start.3 = (bf16[128,3584]{1,0:T(8,128)(2,1)}, bf16[128,3584]{1,0:T(8,128)(2,1)S(1)}, u32[]{:S(2)}, u32[]{:S(2)}) collective-permute-start(bf16[128,3584]{1,0:T(8,128)(2,1)} %mine.1), channel_id=1, source_target_pairs={{0,64},{64,0},{1,65},{65,1},{2,66},{66,2},{3,67},{67,3},{4,68},{68... | collective-permute-start | bytes 2752520 | tf_op jit(solution)/shard_map/ppermute | solution.py:220
  6.2 9.8 %copy-start = (bf16[128,3584]{1,0:T(8,128)(2,1)S(1)}, bf16[128,3584]{1,0:T(8,128)(2,1)}, u32[]{:S(2)}) copy-start(bf16[128,3584]{1,0:T(8,128)(2,1)} %mine.1) | copy-start | bytes 2752516
  6.2 20.6 %copy-start.1 = (bf16[128,1792]{1,0:T(8,128)(2,1)S(1)}, bf16[128,1792]{1,0:T(8,128)(2,1)}, u32[]{:S(2)}) copy-start(bf16[128,1792]{1,0:T(8,128)(2,1)} %queries.1) | copy-start | bytes 1376260
  6.2 35.1 %all-to-all-start = ((bf16[32,112,128]{2,1,0:T(8,128)(2,1)}), bf16[32,112,128]{2,1,0:T(8,128)(2,1)S(1)}, u32[]{:S(2)}, u32[]{:S(2)}) async-start(bf16[32,112,128]{2,1,0:T(8,128)(2,1)} %broadcast_in_dim.6), calls=%async_computation | async-start | bytes 1835008 | tf_op jit(solution)/shard_map/all_to_all | solution.py:200
  16.0 25.3 %collective-permute-start.2 = (bf16[128,3584]{1,0:T(8,128)(2,1)S(1)}, bf16[128,3584]{1,0:T(8,128)(2,1)}, u32[]{:S(2)}, u32[]{:S(2)}) collective-permute-start(bf16[128,3584]{1,0:T(8,128)(2,1)S(1)} %copy-done), channel_id=1, source_target_pairs={{0,32},{32,0},{1,33},{33,1},{2,34},{34,2},{3,35},{35,3},{4,36},{36... | collective-permute-start | bytes 2752520 | tf_op jit(solution)/shard_map/ppermute | solution.py:226
  24.8 16.5 %collective-permute-start.4 = (bf16[128,3584]{1,0:T(8,128)(2,1)S(1)}, bf16[128,3584]{1,0:T(8,128)(2,1)}, u32[]{:S(2)}, u32[]{:S(2)}) collective-permute-start(bf16[128,3584]{1,0:T(8,128)(2,1)S(1)} %collective-permute-done.3.across), channel_id=1, source_target_pairs={{0,32},{32,0},{1,33},{33,1},{2,34},{34,2},{3,35},{35,3},{4,36},{36... | collective-permute-start | bytes 2752520 | tf_op jit(solution)/shard_map/ppermute | solution.py:226
  26.8 14.5 %collective-permute-start.1 = (bf16[16,1792]{1,0:T(8,128)(2,1)S(1)}, bf16[16,1792]{1,0:T(8,128)(2,1)S(1)}, u32[]{:S(2)}, u32[]{:S(2)}) collective-permute-start(bf16[16,1792]{1,0:T(8,128)(2,1)S(1)} %slice.14.head), channel_id=1, source_target_pairs={{0,16},{4,20},{8,24},{12,28},{32,48},{36,52},{40,56},{44,60},{64,8... | collective-permute-start | bytes 172040 | tf_op jit(solution)/shard_map/ppermute | solution.py:213
  28.1 13.2 %collective-permute-start = (bf16[16,1792]{1,0:T(8,128)(2,1)S(1)}, bf16[16,1792]{1,0:T(8,128)(2,1)S(1)}, u32[]{:S(2)}, u32[]{:S(2)}) collective-permute-start(bf16[16,1792]{1,0:T(8,128)(2,1)S(1)} %slice.14.head), channel_id=1, source_target_pairs={{0,8},{4,12},{8,16},{12,20},{16,24},{20,28},{32,40},{36,44},{40,48... | collective-permute-start | bytes 172040 | tf_op jit(solution)/shard_map/ppermute | solution.py:213
  57.2 17.3 %collective-permute-start.6 = (bf16[2,2,512,128]{3,2,1,0:T(8,128)(2,1)S(1)}, bf16[2,2,512,128]{3,2,1,0:T(8,128)(2,1)S(1)}, u32[]{:S(2)}, u32[]{:S(2)}) collective-permute-start(bf16[2,2,512,128]{3,2,1,0:T(8,128)(2,1)S(1)} %bitcast.4), channel_id=1, source_target_pairs={{4,0},{8,4},{12,8},{16,12},{20,16},{24,20},{28,24},{5,1},{9,5},{13... | collective-permute-start | bytes 1572872 | tf_op jit(solution)/shard_map/ppermute | solution.py:204
  60.6 23.5 %collective-permute-start.5 = (bf16[2,2,512,128]{3,2,1,0:T(8,128)(2,1)S(1)}, bf16[2,2,512,128]{3,2,1,0:T(8,128)(2,1)S(1)}, u32[]{:S(2)}, u32[]{:S(2)}) collective-permute-start(bf16[2,2,512,128]{3,2,1,0:T(8,128)(2,1)S(1)} %bitcast.5), channel_id=1, source_target_pairs={{0,4},{4,8},{8,12},{12,16},{16,20},{20,24},{24,28},{1,5},{5,9},{9,... | collective-permute-start | bytes 1572872 | tf_op jit(solution)/shard_map/ppermute | solution.py:204
  63.7 10.7 %copy-start.2 = (s32[2]{0:T(128)S(1)}, s32[2]{0:T(128)}, u32[]{:S(2)}) copy-start(s32[2]{0:T(128)} %tiles.5) | copy-start | bytes 28
  63.7 10.7 %copy-start.3 = (s32[2]{0:T(128)S(1)}, s32[2]{0:T(128)}, u32[]{:S(2)}) copy-start(s32[2]{0:T(128)} %lengths.5) | copy-start | bytes 28
  63.7 20.3 %all-to-all-start.2 = ((bf16[8,4,16,128]{3,2,1,0:T(8,128)(2,1)}), bf16[8,4,16,128]{3,2,1,0:T(8,128)(2,1)S(1)}, u32[]{:S(2)}, u32[]{:S(2)}) async-start(bf16[8,4,16,128]{3,2,1,0:T(8,128)(2,1)} %broadcast_in_dim.15), calls=%async_computation.2 | async-start | bytes 262144 | tf_op jit(solution)/shard_map/all_to_all | solution.py:200
  76.0 13.6 %collective-permute-start.8 = (bf16[240,128]{1,0:T(8,128)(2,1)S(1)}, bf16[240,128]{1,0:T(8,128)(2,1)S(1)}, u32[]{:S(2)}, u32[]{:S(2)}) collective-permute-start(bf16[240,128]{1,0:T(8,128)(2,1)S(1)} %shard_map.66.pack), channel_id=1, source_target_pairs={{16,0},{20,4},{24,8},{28,12},{48,32},{52,36},{56,40},{60,44},{80,6... | collective-permute-start | bytes 184328 | tf_op jit(solution)/shard_map/ppermute | solution.py:213
  78.8 10.8 %collective-permute-start.7 = (bf16[240,128]{1,0:T(8,128)(2,1)S(1)}, bf16[240,128]{1,0:T(8,128)(2,1)S(1)}, u32[]{:S(2)}, u32[]{:S(2)}) collective-permute-start(bf16[240,128]{1,0:T(8,128)(2,1)S(1)} %shard_map.66.pack), channel_id=1, source_target_pairs={{8,0},{12,4},{16,8},{20,12},{24,16},{28,20},{40,32},{44,36},{48,40... | collective-permute-start | bytes 184328 | tf_op jit(solution)/shard_map/ppermute | solution.py:213

commit v5 on v4

--- a/solution.py
+++ b/solution.py
@@ -208,8 +208,8 @@
     return jnp.broadcast_to(array[None], (n,) + array.shape)
 
 
-def along(array, shift):
-    pairs = [(XS * y, XS * (y + shift)) for y in range(YS) if 0 <= y + shift < YS]
+def along(array, shift, source, to):
+    pairs = [(XS * y + source, XS * (y + shift) + to) for y in range(YS) if 0 <= y + shift < YS]
     return lax.ppermute(array, ("y", "x"), pairs)
 
 
@@ -224,7 +224,7 @@
     weights = exchange(copies(shard, YS * XS), ("y", "x")).reshape(tokens.shape[1], HEAD)
     head = queries[:ASK]
     sibling, corner = lax.ppermute(tokens, "core", swap), lax.ppermute(across, "core", swap)
-    head2, head4 = along(head, 2), along(head, 4)
+    head2, head4 = along(head, 2, 0, 1), along(head, 4, 0, 1)
     weights, head2, head4 = lax.optimization_barrier((weights, head2, head4))
 
     rows = call(
@@ -241,7 +241,7 @@
         [pltpu.VMEM(head.shape, bf16)],
         micros=2,
     )(*at, tile, below, head, head2, head4)
-    back2, back4 = along(pack, -2), along(pack, -4)
+    back2, back4 = along(pack, -2, 1, 0), along(pack, -4, 1, 0)
 
     banded = call(
         attend_body,

time: 91.7 us -> 91 us (level)
  the two profiles are of different devices: /device:TPU:176 before, /device:TPU:186 now
where the time goes in v5:
time: 91 us; the launch traced here: 90.3 us
  starting transfers between devices  42.7 us (47%)
  waiting for transfers between devices  20.7 us (23%)
  blocking collectives  13 us (14%)
  Pallas kernels  11.2 us (12%)
  local copies, waits for them, and re-layouts  1.74 us (2%)
    all_to_all x2, starting transfers between devices, exchange(): return lax.all_to_all(array, axis, 0, 0, tiled=False)  18.1 us
    all_to_all x1, blocking collectives, exchange(): return lax.all_to_all(array, axis, 0, 0, tiled=False)  13 us
    ppermute x4, starting transfers between devices, along(): return lax.ppermute(array, ('y', 'x'), pairs)  12.3 us
    ppermute x4, waiting for transfers between devices, along(): return lax.ppermute(array, ('y', 'x'), pairs)  11.5 us
    ppermute x1, waiting for transfers between devices, per_device(): across = lax.ppermute(tokens, 'pair', swap)  7.02 us
    pallas_call x1, Pallas kernels, per_device(): call(attend_body, jax.ShapeDtypeStruct(queries.shape, bf16), 5, [pltpu.VM...  5.55 us
    ppermute x1, starting transfers between devices, per_device(): across = lax.ppermute(tokens, 'pair', swap)  4.27 us
    ppermute x2, starting transfers between devices, down(): lax.ppermute(array, 'y', [(y, y + shift) for y in range(YS) if 0 <= y + s...  4.16 us
  transfers between devices with their start and end apart: 11, of which 4 were waited for; matrix products, arithmetic and copies ran while one was open for 3% of the time, Pallas kernels for 8%

profile of v5, /device:TPU:186, one launch (start us, length us, event | category | flops | bytes accessed | tf_op | source)
XLA Modules:
  0.0 90.3 jit_solution(10900298380041780333)
XLA Ops:
  0.0 4.3 %collective-permute-start.3 = (bf16[128,3584]{1,0:T(8,128)(2,1)}, bf16[128,3584]{1,0:T(8,128)(2,1)S(1)}, u32[]{:S(2)}, u32[]{:S(2)}) collective-permute-start(bf16[128,3584]{1,0:T(8,128)(2,1)} %mine.1), channel_id=1, source_target_pairs={{0,64},{64,0},{1,65},{65,1},{2,66},{66,2},{3,67},{67,3},{4,68},{68... | collective-permute-start | bytes 2752520 | tf_op jit(solution)/shard_map/ppermute | solution.py:220
  4.3 0.8 broadcast_select_fusion
  5.1 1.0 %broadcast_in_dim.6 = bf16[32,112,128]{2,1,0:T(8,128)(2,1)} broadcast(bf16[112,128]{1,0:T(8,128)(2,1)S(1)} %slice_select_fusion), dimensions={1,2} | broadcast | bytes 946176 | tf_op jit(solution)/shard_map/broadcast_in_dim | solution.py:208
  6.2 9.7 %all-to-all-start = ((bf16[32,112,128]{2,1,0:T(8,128)(2,1)}), bf16[32,112,128]{2,1,0:T(8,128)(2,1)S(1)}, u32[]{:S(2)}, u32[]{:S(2)}) async-start(bf16[32,112,128]{2,1,0:T(8,128)(2,1)} %broadcast_in_dim.6), calls=%async_computation | async-start | bytes 1835008 | tf_op jit(solution)/shard_map/all_to_all | solution.py:200
  15.9 1.9 %collective-permute-start.2 = (bf16[128,3584]{1,0:T(8,128)(2,1)S(1)}, bf16[128,3584]{1,0:T(8,128)(2,1)}, u32[]{:S(2)}, u32[]{:S(2)}) collective-permute-start(bf16[128,3584]{1,0:T(8,128)(2,1)S(1)} %copy-done), channel_id=1, source_target_pairs={{0,32},{32,0},{1,33},{33,1},{2,34},{34,2},{3,35},{35,3},{4,36},{36... | collective-permute-start | bytes 2752520 | tf_op jit(solution)/shard_map/ppermute | solution.py:226
  17.8 7.0 %collective-permute-done.3.across = bf16[128,3584]{1,0:T(8,128)(2,1)S(1)} collective-permute-done((bf16[128,3584]{1,0:T(8,128)(2,1)}, bf16[128,3584]{1,0:T(8,128)(2,1)S(1)}, u32[]{:S(2)}, u32[]{:S(2)}) %collective-permute-start.3) | collective-permute-done | bytes 917536 | tf_op jit(solution)/shard_map/ppermute | solution.py:220
  24.8 1.9 %collective-permute-start.4 = (bf16[128,3584]{1,0:T(8,128)(2,1)S(1)}, bf16[128,3584]{1,0:T(8,128)(2,1)}, u32[]{:S(2)}, u32[]{:S(2)}) collective-permute-start(bf16[128,3584]{1,0:T(8,128)(2,1)S(1)} %collective-permute-done.3.across), channel_id=1, source_target_pairs={{0,32},{32,0},{1,33},{33,1},{2,34},{34,2},{3,35},{35,3},{4,36},{36... | collective-permute-start | bytes 2752520 | tf_op jit(solution)/shard_map/ppermute | solution.py:226
  26.8 1.3 %collective-permute-start.1 = (bf16[16,1792]{1,0:T(8,128)(2,1)S(1)}, bf16[16,1792]{1,0:T(8,128)(2,1)S(1)}, u32[]{:S(2)}, u32[]{:S(2)}) collective-permute-start(bf16[16,1792]{1,0:T(8,128)(2,1)S(1)} %slice.14.head), channel_id=1, source_target_pairs={{0,17},{4,21},{8,25},{12,29},{32,49},{36,53},{40,57},{44,61},{64,8... | collective-permute-start | bytes 172040 | tf_op jit(solution)/shard_map/ppermute | solution.py:213
  28.1 1.3 %collective-permute-start = (bf16[16,1792]{1,0:T(8,128)(2,1)S(1)}, bf16[16,1792]{1,0:T(8,128)(2,1)S(1)}, u32[]{:S(2)}, u32[]{:S(2)}) collective-permute-start(bf16[16,1792]{1,0:T(8,128)(2,1)S(1)} %slice.14.head), channel_id=1, source_target_pairs={{0,9},{4,13},{8,17},{12,21},{16,25},{20,29},{32,41},{36,45},{40,49... | collective-permute-start | bytes 172040 | tf_op jit(solution)/shard_map/ppermute | solution.py:213
  29.4 9.7 %collective-permute-done.1.head4 = bf16[16,1792]{1,0:T(8,128)(2,1)S(1)} collective-permute-done((bf16[16,1792]{1,0:T(8,128)(2,1)S(1)}, bf16[16,1792]{1,0:T(8,128)(2,1)S(1)}, u32[]{:S(2)}, u32[]{:S(2)}) %collective-permute-start.1) | collective-permute-done | bytes 57376 | tf_op jit(solution)/shard_map/ppermute | solution.py:213
  39.0 1.8 %collective-permute-done.head2 = bf16[16,1792]{1,0:T(8,128)(2,1)S(1)} collective-permute-done((bf16[16,1792]{1,0:T(8,128)(2,1)S(1)}, bf16[16,1792]{1,0:T(8,128)(2,1)S(1)}, u32[]{:S(2)}, u32[]{:S(2)}) %collective-permute-start) | collective-permute-done | bytes 57376 | tf_op jit(solution)/shard_map/ppermute | solution.py:213
  40.8 0.0 collective-permute-done.2.sibling
  40.8 2.6 %shard_map.64 = bf16[2,2,4,128,128]{4,3,2,1,0:T(8,128)(2,1)S(1)} custom-call(bf16[3584,128]{1,0:T(8,128)(2,1)S(1)} %bitcast.9, bf16[128,3584]{1,0:T(8,128)(2,1)S(1)} %copy-done, bf16[128,3584]{1,0:T(8,128)(2,1)} %collective-permute-done.2.sibling, bf16[128,3584]{1,0:T(8,128)(2,1)S(1)} %collective-permute-done.3.across, ...), custom_call_target="tpu_custom_call" | custom-call | bytes 7380000 | tf_op jit(solution)/shard_map/pallas_call | solution.py:230
  43.4 13.0 %all_to_all.15 = bf16[16,128,128]{2,1,0:T(8,128)(2,1)S(1)} all-to-all(bf16[16,128,128]{2,1,0:T(8,128)(2,1)S(1)} %bitcast.10), channel_id=1, replica_groups=mesh['z'=4,'pair'=2,'core'=2,'y'=8,'x'=4] {'pair','core','x'}, dimensions={0} | all-to-all | bytes 1048576 | tf_op jit(solution)/shard_map/all_to_all | solution.py:200
  56.4 2.9 %collective-permute-start.6 = (bf16[2,2,512,128]{3,2,1,0:T(8,128)(2,1)S(1)}, bf16[2,2,512,128]{3,2,1,0:T(8,128)(2,1)S(1)}, u32[]{:S(2)}, u32[]{:S(2)}) collective-permute-start(bf16[2,2,512,128]{3,2,1,0:T(8,128)(2,1)S(1)} %bitcast.4), channel_id=1, source_target_pairs={{4,0},{8,4},{12,8},{16,12},{20,16},{24,20},{28,24},{5,1},{9,5},{13... | collective-permute-start | bytes 1572872 | tf_op jit(solution)/shard_map/ppermute | solution.py:204
  59.3 1.3 %collective-permute-start.5 = (bf16[2,2,512,128]{3,2,1,0:T(8,128)(2,1)S(1)}, bf16[2,2,512,128]{3,2,1,0:T(8,128)(2,1)S(1)}, u32[]{:S(2)}, u32[]{:S(2)}) collective-permute-start(bf16[2,2,512,128]{3,2,1,0:T(8,128)(2,1)S(1)} %bitcast.5), channel_id=1, source_target_pairs={{0,4},{4,8},{8,12},{12,16},{16,20},{20,24},{24,28},{1,5},{5,9},{9,... | collective-permute-start | bytes 1572872 | tf_op jit(solution)/shard_map/ppermute | solution.py:204
  60.6 0.7 broadcast_in_dim.15
  61.3 8.4 %all-to-all-start.2 = ((bf16[8,4,16,128]{3,2,1,0:T(8,128)(2,1)}), bf16[8,4,16,128]{3,2,1,0:T(8,128)(2,1)S(1)}, u32[]{:S(2)}, u32[]{:S(2)}) async-start(bf16[8,4,16,128]{3,2,1,0:T(8,128)(2,1)} %broadcast_in_dim.15), calls=%async_computation.2 | async-start | bytes 262144 | tf_op jit(solution)/shard_map/all_to_all | solution.py:200
  69.7 2.2 %collective-permute-done.6.below = bf16[2,2,512,128]{3,2,1,0:T(8,128)(2,1)S(1)} collective-permute-done((bf16[2,2,512,128]{3,2,1,0:T(8,128)(2,1)S(1)}, bf16[2,2,512,128]{3,2,1,0:T(8,128)(2,1)S(1)}, u32[]{:S(2)}, u32[]{:S(2)}) %collective-permute-start.6) | collective-permute-done | bytes 524320 | tf_op jit(solution)/shard_map/ppermute | solution.py:204
  71.9 1.6 %shard_map.66.pack = bf16[240,128]{1,0:T(8,128)(2,1)S(1)} custom-call(s32[2]{0:T(128)S(1)} %copy-done.2, s32[2]{0:T(128)S(1)} %copy-done.3, bf16[2,2,512,128]{3,2,1,0:T(8,128)(2,1)S(1)} %bitcast.7, bf16[2,2,512,128]{3,2,1,0:T(8,128)(2,1)S(1)} %collective-permute-done.6.below, bf16[16,1792]{1,0:T(8,128)(2,1)S(1)} %slice.14.head, ...), custom_call_target="tpu_custom_call" | custom-call | bytes 7380000 | tf_op jit(solution)/shard_map/pallas_call | solution.py:237
  73.5 8.4 %collective-permute-start.8 = (bf16[240,128]{1,0:T(8,128)(2,1)S(1)}, bf16[240,128]{1,0:T(8,128)(2,1)S(1)}, u32[]{:S(2)}, u32[]{:S(2)}) collective-permute-start(bf16[240,128]{1,0:T(8,128)(2,1)S(1)} %shard_map.66.pack), channel_id=1, source_target_pairs={{17,0},{21,4},{25,8},{29,12},{49,32},{53,36},{57,40},{61,44},{81,6... | collective-permute-start | bytes 184328 | tf_op jit(solution)/shard_map/ppermute | solution.py:213
  82.0 1.3 %collective-permute-start.7 = (bf16[240,128]{1,0:T(8,128)(2,1)S(1)}, bf16[240,128]{1,0:T(8,128)(2,1)S(1)}, u32[]{:S(2)}, u32[]{:S(2)}) collective-permute-start(bf16[240,128]{1,0:T(8,128)(2,1)S(1)} %shard_map.66.pack), channel_id=1, source_target_pairs={{9,0},{13,4},{17,8},{21,12},{25,16},{29,20},{41,32},{45,36},{49,40... | collective-permute-start | bytes 184328 | tf_op jit(solution)/shard_map/ppermute | solution.py:213
  83.3 5.6 %shard_map.65.banded = bf16[128,1792]{1,0:T(8,128)(2,1)} custom-call(s32[2]{0:T(128)S(1)} %copy-done.2, s32[2]{0:T(128)S(1)} %copy-done.3, bf16[128,1792]{1,0:T(8,128)(2,1)S(1)} %copy-done.1, bf16[2,2,512,128]{3,2,1,0:T(8,128)(2,1)S(1)} %bitcast.8, bf16[2,2,512,128]{3,2,1,0:T(8,128)(2,1)S(1)} %collective-permute-done.5.above, ...), custom_call_target="tpu_custom_call" | custom-call | bytes 18450000 | tf_op jit(solution)/shard_map/pallas_call | solution.py:246
  88.8 1.5 %shard_map.67 = bf16[128,1792]{1,0:T(8,128)(2,1)} custom-call(s32[2]{0:T(128)S(1)} %copy-done.2, s32[2]{0:T(128)S(1)} %copy-done.3, bf16[128,1792]{1,0:T(8,128)(2,1)} %shard_map.65.banded, bf16[240,128]{1,0:T(8,128)(2,1)S(1)} %shard_map.66.pack, bf16[240,128]{1,0:T(8,128)(2,1)S(1)} %collective-permute-done.7.back2, ...), custom_call_target="tpu_custom_call", output_to_operand_aliasing={{}: (2, {})} | custom-call | bytes 3690000 | tf_op jit(solution)/shard_map/pallas_call | solution.py:258
  (17 shorter events, 0.1 us)
Async XLA Ops:
  0.0 24.8 %collective-permute-start.3 = (bf16[128,3584]{1,0:T(8,128)(2,1)}, bf16[128,3584]{1,0:T(8,128)(2,1)S(1)}, u32[]{:S(2)}, u32[]{:S(2)}) collective-permute-start(bf16[128,3584]{1,0:T(8,128)(2,1)} %mine.1), channel_id=1, source_target_pairs={{0,64},{64,0},{1,65},{65,1},{2,66},{66,2},{3,67},{67,3},{4,68},{68... | collective-permute-start | bytes 2752520 | tf_op jit(solution)/shard_map/ppermute | solution.py:220
  6.2 9.7 %copy-start = (bf16[128,3584]{1,0:T(8,128)(2,1)S(1)}, bf16[128,3584]{1,0:T(8,128)(2,1)}, u32[]{:S(2)}) copy-start(bf16[128,3584]{1,0:T(8,128)(2,1)} %mine.1) | copy-start | bytes 2752516
  6.2 20.6 %copy-start.1 = (bf16[128,1792]{1,0:T(8,128)(2,1)S(1)}, bf16[128,1792]{1,0:T(8,128)(2,1)}, u32[]{:S(2)}) copy-start(bf16[128,1792]{1,0:T(8,128)(2,1)} %queries.1) | copy-start | bytes 1376260
  6.2 34.6 %all-to-all-start = ((bf16[32,112,128]{2,1,0:T(8,128)(2,1)}), bf16[32,112,128]{2,1,0:T(8,128)(2,1)S(1)}, u32[]{:S(2)}, u32[]{:S(2)}) async-start(bf16[32,112,128]{2,1,0:T(8,128)(2,1)} %broadcast_in_dim.6), calls=%async_computation | async-start | bytes 1835008 | tf_op jit(solution)/shard_map/all_to_all | solution.py:200
  15.9 25.0 %collective-permute-start.2 = (bf16[128,3584]{1,0:T(8,128)(2,1)S(1)}, bf16[128,3584]{1,0:T(8,128)(2,1)}, u32[]{:S(2)}, u32[]{:S(2)}) collective-permute-start(bf16[128,3584]{1,0:T(8,128)(2,1)S(1)} %copy-done), channel_id=1, source_target_pairs={{0,32},{32,0},{1,33},{33,1},{2,34},{34,2},{3,35},{35,3},{4,36},{36... | collective-permute-start | bytes 2752520 | tf_op jit(solution)/shard_map/ppermute | solution.py:226
  24.8 16.0 %collective-permute-start.4 = (bf16[128,3584]{1,0:T(8,128)(2,1)S(1)}, bf16[128,3584]{1,0:T(8,128)(2,1)}, u32[]{:S(2)}, u32[]{:S(2)}) collective-permute-start(bf16[128,3584]{1,0:T(8,128)(2,1)S(1)} %collective-permute-done.3.across), channel_id=1, source_target_pairs={{0,32},{32,0},{1,33},{33,1},{2,34},{34,2},{3,35},{35,3},{4,36},{36... | collective-permute-start | bytes 2752520 | tf_op jit(solution)/shard_map/ppermute | solution.py:226
  26.8 12.3 %collective-permute-start.1 = (bf16[16,1792]{1,0:T(8,128)(2,1)S(1)}, bf16[16,1792]{1,0:T(8,128)(2,1)S(1)}, u32[]{:S(2)}, u32[]{:S(2)}) collective-permute-start(bf16[16,1792]{1,0:T(8,128)(2,1)S(1)} %slice.14.head), channel_id=1, source_target_pairs={{0,17},{4,21},{8,25},{12,29},{32,49},{36,53},{40,57},{44,61},{64,8... | collective-permute-start | bytes 172040 | tf_op jit(solution)/shard_map/ppermute | solution.py:213
  28.1 12.8 %collective-permute-start = (bf16[16,1792]{1,0:T(8,128)(2,1)S(1)}, bf16[16,1792]{1,0:T(8,128)(2,1)S(1)}, u32[]{:S(2)}, u32[]{:S(2)}) collective-permute-start(bf16[16,1792]{1,0:T(8,128)(2,1)S(1)} %slice.14.head), channel_id=1, source_target_pairs={{0,9},{4,13},{8,17},{12,21},{16,25},{20,29},{32,41},{36,45},{40,49... | collective-permute-start | bytes 172040 | tf_op jit(solution)/shard_map/ppermute | solution.py:213
  56.4 15.5 %collective-permute-start.6 = (bf16[2,2,512,128]{3,2,1,0:T(8,128)(2,1)S(1)}, bf16[2,2,512,128]{3,2,1,0:T(8,128)(2,1)S(1)}, u32[]{:S(2)}, u32[]{:S(2)}) collective-permute-start(bf16[2,2,512,128]{3,2,1,0:T(8,128)(2,1)S(1)} %bitcast.4), channel_id=1, source_target_pairs={{4,0},{8,4},{12,8},{16,12},{20,16},{24,20},{28,24},{5,1},{9,5},{13... | collective-permute-start | bytes 1572872 | tf_op jit(solution)/shard_map/ppermute | solution.py:204
  59.3 24.0 %collective-permute-start.5 = (bf16[2,2,512,128]{3,2,1,0:T(8,128)(2,1)S(1)}, bf16[2,2,512,128]{3,2,1,0:T(8,128)(2,1)S(1)}, u32[]{:S(2)}, u32[]{:S(2)}) collective-permute-start(bf16[2,2,512,128]{3,2,1,0:T(8,128)(2,1)S(1)} %bitcast.5), channel_id=1, source_target_pairs={{0,4},{4,8},{8,12},{12,16},{16,20},{20,24},{24,28},{1,5},{5,9},{9,... | collective-permute-start | bytes 1572872 | tf_op jit(solution)/shard_map/ppermute | solution.py:204
  61.3 10.6 %copy-start.2 = (s32[2]{0:T(128)S(1)}, s32[2]{0:T(128)}, u32[]{:S(2)}) copy-start(s32[2]{0:T(128)} %tiles.5) | copy-start | bytes 28
  61.3 10.6 %copy-start.3 = (s32[2]{0:T(128)S(1)}, s32[2]{0:T(128)}, u32[]{:S(2)}) copy-start(s32[2]{0:T(128)} %lengths.5) | copy-start | bytes 28
  61.3 22.0 %all-to-all-start.2 = ((bf16[8,4,16,128]{3,2,1,0:T(8,128)(2,1)}), bf16[8,4,16,128]{3,2,1,0:T(8,128)(2,1)S(1)}, u32[]{:S(2)}, u32[]{:S(2)}) async-start(bf16[8,4,16,128]{3,2,1,0:T(8,128)(2,1)} %broadcast_in_dim.15), calls=%async_computation.2 | async-start | bytes 262144 | tf_op jit(solution)/shard_map/all_to_all | solution.py:200
  73.5 15.3 %collective-permute-start.8 = (bf16[240,128]{1,0:T(8,128)(2,1)S(1)}, bf16[240,128]{1,0:T(8,128)(2,1)S(1)}, u32[]{:S(2)}, u32[]{:S(2)}) collective-permute-start(bf16[240,128]{1,0:T(8,128)(2,1)S(1)} %shard_map.66.pack), channel_id=1, source_target_pairs={{17,0},{21,4},{25,8},{29,12},{49,32},{53,36},{57,40},{61,44},{81,6... | collective-permute-start | bytes 184328 | tf_op jit(solution)/shard_map/ppermute | solution.py:213
  82.0 6.9 %collective-permute-start.7 = (bf16[240,128]{1,0:T(8,128)(2,1)S(1)}, bf16[240,128]{1,0:T(8,128)(2,1)S(1)}, u32[]{:S(2)}, u32[]{:S(2)}) collective-permute-start(bf16[240,128]{1,0:T(8,128)(2,1)S(1)} %shard_map.66.pack), channel_id=1, source_target_pairs={{9,0},{13,4},{17,8},{21,12},{25,16},{29,20},{41,32},{45,36},{49,40... | collective-permute-start | bytes 184328 | tf_op jit(solution)/shard_map/ppermute | solution.py:213

commit v6 on v5

--- a/solution.py
+++ b/solution.py
@@ -169,14 +169,16 @@
             out[:, head_columns(GROUP * h + g)] = answer[g * ROWS : (g + 1) * ROWS]
 
 
-def patch_body(tiles, lengths, banded, pack, back2, back4, out):
+def patch_body(tiles, lengths, banded, pack, back2, back4, out, top, arrived, left):
     y, x, start, stop, asked = place(tiles, lengths)
-    out[...] = banded[...]
 
     @pl.when((y == start) & (x == 0))
     def _():
+        fetch = pltpu.make_async_copy(banded.at[pl.ds(0, ASK), :], top, arrived)
+        fetch.start()
         chosen = lax.broadcasted_iota(jnp.int32, (ASK, HEAD), 0) < asked
         sources = ((pack, True), (back2, start + 2 < stop), (back4, start + 4 < stop))
+        answers = []
         for h in range(KV):
             logs = []
             for source, valid in sources:
@@ -190,10 +192,16 @@
             for share, (source, valid) in zip(shares, sources):
                 block = jnp.where(valid, source[h * BLOCK : (h + 1) * BLOCK, :].astype(f32), 0.0)
                 answer = answer + to_column(share / total, BLOCK) * block
+            answers.append(answer)
+        fetch.wait()
+        for h in range(KV):
             for g in range(GROUP):
                 mine = head_columns(GROUP * h + g)
-                old = out[0:ASK, mine].astype(f32)
-                out[0:ASK, mine] = jnp.where(chosen, answer[g * ASK : (g + 1) * ASK], old).astype(bf16)
+                old = top[:, mine].astype(f32)
+                top[:, mine] = jnp.where(chosen, answers[h][g * ASK : (g + 1) * ASK], old).astype(bf16)
+        store = pltpu.make_async_copy(top, out.at[pl.ds(0, ASK), :], left)
+        store.start()
+        store.wait()
 
 
 def exchange(array, axis):
@@ -254,13 +262,16 @@
         ],
         micros=5,
     )(*at, queries, tile, above, below, questions)
-    top = pl.BlockSpec((ASK, queries.shape[1]), lambda i: (0, 0))
     return pl.pallas_call(
         patch_body,
         out_shape=jax.ShapeDtypeStruct(queries.shape, bf16),
-        grid=(1,),
-        in_specs=[spec(pltpu.SMEM)] * 2 + [top] + [spec(pltpu.VMEM)] * 3,
-        out_specs=top,
+        in_specs=[spec(pltpu.SMEM)] * 2 + [spec(pl.ANY)] + [spec(pltpu.VMEM)] * 3,
+        out_specs=spec(pl.ANY),
+        scratch_shapes=[
+            pltpu.VMEM((ASK, queries.shape[1]), bf16),
+            pltpu.SemaphoreType.DMA,
+            pltpu.SemaphoreType.DMA,
+        ],
         input_output_aliases={2: 0},
         compiler_params=pltpu.CompilerParams(vmem_limit_bytes=4 * 1024 * 1024),
         cost_estimate=pl.CostEstimate(flops=0, bytes_accessed=3690000, transcendentals=0),

time: 91 us -> 91.1 us (level)
  the two profiles are of different devices: /device:TPU:186 before, /device:TPU:128 now
where the time goes in v6:
time: 91.1 us; the launch traced here: 90.5 us
  starting transfers between devices  41.9 us (46%)
  waiting for transfers between devices  20.4 us (22%)
  blocking collectives  13.7 us (15%)
  Pallas kernels  11.7 us (13%)
  local copies, waits for them, and re-layouts  1.74 us (2%)
    all_to_all x2, starting transfers between devices, exchange(): return lax.all_to_all(array, axis, 0, 0, tiled=False)  15.4 us
    all_to_all x1, blocking collectives, exchange(): return lax.all_to_all(array, axis, 0, 0, tiled=False)  13.7 us
    ppermute x4, starting transfers between devices, along(): return lax.ppermute(array, ('y', 'x'), pairs)  12.5 us
    ppermute x1, waiting for transfers between devices, per_device(): across = lax.ppermute(tokens, 'pair', swap)  6.6 us
    ppermute x2, starting transfers between devices, down(): lax.ppermute(array, 'y', [(y, y + shift) for y in range(YS) if 0 <= y + s...  5.86 us
    all_to_all x2, waiting for transfers between devices, exchange(): return lax.all_to_all(array, axis, 0, 0, tiled=False)  5.82 us
    pallas_call x1, Pallas kernels, per_device(): call(attend_body, jax.ShapeDtypeStruct(queries.shape, bf16), 5, [pltpu.VM...  5.55 us
    ppermute x2, waiting for transfers between devices, down(): lax.ppermute(array, 'y', [(y, y + shift) for y in range(YS) if 0 <= y + s...  5.07 us
  transfers between devices with their start and end apart: 11, of which 7 were waited for; matrix products, arithmetic and copies ran while one was open for 3% of the time, Pallas kernels for 8%

profile of v6, /device:TPU:128, one launch (start us, length us, event | category | flops | bytes accessed | tf_op | source)
XLA Modules:
  0.0 90.5 jit_solution(6883255925169206726)
XLA Ops:
  0.0 4.3 %collective-permute-start.3 = (bf16[128,3584]{1,0:T(8,128)(2,1)}, bf16[128,3584]{1,0:T(8,128)(2,1)S(1)}, u32[]{:S(2)}, u32[]{:S(2)}) collective-permute-start(bf16[128,3584]{1,0:T(8,128)(2,1)} %mine.1), channel_id=1, source_target_pairs={{0,64},{64,0},{1,65},{65,1},{2,66},{66,2},{3,67},{67,3},{4,68},{68... | collective-permute-start | bytes 2752520 | tf_op jit(solution)/shard_map/ppermute | solution.py:228
  4.3 0.8 broadcast_select_fusion
  5.1 1.0 %broadcast_in_dim.6 = bf16[32,112,128]{2,1,0:T(8,128)(2,1)} broadcast(bf16[112,128]{1,0:T(8,128)(2,1)S(1)} %slice_select_fusion), dimensions={1,2} | broadcast | bytes 946176 | tf_op jit(solution)/shard_map/broadcast_in_dim | solution.py:216
  6.2 10.1 %all-to-all-start = ((bf16[32,112,128]{2,1,0:T(8,128)(2,1)}), bf16[32,112,128]{2,1,0:T(8,128)(2,1)S(1)}, u32[]{:S(2)}, u32[]{:S(2)}) async-start(bf16[32,112,128]{2,1,0:T(8,128)(2,1)} %broadcast_in_dim.6), calls=%async_computation | async-start | bytes 1835008 | tf_op jit(solution)/shard_map/all_to_all | solution.py:208
  16.3 1.9 %collective-permute-start.2 = (bf16[128,3584]{1,0:T(8,128)(2,1)S(1)}, bf16[128,3584]{1,0:T(8,128)(2,1)}, u32[]{:S(2)}, u32[]{:S(2)}) collective-permute-start(bf16[128,3584]{1,0:T(8,128)(2,1)S(1)} %copy-done), channel_id=1, source_target_pairs={{0,32},{32,0},{1,33},{33,1},{2,34},{34,2},{3,35},{35,3},{4,36},{36... | collective-permute-start | bytes 2752520 | tf_op jit(solution)/shard_map/ppermute | solution.py:234
  18.2 6.6 %collective-permute-done.3.across = bf16[128,3584]{1,0:T(8,128)(2,1)S(1)} collective-permute-done((bf16[128,3584]{1,0:T(8,128)(2,1)}, bf16[128,3584]{1,0:T(8,128)(2,1)S(1)}, u32[]{:S(2)}, u32[]{:S(2)}) %collective-permute-start.3) | collective-permute-done | bytes 917536 | tf_op jit(solution)/shard_map/ppermute | solution.py:228
  24.8 1.9 %collective-permute-start.4 = (bf16[128,3584]{1,0:T(8,128)(2,1)S(1)}, bf16[128,3584]{1,0:T(8,128)(2,1)}, u32[]{:S(2)}, u32[]{:S(2)}) collective-permute-start(bf16[128,3584]{1,0:T(8,128)(2,1)S(1)} %collective-permute-done.3.across), channel_id=1, source_target_pairs={{0,32},{32,0},{1,33},{33,1},{2,34},{34,2},{3,35},{35,3},{4,36},{36... | collective-permute-start | bytes 2752520 | tf_op jit(solution)/shard_map/ppermute | solution.py:234
  26.8 8.7 %collective-permute-start.1 = (bf16[16,1792]{1,0:T(8,128)(2,1)S(1)}, bf16[16,1792]{1,0:T(8,128)(2,1)S(1)}, u32[]{:S(2)}, u32[]{:S(2)}) collective-permute-start(bf16[16,1792]{1,0:T(8,128)(2,1)S(1)} %slice.14.head), channel_id=1, source_target_pairs={{0,17},{4,21},{8,25},{12,29},{32,49},{36,53},{40,57},{44,61},{64,8... | collective-permute-start | bytes 172040 | tf_op jit(solution)/shard_map/ppermute | solution.py:221
  35.4 1.3 %collective-permute-start = (bf16[16,1792]{1,0:T(8,128)(2,1)S(1)}, bf16[16,1792]{1,0:T(8,128)(2,1)S(1)}, u32[]{:S(2)}, u32[]{:S(2)}) collective-permute-start(bf16[16,1792]{1,0:T(8,128)(2,1)S(1)} %slice.14.head), channel_id=1, source_target_pairs={{0,9},{4,13},{8,17},{12,21},{16,25},{20,29},{32,41},{36,45},{40,49... | collective-permute-start | bytes 172040 | tf_op jit(solution)/shard_map/ppermute | solution.py:221
  36.7 1.1 %collective-permute-done.1.head4 = bf16[16,1792]{1,0:T(8,128)(2,1)S(1)} collective-permute-done((bf16[16,1792]{1,0:T(8,128)(2,1)S(1)}, bf16[16,1792]{1,0:T(8,128)(2,1)S(1)}, u32[]{:S(2)}, u32[]{:S(2)}) %collective-permute-start.1) | collective-permute-done | bytes 57376 | tf_op jit(solution)/shard_map/ppermute | solution.py:221
  37.8 1.3 %collective-permute-done.head2 = bf16[16,1792]{1,0:T(8,128)(2,1)S(1)} collective-permute-done((bf16[16,1792]{1,0:T(8,128)(2,1)S(1)}, bf16[16,1792]{1,0:T(8,128)(2,1)S(1)}, u32[]{:S(2)}, u32[]{:S(2)}) %collective-permute-start) | collective-permute-done | bytes 57376 | tf_op jit(solution)/shard_map/ppermute | solution.py:221
  39.1 3.6 %all-to-all-done = bf16[32,112,128]{2,1,0:T(8,128)(2,1)S(1)} async-done(((bf16[32,112,128]{2,1,0:T(8,128)(2,1)}), bf16[32,112,128]{2,1,0:T(8,128)(2,1)S(1)}, u32[]{:S(2)}, u32[]{:S(2)}) %all-to-all-start) | async-done | bytes 917536 | tf_op jit(solution)/shard_map/all_to_all | solution.py:208
  42.7 2.6 %shard_map.64 = bf16[2,2,4,128,128]{4,3,2,1,0:T(8,128)(2,1)S(1)} custom-call(bf16[3584,128]{1,0:T(8,128)(2,1)S(1)} %bitcast.9, bf16[128,3584]{1,0:T(8,128)(2,1)S(1)} %copy-done, bf16[128,3584]{1,0:T(8,128)(2,1)} %collective-permute-done.2.sibling, bf16[128,3584]{1,0:T(8,128)(2,1)S(1)} %collective-permute-done.3.across, ...), custom_call_target="tpu_custom_call" | custom-call | bytes 7380000 | tf_op jit(solution)/shard_map/pallas_call | solution.py:238
  45.3 13.7 %all_to_all.15 = bf16[16,128,128]{2,1,0:T(8,128)(2,1)S(1)} all-to-all(bf16[16,128,128]{2,1,0:T(8,128)(2,1)S(1)} %bitcast.10), channel_id=1, replica_groups=mesh['z'=4,'pair'=2,'core'=2,'y'=8,'x'=4] {'pair','core','x'}, dimensions={0} | all-to-all | bytes 1048576 | tf_op jit(solution)/shard_map/all_to_all | solution.py:208
  59.0 1.3 %collective-permute-start.6 = (bf16[2,2,512,128]{3,2,1,0:T(8,128)(2,1)S(1)}, bf16[2,2,512,128]{3,2,1,0:T(8,128)(2,1)S(1)}, u32[]{:S(2)}, u32[]{:S(2)}) collective-permute-start(bf16[2,2,512,128]{3,2,1,0:T(8,128)(2,1)S(1)} %bitcast.4), channel_id=1, source_target_pairs={{4,0},{8,4},{12,8},{16,12},{20,16},{24,20},{28,24},{5,1},{9,5},{13... | collective-permute-start | bytes 1572872 | tf_op jit(solution)/shard_map/ppermute | solution.py:212
  60.3 4.6 %collective-permute-start.5 = (bf16[2,2,512,128]{3,2,1,0:T(8,128)(2,1)S(1)}, bf16[2,2,512,128]{3,2,1,0:T(8,128)(2,1)S(1)}, u32[]{:S(2)}, u32[]{:S(2)}) collective-permute-start(bf16[2,2,512,128]{3,2,1,0:T(8,128)(2,1)S(1)} %bitcast.5), channel_id=1, source_target_pairs={{0,4},{4,8},{8,12},{12,16},{16,20},{20,24},{24,28},{1,5},{5,9},{9,... | collective-permute-start | bytes 1572872 | tf_op jit(solution)/shard_map/ppermute | solution.py:212
  65.5 5.4 %all-to-all-start.2 = ((bf16[8,4,16,128]{3,2,1,0:T(8,128)(2,1)}), bf16[8,4,16,128]{3,2,1,0:T(8,128)(2,1)S(1)}, u32[]{:S(2)}, u32[]{:S(2)}) async-start(bf16[8,4,16,128]{3,2,1,0:T(8,128)(2,1)} %broadcast_in_dim.15), calls=%async_computation.2 | async-start | bytes 262144 | tf_op jit(solution)/shard_map/all_to_all | solution.py:208
  70.9 5.1 %collective-permute-done.6.below = bf16[2,2,512,128]{3,2,1,0:T(8,128)(2,1)S(1)} collective-permute-done((bf16[2,2,512,128]{3,2,1,0:T(8,128)(2,1)S(1)}, bf16[2,2,512,128]{3,2,1,0:T(8,128)(2,1)S(1)}, u32[]{:S(2)}, u32[]{:S(2)}) %collective-permute-start.6) | collective-permute-done | bytes 524320 | tf_op jit(solution)/shard_map/ppermute | solution.py:212
  76.0 1.6 %shard_map.66.pack = bf16[240,128]{1,0:T(8,128)(2,1)S(1)} custom-call(s32[2]{0:T(128)S(1)} %copy-done.2, s32[2]{0:T(128)S(1)} %copy-done.3, bf16[2,2,512,128]{3,2,1,0:T(8,128)(2,1)S(1)} %bitcast.7, bf16[2,2,512,128]{3,2,1,0:T(8,128)(2,1)S(1)} %collective-permute-done.6.below, bf16[16,1792]{1,0:T(8,128)(2,1)S(1)} %slice.14.head, ...), custom_call_target="tpu_custom_call" | custom-call | bytes 7380000 | tf_op jit(solution)/shard_map/pallas_call | solution.py:245
  77.5 1.3 %collective-permute-start.8 = (bf16[240,128]{1,0:T(8,128)(2,1)S(1)}, bf16[240,128]{1,0:T(8,128)(2,1)S(1)}, u32[]{:S(2)}, u32[]{:S(2)}) collective-permute-start(bf16[240,128]{1,0:T(8,128)(2,1)S(1)} %shard_map.66.pack), channel_id=1, source_target_pairs={{17,0},{21,4},{25,8},{29,12},{49,32},{53,36},{57,40},{61,44},{81,6... | collective-permute-start | bytes 184328 | tf_op jit(solution)/shard_map/ppermute | solution.py:221
  78.8 1.3 %collective-permute-start.7 = (bf16[240,128]{1,0:T(8,128)(2,1)S(1)}, bf16[240,128]{1,0:T(8,128)(2,1)S(1)}, u32[]{:S(2)}, u32[]{:S(2)}) collective-permute-start(bf16[240,128]{1,0:T(8,128)(2,1)S(1)} %shard_map.66.pack), channel_id=1, source_target_pairs={{9,0},{13,4},{17,8},{21,12},{25,16},{29,20},{41,32},{45,36},{49,40... | collective-permute-start | bytes 184328 | tf_op jit(solution)/shard_map/ppermute | solution.py:221
  80.1 2.2 %all-to-all-done.2.questions = bf16[8,4,16,128]{3,2,1,0:T(8,128)(2,1)S(1)} async-done(((bf16[8,4,16,128]{3,2,1,0:T(8,128)(2,1)}), bf16[8,4,16,128]{3,2,1,0:T(8,128)(2,1)S(1)}, u32[]{:S(2)}, u32[]{:S(2)}) %all-to-all-start.2) | async-done | bytes 131104 | tf_op jit(solution)/shard_map/all_to_all | solution.py:208
  82.4 5.6 %shard_map.65.banded = bf16[128,1792]{1,0:T(8,128)(2,1)} custom-call(s32[2]{0:T(128)S(1)} %copy-done.2, s32[2]{0:T(128)S(1)} %copy-done.3, bf16[128,1792]{1,0:T(8,128)(2,1)S(1)} %copy-done.1, bf16[2,2,512,128]{3,2,1,0:T(8,128)(2,1)S(1)} %bitcast.8, bf16[2,2,512,128]{3,2,1,0:T(8,128)(2,1)S(1)} %collective-permute-done.5.above, ...), custom_call_target="tpu_custom_call" | custom-call | bytes 18450000 | tf_op jit(solution)/shard_map/pallas_call | solution.py:254
  88.5 2.0 %shard_map.67 = bf16[128,1792]{1,0:T(8,128)(2,1)} custom-call(s32[2]{0:T(128)S(1)} %copy-done.2, s32[2]{0:T(128)S(1)} %copy-done.3, bf16[128,1792]{1,0:T(8,128)(2,1)} %shard_map.65.banded, bf16[240,128]{1,0:T(8,128)(2,1)S(1)} %shard_map.66.pack, bf16[240,128]{1,0:T(8,128)(2,1)S(1)} %collective-permute-done.7.back2, ...), custom_call_target="tpu_custom_call", output_to_operand_aliasing={{}: (2, {})} | custom-call | bytes 3690000 | tf_op jit(solution)/shard_map/pallas_call | solution.py:265
  (17 shorter events, 1.2 us)
Async XLA Ops:
  0.0 24.8 %collective-permute-start.3 = (bf16[128,3584]{1,0:T(8,128)(2,1)}, bf16[128,3584]{1,0:T(8,128)(2,1)S(1)}, u32[]{:S(2)}, u32[]{:S(2)}) collective-permute-start(bf16[128,3584]{1,0:T(8,128)(2,1)} %mine.1), channel_id=1, source_target_pairs={{0,64},{64,0},{1,65},{65,1},{2,66},{66,2},{3,67},{67,3},{4,68},{68... | collective-permute-start | bytes 2752520 | tf_op jit(solution)/shard_map/ppermute | solution.py:228
  6.2 10.1 %copy-start = (bf16[128,3584]{1,0:T(8,128)(2,1)S(1)}, bf16[128,3584]{1,0:T(8,128)(2,1)}, u32[]{:S(2)}) copy-start(bf16[128,3584]{1,0:T(8,128)(2,1)} %mine.1) | copy-start | bytes 2752516
  6.2 20.6 %copy-start.1 = (bf16[128,1792]{1,0:T(8,128)(2,1)S(1)}, bf16[128,1792]{1,0:T(8,128)(2,1)}, u32[]{:S(2)}) copy-start(bf16[128,1792]{1,0:T(8,128)(2,1)} %queries.1) | copy-start | bytes 1376260
  6.2 36.5 %all-to-all-start = ((bf16[32,112,128]{2,1,0:T(8,128)(2,1)}), bf16[32,112,128]{2,1,0:T(8,128)(2,1)S(1)}, u32[]{:S(2)}, u32[]{:S(2)}) async-start(bf16[32,112,128]{2,1,0:T(8,128)(2,1)} %broadcast_in_dim.6), calls=%async_computation | async-start | bytes 1835008 | tf_op jit(solution)/shard_map/all_to_all | solution.py:208
  16.3 26.4 %collective-permute-start.2 = (bf16[128,3584]{1,0:T(8,128)(2,1)S(1)}, bf16[128,3584]{1,0:T(8,128)(2,1)}, u32[]{:S(2)}, u32[]{:S(2)}) collective-permute-start(bf16[128,3584]{1,0:T(8,128)(2,1)S(1)} %copy-done), channel_id=1, source_target_pairs={{0,32},{32,0},{1,33},{33,1},{2,34},{34,2},{3,35},{35,3},{4,36},{36... | collective-permute-start | bytes 2752520 | tf_op jit(solution)/shard_map/ppermute | solution.py:234
  24.8 17.9 %collective-permute-start.4 = (bf16[128,3584]{1,0:T(8,128)(2,1)S(1)}, bf16[128,3584]{1,0:T(8,128)(2,1)}, u32[]{:S(2)}, u32[]{:S(2)}) collective-permute-start(bf16[128,3584]{1,0:T(8,128)(2,1)S(1)} %collective-permute-done.3.across), channel_id=1, source_target_pairs={{0,32},{32,0},{1,33},{33,1},{2,34},{34,2},{3,35},{35,3},{4,36},{36... | collective-permute-start | bytes 2752520 | tf_op jit(solution)/shard_map/ppermute | solution.py:234
  26.8 11.1 %collective-permute-start.1 = (bf16[16,1792]{1,0:T(8,128)(2,1)S(1)}, bf16[16,1792]{1,0:T(8,128)(2,1)S(1)}, u32[]{:S(2)}, u32[]{:S(2)}) collective-permute-start(bf16[16,1792]{1,0:T(8,128)(2,1)S(1)} %slice.14.head), channel_id=1, source_target_pairs={{0,17},{4,21},{8,25},{12,29},{32,49},{36,53},{40,57},{44,61},{64,8... | collective-permute-start | bytes 172040 | tf_op jit(solution)/shard_map/ppermute | solution.py:221
  35.4 3.7 %collective-permute-start = (bf16[16,1792]{1,0:T(8,128)(2,1)S(1)}, bf16[16,1792]{1,0:T(8,128)(2,1)S(1)}, u32[]{:S(2)}, u32[]{:S(2)}) collective-permute-start(bf16[16,1792]{1,0:T(8,128)(2,1)S(1)} %slice.14.head), channel_id=1, source_target_pairs={{0,9},{4,13},{8,17},{12,21},{16,25},{20,29},{32,41},{36,45},{40,49... | collective-permute-start | bytes 172040 | tf_op jit(solution)/shard_map/ppermute | solution.py:221
  59.0 17.0 %collective-permute-start.6 = (bf16[2,2,512,128]{3,2,1,0:T(8,128)(2,1)S(1)}, bf16[2,2,512,128]{3,2,1,0:T(8,128)(2,1)S(1)}, u32[]{:S(2)}, u32[]{:S(2)}) collective-permute-start(bf16[2,2,512,128]{3,2,1,0:T(8,128)(2,1)S(1)} %bitcast.4), channel_id=1, source_target_pairs={{4,0},{8,4},{12,8},{16,12},{20,16},{24,20},{28,24},{5,1},{9,5},{13... | collective-permute-start | bytes 1572872 | tf_op jit(solution)/shard_map/ppermute | solution.py:212
  60.3 22.1 %collective-permute-start.5 = (bf16[2,2,512,128]{3,2,1,0:T(8,128)(2,1)S(1)}, bf16[2,2,512,128]{3,2,1,0:T(8,128)(2,1)S(1)}, u32[]{:S(2)}, u32[]{:S(2)}) collective-permute-start(bf16[2,2,512,128]{3,2,1,0:T(8,128)(2,1)S(1)} %bitcast.5), channel_id=1, source_target_pairs={{0,4},{4,8},{8,12},{12,16},{16,20},{20,24},{24,28},{1,5},{5,9},{9,... | collective-permute-start | bytes 1572872 | tf_op jit(solution)/shard_map/ppermute | solution.py:212
  65.5 10.4 %copy-start.2 = (s32[2]{0:T(128)S(1)}, s32[2]{0:T(128)}, u32[]{:S(2)}) copy-start(s32[2]{0:T(128)} %tiles.5) | copy-start | bytes 28
  65.5 10.4 %copy-start.3 = (s32[2]{0:T(128)S(1)}, s32[2]{0:T(128)}, u32[]{:S(2)}) copy-start(s32[2]{0:T(128)} %lengths.5) | copy-start | bytes 28
  65.5 16.8 %all-to-all-start.2 = ((bf16[8,4,16,128]{3,2,1,0:T(8,128)(2,1)}), bf16[8,4,16,128]{3,2,1,0:T(8,128)(2,1)S(1)}, u32[]{:S(2)}, u32[]{:S(2)}) async-start(bf16[8,4,16,128]{3,2,1,0:T(8,128)(2,1)} %broadcast_in_dim.15), calls=%async_computation.2 | async-start | bytes 262144 | tf_op jit(solution)/shard_map/all_to_all | solution.py:208
  77.5 10.9 %collective-permute-start.8 = (bf16[240,128]{1,0:T(8,128)(2,1)S(1)}, bf16[240,128]{1,0:T(8,128)(2,1)S(1)}, u32[]{:S(2)}, u32[]{:S(2)}) collective-permute-start(bf16[240,128]{1,0:T(8,128)(2,1)S(1)} %shard_map.66.pack), channel_id=1, source_target_pairs={{17,0},{21,4},{25,8},{29,12},{49,32},{53,36},{57,40},{61,44},{81,6... | collective-permute-start | bytes 184328 | tf_op jit(solution)/shard_map/ppermute | solution.py:221
  78.8 9.6 %collective-permute-start.7 = (bf16[240,128]{1,0:T(8,128)(2,1)S(1)}, bf16[240,128]{1,0:T(8,128)(2,1)S(1)}, u32[]{:S(2)}, u32[]{:S(2)}) collective-permute-start(bf16[240,128]{1,0:T(8,128)(2,1)S(1)} %shard_map.66.pack), channel_id=1, source_target_pairs={{9,0},{13,4},{17,8},{21,12},{25,16},{29,20},{41,32},{45,36},{49,40... | collective-permute-start | bytes 184328 | tf_op jit(solution)/shard_map/ppermute | solution.py:221

commit v7 on v6

--- a/solution.py
+++ b/solution.py
@@ -47,7 +47,11 @@
     return y, x, start, stop, jnp.where(second, lengths[1], lengths[0])
 
 
-def project_body(weights, mine, sibling, across, corner, out):
+def project_body(weights, mine, sibling, across, corner, out, whole):
+    depth = weights.shape[2]
+    for x in range(XS):
+        for y in range(YS):
+            whole[pl.ds((XS * y + x) * depth, depth), :] = weights[x, y]
     pair, core = lax.axis_index("pair"), lax.axis_index("core")
     for z, c, tokens in (
         (pair, core, mine),
@@ -55,7 +59,7 @@
         (1 - pair, core, across),
         (1 - pair, 1 - core, corner),
     ):
-        rows = jnp.dot(tokens[...], weights[...], preferred_element_type=f32).astype(bf16)
+        rows = jnp.dot(tokens[...], whole[...], preferred_element_type=f32).astype(bf16)
         for x in range(XS):
             out[z, c, x] = rows
 
@@ -229,14 +233,20 @@
 
     shard = jnp.where(core == 0, key_matrix, value_matrix)
     shard = jnp.where(pair == 0, shard[:, :HEAD], shard[:, HEAD:])
-    weights = exchange(copies(shard, YS * XS), ("y", "x")).reshape(tokens.shape[1], HEAD)
+    weights = exchange(copies(shard, YS * XS), ("x", "y"))
+    weights = weights.reshape((XS, YS) + weights.shape[1:])
     head = queries[:ASK]
     sibling, corner = lax.ppermute(tokens, "core", swap), lax.ppermute(across, "core", swap)
     head2, head4 = along(head, 2, 0, 1), along(head, 4, 0, 1)
     weights, head2, head4 = lax.optimization_barrier((weights, head2, head4))
 
     rows = call(
-        project_body, jax.ShapeDtypeStruct((2, 2, XS, ROWS, HEAD), bf16), 5, micros=2, scalars=0
+        project_body,
+        jax.ShapeDtypeStruct((2, 2, XS, ROWS, HEAD), bf16),
+        5,
+        [pltpu.VMEM((tokens.shape[1], HEAD), bf16)],
+        micros=2,
+        scalars=0,
     )(weights, tokens, sibling, across, corner)
     tile = exchange(rows.reshape(4 * XS, ROWS, HEAD), ("pair", "core", "x")).reshape(KV, 2, TILE, HEAD)
 

time: 91.1 us -> 90.9 us (level)
  waiting for transfers between devices: 20.4 us -> 19.3 us
  starting transfers between devices: 41.9 us -> 42.9 us
    ppermute x2, waiting for transfers between devices: 5.07 us -> 3.7 us  [down(): lax.ppermute(array, 'y', [(y, y + shift) for y in range(YS) if 0 <= y + s...]
    all_to_all x2, waiting for transfers between devices: 5.82 us -> 6.85 us  [exchange(): return lax.all_to_all(array, axis, 0, 0, tiled=False)]
    all_to_all x2, starting transfers between devices: 15.4 us -> 16.4 us  [exchange(): return lax.all_to_all(array, axis, 0, 0, tiled=False)]
  transfers between devices with their start and end apart: 11 -> 11, of which waited for: 7 -> 6; matrix products, arithmetic and copies ran while one was open for 3% -> 3% of each run, Pallas kernels for 8% -> 8%
where the time goes in v7:
time: 90.9 us; the launch traced here: 90 us
  starting transfers between devices  42.9 us (47%)
  waiting for transfers between devices  19.3 us (21%)
  blocking collectives  13.3 us (15%)
  Pallas kernels  11.8 us (13%)
  local copies, waits for them, and re-layouts  1.74 us (2%)
    all_to_all x2, starting transfers between devices, exchange(): return lax.all_to_all(array, axis, 0, 0, tiled=False)  16.4 us
    all_to_all x1, blocking collectives, exchange(): return lax.all_to_all(array, axis, 0, 0, tiled=False)  13.3 us
    ppermute x4, starting transfers between devices, along(): return lax.ppermute(array, ('y', 'x'), pairs)  12.5 us
    all_to_all x2, waiting for transfers between devices, exchange(): return lax.all_to_all(array, axis, 0, 0, tiled=False)  6.85 us
    ppermute x1, waiting for transfers between devices, per_device(): across = lax.ppermute(tokens, 'pair', swap)  6.6 us
    ppermute x2, starting transfers between devices, down(): lax.ppermute(array, 'y', [(y, y + shift) for y in range(YS) if 0 <= y + s...  5.86 us
    pallas_call x1, Pallas kernels, per_device(): call(attend_body, jax.ShapeDtypeStruct(queries.shape, bf16), 5, [pltpu.VM...  5.55 us
    ppermute x1, starting transfers between devices, per_device(): across = lax.ppermute(tokens, 'pair', swap)  4.27 us
  transfers between devices with their start and end apart: 11, of which 6 were waited for; matrix products, arithmetic and copies ran while one was open for 3% of the time, Pallas kernels for 8%

profile of v7, /device:TPU:128, one launch (start us, length us, event | category | flops | bytes accessed | tf_op | source)
XLA Modules:
  0.0 90.0 jit_solution(6206985033133357313)
XLA Ops:
  0.0 4.3 %collective-permute-start.3 = (bf16[128,3584]{1,0:T(8,128)(2,1)}, bf16[128,3584]{1,0:T(8,128)(2,1)S(1)}, u32[]{:S(2)}, u32[]{:S(2)}) collective-permute-start(bf16[128,3584]{1,0:T(8,128)(2,1)} %mine.1), channel_id=1, source_target_pairs={{0,64},{64,0},{1,65},{65,1},{2,66},{66,2},{3,67},{67,3},{4,68},{68... | collective-permute-start | bytes 2752520 | tf_op jit(solution)/shard_map/ppermute | solution.py:232
  4.3 0.8 broadcast_select_fusion
  5.1 1.0 %broadcast_in_dim.6 = bf16[32,112,128]{2,1,0:T(8,128)(2,1)} broadcast(bf16[112,128]{1,0:T(8,128)(2,1)S(1)} %slice_select_fusion), dimensions={1,2} | broadcast | bytes 946176 | tf_op jit(solution)/shard_map/broadcast_in_dim | solution.py:220
  6.2 10.1 %all-to-all-start = ((bf16[32,112,128]{2,1,0:T(8,128)(2,1)}), bf16[32,112,128]{2,1,0:T(8,128)(2,1)S(1)}, u32[]{:S(2)}, u32[]{:S(2)}) async-start(bf16[32,112,128]{2,1,0:T(8,128)(2,1)} %broadcast_in_dim.6), calls=%async_computation | async-start | bytes 1835008 | tf_op jit(solution)/shard_map/all_to_all | solution.py:212
  16.3 1.9 %collective-permute-start.2 = (bf16[128,3584]{1,0:T(8,128)(2,1)S(1)}, bf16[128,3584]{1,0:T(8,128)(2,1)}, u32[]{:S(2)}, u32[]{:S(2)}) collective-permute-start(bf16[128,3584]{1,0:T(8,128)(2,1)S(1)} %copy-done), channel_id=1, source_target_pairs={{0,32},{32,0},{1,33},{33,1},{2,34},{34,2},{3,35},{35,3},{4,36},{36... | collective-permute-start | bytes 2752520 | tf_op jit(solution)/shard_map/ppermute | solution.py:239
  18.2 6.6 %collective-permute-done.3.across = bf16[128,3584]{1,0:T(8,128)(2,1)S(1)} collective-permute-done((bf16[128,3584]{1,0:T(8,128)(2,1)}, bf16[128,3584]{1,0:T(8,128)(2,1)S(1)}, u32[]{:S(2)}, u32[]{:S(2)}) %collective-permute-start.3) | collective-permute-done | bytes 917536 | tf_op jit(solution)/shard_map/ppermute | solution.py:232
  24.8 1.9 %collective-permute-start.4 = (bf16[128,3584]{1,0:T(8,128)(2,1)S(1)}, bf16[128,3584]{1,0:T(8,128)(2,1)}, u32[]{:S(2)}, u32[]{:S(2)}) collective-permute-start(bf16[128,3584]{1,0:T(8,128)(2,1)S(1)} %collective-permute-done.3.across), channel_id=1, source_target_pairs={{0,32},{32,0},{1,33},{33,1},{2,34},{34,2},{3,35},{35,3},{4,36},{36... | collective-permute-start | bytes 2752520 | tf_op jit(solution)/shard_map/ppermute | solution.py:239
  26.8 8.7 %collective-permute-start.1 = (bf16[16,1792]{1,0:T(8,128)(2,1)S(1)}, bf16[16,1792]{1,0:T(8,128)(2,1)S(1)}, u32[]{:S(2)}, u32[]{:S(2)}) collective-permute-start(bf16[16,1792]{1,0:T(8,128)(2,1)S(1)} %slice.14.head), channel_id=1, source_target_pairs={{0,17},{4,21},{8,25},{12,29},{32,49},{36,53},{40,57},{44,61},{64,8... | collective-permute-start | bytes 172040 | tf_op jit(solution)/shard_map/ppermute | solution.py:225
  35.4 1.3 %collective-permute-start = (bf16[16,1792]{1,0:T(8,128)(2,1)S(1)}, bf16[16,1792]{1,0:T(8,128)(2,1)S(1)}, u32[]{:S(2)}, u32[]{:S(2)}) collective-permute-start(bf16[16,1792]{1,0:T(8,128)(2,1)S(1)} %slice.14.head), channel_id=1, source_target_pairs={{0,9},{4,13},{8,17},{12,21},{16,25},{20,29},{32,41},{36,45},{40,49... | collective-permute-start | bytes 172040 | tf_op jit(solution)/shard_map/ppermute | solution.py:225
  37.3 1.5 %collective-permute-done.head2 = bf16[16,1792]{1,0:T(8,128)(2,1)S(1)} collective-permute-done((bf16[16,1792]{1,0:T(8,128)(2,1)S(1)}, bf16[16,1792]{1,0:T(8,128)(2,1)S(1)}, u32[]{:S(2)}, u32[]{:S(2)}) %collective-permute-start) | collective-permute-done | bytes 57376 | tf_op jit(solution)/shard_map/ppermute | solution.py:225
  38.9 3.3 %all-to-all-done = bf16[32,112,128]{2,1,0:T(8,128)(2,1)S(1)} async-done(((bf16[32,112,128]{2,1,0:T(8,128)(2,1)}), bf16[32,112,128]{2,1,0:T(8,128)(2,1)S(1)}, u32[]{:S(2)}, u32[]{:S(2)}) %all-to-all-start) | async-done | bytes 917536 | tf_op jit(solution)/shard_map/all_to_all | solution.py:212
  42.1 2.6 %shard_map.64 = bf16[2,2,4,128,128]{4,3,2,1,0:T(8,128)(2,1)S(1)} custom-call(bf16[4,8,112,128]{3,2,1,0:T(8,128)(2,1)S(1)} %bitcast.9, bf16[128,3584]{1,0:T(8,128)(2,1)S(1)} %copy-done, bf16[128,3584]{1,0:T(8,128)(2,1)} %collective-permute-done.2.sibling, bf16[128,3584]{1,0:T(8,128)(2,1)S(1)} %collective-permute-done.3.across, ...), custom_call_target="tpu_custom_call" | custom-call | bytes 7380000 | tf_op jit(solution)/shard_map/pallas_call | solution.py:243
  44.8 13.3 %all_to_all.15 = bf16[16,128,128]{2,1,0:T(8,128)(2,1)S(1)} all-to-all(bf16[16,128,128]{2,1,0:T(8,128)(2,1)S(1)} %bitcast.10), channel_id=1, replica_groups=mesh['z'=4,'pair'=2,'core'=2,'y'=8,'x'=4] {'pair','core','x'}, dimensions={0} | all-to-all | bytes 1048576 | tf_op jit(solution)/shard_map/all_to_all | solution.py:212
  58.1 1.3 %collective-permute-start.6 = (bf16[2,2,512,128]{3,2,1,0:T(8,128)(2,1)S(1)}, bf16[2,2,512,128]{3,2,1,0:T(8,128)(2,1)S(1)}, u32[]{:S(2)}, u32[]{:S(2)}) collective-permute-start(bf16[2,2,512,128]{3,2,1,0:T(8,128)(2,1)S(1)} %bitcast.4), channel_id=1, source_target_pairs={{4,0},{8,4},{12,8},{16,12},{20,16},{24,20},{28,24},{5,1},{9,5},{13... | collective-permute-start | bytes 1572872 | tf_op jit(solution)/shard_map/ppermute | solution.py:216
  59.3 4.6 %collective-permute-start.5 = (bf16[2,2,512,128]{3,2,1,0:T(8,128)(2,1)S(1)}, bf16[2,2,512,128]{3,2,1,0:T(8,128)(2,1)S(1)}, u32[]{:S(2)}, u32[]{:S(2)}) collective-permute-start(bf16[2,2,512,128]{3,2,1,0:T(8,128)(2,1)S(1)} %bitcast.5), channel_id=1, source_target_pairs={{0,4},{4,8},{8,12},{12,16},{16,20},{20,24},{24,28},{1,5},{5,9},{9,... | collective-permute-start | bytes 1572872 | tf_op jit(solution)/shard_map/ppermute | solution.py:216
  63.9 0.7 broadcast_in_dim.15
  64.6 6.3 %all-to-all-start.2 = ((bf16[8,4,16,128]{3,2,1,0:T(8,128)(2,1)}), bf16[8,4,16,128]{3,2,1,0:T(8,128)(2,1)S(1)}, u32[]{:S(2)}, u32[]{:S(2)}) async-start(bf16[8,4,16,128]{3,2,1,0:T(8,128)(2,1)} %broadcast_in_dim.15), calls=%async_computation.2 | async-start | bytes 262144 | tf_op jit(solution)/shard_map/all_to_all | solution.py:212
  71.0 3.7 %collective-permute-done.6.below = bf16[2,2,512,128]{3,2,1,0:T(8,128)(2,1)S(1)} collective-permute-done((bf16[2,2,512,128]{3,2,1,0:T(8,128)(2,1)S(1)}, bf16[2,2,512,128]{3,2,1,0:T(8,128)(2,1)S(1)}, u32[]{:S(2)}, u32[]{:S(2)}) %collective-permute-start.6) | collective-permute-done | bytes 524320 | tf_op jit(solution)/shard_map/ppermute | solution.py:216
  74.7 1.6 %shard_map.66.pack = bf16[240,128]{1,0:T(8,128)(2,1)S(1)} custom-call(s32[2]{0:T(128)S(1)} %copy-done.2, s32[2]{0:T(128)S(1)} %copy-done.3, bf16[2,2,512,128]{3,2,1,0:T(8,128)(2,1)S(1)} %bitcast.7, bf16[2,2,512,128]{3,2,1,0:T(8,128)(2,1)S(1)} %collective-permute-done.6.below, bf16[16,1792]{1,0:T(8,128)(2,1)S(1)} %slice.14.head, ...), custom_call_target="tpu_custom_call" | custom-call | bytes 7380000 | tf_op jit(solution)/shard_map/pallas_call | solution.py:255
  76.2 1.3 %collective-permute-start.8 = (bf16[240,128]{1,0:T(8,128)(2,1)S(1)}, bf16[240,128]{1,0:T(8,128)(2,1)S(1)}, u32[]{:S(2)}, u32[]{:S(2)}) collective-permute-start(bf16[240,128]{1,0:T(8,128)(2,1)S(1)} %shard_map.66.pack), channel_id=1, source_target_pairs={{17,0},{21,4},{25,8},{29,12},{49,32},{53,36},{57,40},{61,44},{81,6... | collective-permute-start | bytes 184328 | tf_op jit(solution)/shard_map/ppermute | solution.py:225
  77.5 1.3 %collective-permute-start.7 = (bf16[240,128]{1,0:T(8,128)(2,1)S(1)}, bf16[240,128]{1,0:T(8,128)(2,1)S(1)}, u32[]{:S(2)}, u32[]{:S(2)}) collective-permute-start(bf16[240,128]{1,0:T(8,128)(2,1)S(1)} %shard_map.66.pack), channel_id=1, source_target_pairs={{9,0},{13,4},{17,8},{21,12},{25,16},{29,20},{41,32},{45,36},{49,40... | collective-permute-start | bytes 184328 | tf_op jit(solution)/shard_map/ppermute | solution.py:225
  78.8 3.6 %all-to-all-done.2.questions = bf16[8,4,16,128]{3,2,1,0:T(8,128)(2,1)S(1)} async-done(((bf16[8,4,16,128]{3,2,1,0:T(8,128)(2,1)}), bf16[8,4,16,128]{3,2,1,0:T(8,128)(2,1)S(1)}, u32[]{:S(2)}, u32[]{:S(2)}) %all-to-all-start.2) | async-done | bytes 131104 | tf_op jit(solution)/shard_map/all_to_all | solution.py:212
  82.4 5.6 %shard_map.65.banded = bf16[128,1792]{1,0:T(8,128)(2,1)} custom-call(s32[2]{0:T(128)S(1)} %copy-done.2, s32[2]{0:T(128)S(1)} %copy-done.3, bf16[128,1792]{1,0:T(8,128)(2,1)S(1)} %copy-done.1, bf16[2,2,512,128]{3,2,1,0:T(8,128)(2,1)S(1)} %bitcast.8, bf16[2,2,512,128]{3,2,1,0:T(8,128)(2,1)S(1)} %collective-permute-done.5.above, ...), custom_call_target="tpu_custom_call" | custom-call | bytes 18450000 | tf_op jit(solution)/shard_map/pallas_call | solution.py:264
  88.0 2.0 %shard_map.67 = bf16[128,1792]{1,0:T(8,128)(2,1)} custom-call(s32[2]{0:T(128)S(1)} %copy-done.2, s32[2]{0:T(128)S(1)} %copy-done.3, bf16[128,1792]{1,0:T(8,128)(2,1)} %shard_map.65.banded, bf16[240,128]{1,0:T(8,128)(2,1)S(1)} %shard_map.66.pack, bf16[240,128]{1,0:T(8,128)(2,1)S(1)} %collective-permute-done.7.back2, ...), custom_call_target="tpu_custom_call", output_to_operand_aliasing={{}: (2, {})} | custom-call | bytes 3690000 | tf_op jit(solution)/shard_map/pallas_call | solution.py:275
  (17 shorter events, 0.7 us)
Async XLA Ops:
  0.0 24.8 %collective-permute-start.3 = (bf16[128,3584]{1,0:T(8,128)(2,1)}, bf16[128,3584]{1,0:T(8,128)(2,1)S(1)}, u32[]{:S(2)}, u32[]{:S(2)}) collective-permute-start(bf16[128,3584]{1,0:T(8,128)(2,1)} %mine.1), channel_id=1, source_target_pairs={{0,64},{64,0},{1,65},{65,1},{2,66},{66,2},{3,67},{67,3},{4,68},{68... | collective-permute-start | bytes 2752520 | tf_op jit(solution)/shard_map/ppermute | solution.py:232
  6.2 10.1 %copy-start = (bf16[128,3584]{1,0:T(8,128)(2,1)S(1)}, bf16[128,3584]{1,0:T(8,128)(2,1)}, u32[]{:S(2)}) copy-start(bf16[128,3584]{1,0:T(8,128)(2,1)} %mine.1) | copy-start | bytes 2752516
  6.2 20.6 %copy-start.1 = (bf16[128,1792]{1,0:T(8,128)(2,1)S(1)}, bf16[128,1792]{1,0:T(8,128)(2,1)}, u32[]{:S(2)}) copy-start(bf16[128,1792]{1,0:T(8,128)(2,1)} %queries.1) | copy-start | bytes 1376260
  6.2 35.9 %all-to-all-start = ((bf16[32,112,128]{2,1,0:T(8,128)(2,1)}), bf16[32,112,128]{2,1,0:T(8,128)(2,1)S(1)}, u32[]{:S(2)}, u32[]{:S(2)}) async-start(bf16[32,112,128]{2,1,0:T(8,128)(2,1)} %broadcast_in_dim.6), calls=%async_computation | async-start | bytes 1835008 | tf_op jit(solution)/shard_map/all_to_all | solution.py:212
  16.3 25.9 %collective-permute-start.2 = (bf16[128,3584]{1,0:T(8,128)(2,1)S(1)}, bf16[128,3584]{1,0:T(8,128)(2,1)}, u32[]{:S(2)}, u32[]{:S(2)}) collective-permute-start(bf16[128,3584]{1,0:T(8,128)(2,1)S(1)} %copy-done), channel_id=1, source_target_pairs={{0,32},{32,0},{1,33},{33,1},{2,34},{34,2},{3,35},{35,3},{4,36},{36... | collective-permute-start | bytes 2752520 | tf_op jit(solution)/shard_map/ppermute | solution.py:239
  24.8 17.3 %collective-permute-start.4 = (bf16[128,3584]{1,0:T(8,128)(2,1)S(1)}, bf16[128,3584]{1,0:T(8,128)(2,1)}, u32[]{:S(2)}, u32[]{:S(2)}) collective-permute-start(bf16[128,3584]{1,0:T(8,128)(2,1)S(1)} %collective-permute-done.3.across), channel_id=1, source_target_pairs={{0,32},{32,0},{1,33},{33,1},{2,34},{34,2},{3,35},{35,3},{4,36},{36... | collective-permute-start | bytes 2752520 | tf_op jit(solution)/shard_map/ppermute | solution.py:239
  26.8 10.6 %collective-permute-start.1 = (bf16[16,1792]{1,0:T(8,128)(2,1)S(1)}, bf16[16,1792]{1,0:T(8,128)(2,1)S(1)}, u32[]{:S(2)}, u32[]{:S(2)}) collective-permute-start(bf16[16,1792]{1,0:T(8,128)(2,1)S(1)} %slice.14.head), channel_id=1, source_target_pairs={{0,17},{4,21},{8,25},{12,29},{32,49},{36,53},{40,57},{44,61},{64,8... | collective-permute-start | bytes 172040 | tf_op jit(solution)/shard_map/ppermute | solution.py:225
  35.4 3.4 %collective-permute-start = (bf16[16,1792]{1,0:T(8,128)(2,1)S(1)}, bf16[16,1792]{1,0:T(8,128)(2,1)S(1)}, u32[]{:S(2)}, u32[]{:S(2)}) collective-permute-start(bf16[16,1792]{1,0:T(8,128)(2,1)S(1)} %slice.14.head), channel_id=1, source_target_pairs={{0,9},{4,13},{8,17},{12,21},{16,25},{20,29},{32,41},{36,45},{40,49... | collective-permute-start | bytes 172040 | tf_op jit(solution)/shard_map/ppermute | solution.py:225
  58.1 16.6 %collective-permute-start.6 = (bf16[2,2,512,128]{3,2,1,0:T(8,128)(2,1)S(1)}, bf16[2,2,512,128]{3,2,1,0:T(8,128)(2,1)S(1)}, u32[]{:S(2)}, u32[]{:S(2)}) collective-permute-start(bf16[2,2,512,128]{3,2,1,0:T(8,128)(2,1)S(1)} %bitcast.4), channel_id=1, source_target_pairs={{4,0},{8,4},{12,8},{16,12},{20,16},{24,20},{28,24},{5,1},{9,5},{13... | collective-permute-start | bytes 1572872 | tf_op jit(solution)/shard_map/ppermute | solution.py:216
  59.3 23.1 %collective-permute-start.5 = (bf16[2,2,512,128]{3,2,1,0:T(8,128)(2,1)S(1)}, bf16[2,2,512,128]{3,2,1,0:T(8,128)(2,1)S(1)}, u32[]{:S(2)}, u32[]{:S(2)}) collective-permute-start(bf16[2,2,512,128]{3,2,1,0:T(8,128)(2,1)S(1)} %bitcast.5), channel_id=1, source_target_pairs={{0,4},{4,8},{8,12},{12,16},{16,20},{20,24},{24,28},{1,5},{5,9},{9,... | collective-permute-start | bytes 1572872 | tf_op jit(solution)/shard_map/ppermute | solution.py:216
  64.6 10.0 %copy-start.2 = (s32[2]{0:T(128)S(1)}, s32[2]{0:T(128)}, u32[]{:S(2)}) copy-start(s32[2]{0:T(128)} %tiles.5) | copy-start | bytes 28
  64.6 10.0 %copy-start.3 = (s32[2]{0:T(128)S(1)}, s32[2]{0:T(128)}, u32[]{:S(2)}) copy-start(s32[2]{0:T(128)} %lengths.5) | copy-start | bytes 28
  64.6 17.8 %all-to-all-start.2 = ((bf16[8,4,16,128]{3,2,1,0:T(8,128)(2,1)}), bf16[8,4,16,128]{3,2,1,0:T(8,128)(2,1)S(1)}, u32[]{:S(2)}, u32[]{:S(2)}) async-start(bf16[8,4,16,128]{3,2,1,0:T(8,128)(2,1)} %broadcast_in_dim.15), calls=%async_computation.2 | async-start | bytes 262144 | tf_op jit(solution)/shard_map/all_to_all | solution.py:212
  76.2 11.7 %collective-permute-start.8 = (bf16[240,128]{1,0:T(8,128)(2,1)S(1)}, bf16[240,128]{1,0:T(8,128)(2,1)S(1)}, u32[]{:S(2)}, u32[]{:S(2)}) collective-permute-start(bf16[240,128]{1,0:T(8,128)(2,1)S(1)} %shard_map.66.pack), channel_id=1, source_target_pairs={{17,0},{21,4},{25,8},{29,12},{49,32},{53,36},{57,40},{61,44},{81,6... | collective-permute-start | bytes 184328 | tf_op jit(solution)/shard_map/ppermute | solution.py:225
  77.5 10.4 %collective-permute-start.7 = (bf16[240,128]{1,0:T(8,128)(2,1)S(1)}, bf16[240,128]{1,0:T(8,128)(2,1)S(1)}, u32[]{:S(2)}, u32[]{:S(2)}) collective-permute-start(bf16[240,128]{1,0:T(8,128)(2,1)S(1)} %shard_map.66.pack), channel_id=1, source_target_pairs={{9,0},{13,4},{17,8},{21,12},{25,16},{29,20},{41,32},{45,36},{49,40... | collective-permute-start | bytes 184328 | tf_op jit(solution)/shard_map/ppermute | solution.py:225
